TPU v7x, 256 devices: a whole 4x4x8 slice. The times are simulated.
256 devices in a mesh: slab: 32 (over y, z), narrow: 8 (over x, core).
Axes of the slice: x: 4, y: 4, z: 8, core: 2. Of those that a mesh axis runs over, the one named last changes fastest.
Arguments:
- rhs: float32 [128, 128, 16, 256], P('slab', 'narrow'), may hold values from -6 to 6
- skeleton_matrix_fine: float32 [24, 40], replicated, may hold values from -0.5 to 0.5
- elimination_inverse_fine: float32 [40, 40], replicated, may hold values from -1 to 1
- schur_update_fine: float32 [27, 24, 40], replicated, may hold values from -0.109375 to 0.109375
- skeleton_matrix_mid: float32 [48, 144], replicated, may hold values from -0.3125 to 0.3125
- elimination_inverse_mid: float32 [144, 144], replicated, may hold values from -0.5 to 0.5
- schur_update_mid: float32 [27, 48, 144], replicated, may hold values from -0.0546875 to 0.0546875
- skeleton_matrix_coarse: float32 [96, 288], replicated, may hold values from -0.21875 to 0.21875
- elimination_inverse_coarse: float32 [288, 288], replicated, may hold values from -0.375 to 0.375
- schur_update_coarse: float32 [27, 96, 288], replicated, may hold values from -0.0390625 to 0.0390625
Outputs:
- solved1: float32 [128, 128, 16, 160], P('slab', 'narrow')
- solved2: float32 [64, 64, 8, 576], P('slab', 'narrow')
- solved3: float32 [32, 32, 4, 1152], P('slab', 'narrow')
- coarse_rhs: float32 [32, 32, 4, 384], P('slab')
All inputs are finite; a program needn't handle non-finite values.
Results may differ from a plain program's by a relative error of at most 0.0001.
Values sent between devices are 32-bit elements; how exact they have to be, the bound alone decides.
No kernel may reach another device: no remote copies, remote signals or barrier semaphores. Data moves between devices by JAX's collectives and lax.ppermute only.
A program may use at most 256 MiB of HBM per device.

v0:
```python
import functools

import jax
import jax.numpy as jnp
from jax import lax
from jax.experimental import pallas as pl
from jax.experimental.pallas import tpu as pltpu
from jax.sharding import PartitionSpec as P

F32 = jnp.float32
BF16 = jnp.bfloat16
VMEM_LIMIT = 48 * 1024 * 1024


def dot(a, b):
    return lax.dot_general(a, b, (((1,), (0,)), ((), ())), preferred_element_type=F32)


def halves(x):
    high = x.astype(BF16)
    return high, (x - high.astype(F32)).astype(BF16)


def dot3(a_high, a_low, b):
    b_high, b_low = halves(b)
    return dot(a_high, b_high) + dot(a_low, b_high) + dot(a_high, b_low)


def lanes(shape):
    return lax.broadcasted_iota(jnp.int32, shape, len(shape) - 1)


def roll(x, shift):
    size = x.shape[1]
    shift = shift % size
    return x if shift == 0 else pltpu.roll(x, shift, 1)


def stacked(x):
    high = x.astype(BF16).astype(F32)
    zeros = jnp.zeros((8, x.shape[1]), F32)
    return jnp.concatenate([high, high, x - high, zeros], axis=0).astype(BF16)


def packed_left(ref, block, x):
    high = x.astype(BF16).astype(F32)
    base = block * 128
    ref[:, base : base + 40] = high
    ref[:, base + 40 : base + 80] = x - high
    ref[:, base + 80 : base + 120] = high


def to_partners(even, upward, downward):
    return jnp.where(even, upward, downward), jnp.where(even, downward, upward)


def from_partners(index, count, first, second):
    even = index % 2 == 0
    above = jnp.where(even, first, second)
    below = jnp.where(even, second, first)
    zeros = jnp.zeros_like(above)
    return jnp.where(index < count - 1, above, zeros), jnp.where(index > 0, below, zeros)


def fine_kernel(
    place, rhs, skel, elim, update, solved, skeleton, inner, edge, send_a, send_b,
    left_c, left_u, turned, cat, out_rows,
):
    left_c[...] = jnp.zeros_like(left_c)
    left_u[...] = jnp.zeros_like(left_u)
    packed_left(left_c, 0, jnp.concatenate([elim[...], skel[...]], axis=0))
    for dx in range(3):
        packed_left(left_u, dx, update[dx * 216 : (dx + 1) * 216, :])
    solve = left_c[...].astype(BF16)
    for x in range(4):
        for part in range(2):
            turned[part] = rhs[x * 256 + part * 128 : x * 256 + (part + 1) * 128, :].T
        for k in range(4):
            vector = jnp.concatenate(
                [turned[part, pl.ds(k, 64, stride=4), :] for part in range(2)], axis=1
            )
            product = dot(solve, stacked(vector[24:64]))
            skeleton[x, :, k * 256 : (k + 1) * 256] = vector[:24] - product[40:64]
            solution_vector = product[:40]
            cat[k, x] = stacked(solution_vector)
            for part in range(2):
                out_rows[part, pl.ds(k, 40, stride=4), :] = solution_vector[
                    :, part * 128 : (part + 1) * 128
                ]
        for part in range(2):
            solved[x * 256 + part * 128 : x * 256 + (part + 1) * 128, :] = out_rows[part].T

    operator = left_u[...].astype(BF16)
    lane = lanes((24, 256))
    z = lane % 16
    half = lanes((24, 128))
    low = [jnp.zeros((24, 128), F32)] * 3
    high = [jnp.zeros((24, 128), F32)] * 3
    for k in range(4):
        for c in range(6):
            first = max(0, c - 2)
            last = min(3, c)
            columns = operator[:, (first - c + 2) * 128 : (last - c + 3) * 128]
            right = cat[k, first : last + 1].reshape((last + 1 - first) * 128, 256)
            product = dot(columns, right)
            sums = []
            for dy in range(3):
                parts = [product[(dy * 3 + dz) * 24 : (dy * 3 + dz + 1) * 24] for dz in range(3)]
                sums.append(
                    parts[1]
                    + jnp.where(z > 0, roll(parts[0], 1), 0.0)
                    + jnp.where(z < 15, roll(parts[2], -1), 0.0)
                )
            from_below = roll(sums[0], 16)
            from_above = roll(sums[2], -16)
            total = (
                sums[1]
                + jnp.where(lane >= 16, from_below, 0.0)
                + jnp.where(lane < 240, from_above, 0.0)
            )
            here = slice(k * 256, (k + 1) * 256)
            if c == 0:
                edge[0, :, here] = total
            elif c == 5:
                edge[1, :, here] = total
            else:
                inner[c - 1, :, here] = total
            slot = k * 6 + c
            q, u = slot // 8, slot % 8
            border = roll(jnp.where(half >= 112, from_above[:, 128:], from_below[:, :128]), 16 * u)
            high[q] = jnp.where(half // 16 == u, border, high[q])
            low[q] = jnp.where(half // 16 == (u + 7) % 8, border, low[q])
    even = place[1] % 2 == 0
    for q in range(3):
        here = slice(q * 128, (q + 1) * 128)
        send_a[:, here], send_b[:, here] = to_partners(even, high[q], low[q])


def fine_border(above, below, slot):
    half = lanes((24, 128))
    q, u = slot // 8, slot % 8
    here = slice(q * 128, (q + 1) * 128)
    start = jnp.where(half < 16, roll(below[:, here], -16 * u), 0.0)
    end = jnp.where(half >= 112, roll(above[:, here], -16 * u), 0.0)
    return start, end


def fine_edge_kernel(narrow, place, edge, got_a, got_b, send_a, send_b):
    above, below = from_partners(place[1], narrow, got_a[...], got_b[...])
    even = place[0] % 2 == 0
    for k in range(4):
        planes = []
        for side, c in ((0, 0), (1, 5)):
            start, end = fine_border(above, below, k * 6 + c)
            planes.append(
                (
                    edge[side, :, k * 256 : k * 256 + 128] + start,
                    edge[side, :, k * 256 + 128 : (k + 1) * 256] + end,
                )
            )
        for part in range(2):
            here = slice(k * 256 + part * 128, k * 256 + (part + 1) * 128)
            send_a[:, here], send_b[:, here] = to_partners(even, planes[1][part], planes[0][part])


def operators_kernel(
    skel2, elim2, update2, skel3, elim3, update3,
    solve2_h, solve2_l, update2_h, update2_l, solve3_h, solve3_l, update3_h, update3_l, sort2, sort3,
):
    solve2_h[...], solve2_l[...] = halves(jnp.concatenate([elim2[...], skel2[...]], axis=0))
    update2_h[...], update2_l[...] = halves(update2[...])
    solve3_h[...], solve3_l[...] = halves(jnp.concatenate([elim3[...], skel3[...]], axis=0))
    update3_h[...], update3_l[...] = halves(update3[...])
    row = lax.broadcasted_iota(jnp.int32, (256, 256), 0)
    y, z = row // 16, row % 16
    goal = ((y % 2) * 2 + z % 2) * 64 + (y // 2) * 8 + z // 2
    sort2[...] = jnp.where(goal == lanes((256, 256)), 1.0, 0.0).astype(BF16)
    row = lax.broadcasted_iota(jnp.int32, (128, 256), 0)
    x, y, z = row // 64, row // 8 % 8, row % 8
    goal = ((x * 2 + y % 2) * 2 + z % 2) * 32 + (y // 2 + 2) * 4 + z // 2
    sort3[...] = jnp.where(goal == lanes((128, 256)), 1.0, 0.0).astype(BF16)


def mid_kernel(
    slabs, narrow, place, skeleton1, inner1, got_a, got_b, plane_a, plane_b, sort,
    solve_h, solve_l, update_h, update_l,
    solved, skeleton, inner, edge, send_a, send_b,
    parts, vector, product, out_rows,
):
    above, below = from_partners(place[1], narrow, got_a[...], got_b[...])
    plane_above, plane_below = from_partners(place[0], slabs, plane_a[...], plane_b[...])
    for k in range(4):
        for x in range(4):
            start, end = fine_border(above, below, k * 6 + x + 1)
            here = slice(k * 256, (k + 1) * 256)
            value = (
                skeleton1[x, :, here] - inner1[x, :, here] - jnp.concatenate([start, end], axis=1)
            )
            if x == 0:
                value = value - plane_below[:, here]
            if x == 3:
                value = value - plane_above[:, here]
            top = value.astype(BF16).astype(F32)
            parts[k * 4 + x] = jnp.concatenate([top, value - top], axis=0).astype(BF16)
    arranged = dot(parts[...].reshape(16 * 48, 256), sort[...])
    half = lanes((24, 128))
    for k in range(4):
        for dx in range(2):
            pair = []
            for x in (dx, 2 + dx):
                base = (k * 4 + x) * 48
                pair.append(arranged[base : base + 24] + arranged[base + 24 : base + 48])
            for dy in range(2):
                first, second = [v[:, dy * 128 : (dy + 1) * 128] for v in pair]
                here = slice(k * 128, (k + 1) * 128)
                child = (dx * 2 + dy) * 2
                vector[child * 24 : child * 24 + 24, here] = jnp.where(
                    half < 64, first, roll(second, 64)
                )
                vector[child * 24 + 24 : child * 24 + 48, here] = jnp.where(
                    half < 64, roll(first, 64), second
                )
    result = dot3(solve_h[...], solve_l[...], vector[48:, :])
    solution_vector = result[:144]
    skeleton[...] = vector[:48, :] - result[144:]
    for k in range(4):
        out_rows[pl.ds(k, 144, stride=4), :] = solution_vector[:, k * 128 : (k + 1) * 128]
    product[...] = dot3(update_h[...], update_l[...], solution_vector)
    solved[...] = out_rows[...].T

    lane = lanes((48, 128))
    i, j, l = lane // 64, lane // 8 % 8, lane % 8
    low = jnp.zeros((48, 128), F32)
    high = jnp.zeros((48, 128), F32)
    for k in range(4):
        here = slice(k * 128, (k + 1) * 128)
        totals, borders = [], []
        for dx in range(3):
            sums = []
            for dy in range(3):
                base = (dx * 9 + dy * 3) * 48
                terms = [product[base + dz * 48 : base + (dz + 1) * 48, here] for dz in range(3)]
                sums.append(
                    terms[1]
                    + jnp.where(l > 0, roll(terms[0], 1), 0.0)
                    + jnp.where(l < 7, roll(terms[2], -1), 0.0)
                )
            from_below = roll(sums[0], 8)
            from_above = roll(sums[2], -8)
            totals.append(
                sums[1] + jnp.where(j > 0, from_below, 0.0) + jnp.where(j < 7, from_above, 0.0)
            )
            borders.append(roll(jnp.where(j == 7, from_above, from_below), 64))
        for kind, (minus, zero, plus) in enumerate((totals, borders)):
            inside = zero + jnp.where(i == 0, roll(plus, 64), roll(minus, 64))
            outside = jnp.where(i == 0, plus, minus)
            if kind == 0:
                inner[:, here] = inside
                edge[:, here] = outside
            else:
                for a, value in enumerate((inside, outside)):
                    u = k * 2 + a
                    moved = roll(value, 8 * u)
                    high = jnp.where(j == u, moved, high)
                    low = jnp.where(j == (u + 7) % 8, moved, low)
    send_a[...], send_b[...] = to_partners(place[1] % 2 == 0, high, low)


def mid_border(above, below, u):
    j = lanes((48, 128)) // 8 % 8
    return jnp.where(j == 0, roll(below, -8 * u), 0.0) + jnp.where(j == 7, roll(above, -8 * u), 0.0)


def mid_edge_kernel(narrow, place, edge, got_a, got_b, send_a, send_b):
    above, below = from_partners(place[1], narrow, got_a[...], got_b[...])
    even = place[0] % 2 == 0
    half = lanes((48, 128))
    for p in range(2):
        pair = []
        for k in (2 * p, 2 * p + 1):
            pair.append(edge[:, k * 128 : (k + 1) * 128] + mid_border(above, below, k * 2 + 1))
        moved = roll(pair[0], 64)
        low = jnp.where(half >= 64, moved, pair[1])
        high = jnp.where(half < 64, moved, pair[1])
        here = slice(p * 128, (p + 1) * 128)
        send_a[:, here], send_b[:, here] = to_partners(even, high, low)


def coarse_kernel(
    slabs, narrow, place, skeleton2, inner2, got_a, got_b, plane_a, plane_b, sort,
    solve_h, solve_l, update_h, update_l,
    solved, rest, send_a, send_b,
    parts, vector, product, out_rows,
):
    above, below = from_partners(place[1], narrow, got_a[...], got_b[...])
    plane_above, plane_below = from_partners(place[0], slabs, plane_a[...], plane_b[...])
    half = lanes((48, 128))
    for k in range(4):
        here = slice(k * 128, (k + 1) * 128)
        pack = slice(k // 2 * 128, (k // 2 + 1) * 128)
        up, down = plane_above[:, pack], plane_below[:, pack]
        if k % 2 == 1:
            up, down = roll(up, 64), roll(down, 64)
        value = (
            skeleton2[:, here]
            - inner2[:, here]
            - mid_border(above, below, k * 2)
            - jnp.where(half < 64, down, up)
        )
        top = value.astype(BF16).astype(F32)
        parts[k] = jnp.concatenate([top, value - top], axis=0).astype(BF16)
    arranged = dot(parts[...].reshape(4 * 96, 128), sort[...])
    for child in range(8):
        total = None
        for k in range(4):
            from_columns = slice(child // 4 * 128, (child // 4 + 1) * 128)
            value = (
                arranged[k * 96 : k * 96 + 48, from_columns]
                + arranged[k * 96 + 48 : k * 96 + 96, from_columns]
            )
            moved = roll(value, 32 * (k - child % 4))
            total = moved if total is None else jnp.where(half // 32 == k, moved, total)
        vector[child * 48 : (child + 1) * 48, :] = total
    result = dot3(solve_h[...], solve_l[...], vector[96:, :])
    solution_vector = result[:288]
    for k in range(4):
        out_rows[pl.ds(k, 288, stride=4), :] = roll(solution_vector, -32 * k)
    sol_h, sol_l = halves(solution_vector)
    both = dot(update_h[...], jnp.concatenate([sol_h, sol_l], axis=1))
    product[...] = both[:, :128] + both[:, 128:] + dot(update_l[...], sol_h)
    solved[...] = out_rows[...].T[8:24, :]

    l = lanes((96, 128)) % 4
    sums = []
    for dx in range(3):
        total = None
        for dz in range(3):
            column = None
            for dy in range(3):
                base = (dx * 9 + dy * 3 + dz) * 96
                moved = roll(product[base : base + 96, :], -((dy - 1) * 4 + dz - 1))
                column = moved if column is None else column + moved
            if dz == 0:
                column = jnp.where(l > 0, column, 0.0)
            if dz == 2:
                column = jnp.where(l < 3, column, 0.0)
            total = column if total is None else total + column
        sums.append(total)
    rest[...] = vector[:96, :] - result[288:] - sums[1]
    send_a[...], send_b[...] = to_partners(place[0] % 2 == 0, sums[0], sums[2])


def coarse_edge_kernel(slabs, place, rest, plane_a, plane_b, out, rows):
    above, below = from_partners(place[0], slabs, plane_a[...], plane_b[...])
    value = rest[...] - above - below
    for k in range(4):
        rows[pl.ds(k, 96, stride=4), :] = roll(value, -32 * k)
    out[...] = rows[...].T[4:28, :]


def pair_kernel(place, own, other, out):
    even = place[1] % 2 == 0
    first = jnp.where(even, own[...], other[...])
    second = jnp.where(even, other[...], own[...])
    out[...] = jnp.zeros_like(out)
    out[0:24, :] = first
    out[16:40, :] = out[16:40, :] + second


def gather_kernel(pairs, place, *refs):
    blocks, out, rows = refs[:pairs], refs[pairs], refs[pairs + 1]
    mine = place[1] // 2
    rows[...] = jnp.zeros_like(rows)
    for distance in range(pairs):
        base = pl.multiple_of((mine ^ distance) * 32, 8)
        rows[pl.ds(base, 40), :] = rows[pl.ds(base, 40), :] + blocks[distance][...]
    out[...] = rows[4 : 4 + pairs * 32, :]


def call(kernel, place, operands, outs, scratch=(), flops=0):
    vmem = pl.BlockSpec(memory_space=pltpu.VMEM)
    smem = pl.BlockSpec(memory_space=pltpu.SMEM)
    out_shape = [jax.ShapeDtypeStruct(shape, dtype) for shape, dtype in outs]
    moved = sum(x.size * x.dtype.itemsize for x in list(operands) + out_shape)
    given = ([] if place is None else [place]) + list(operands)
    specs = ([] if place is None else [smem]) + [vmem] * len(operands)
    return pl.pallas_call(
        kernel,
        out_shape=out_shape,
        in_specs=specs,
        out_specs=[vmem] * len(outs),
        scratch_shapes=[pltpu.VMEM(shape, dtype) for shape, dtype in scratch],
        compiler_params=pltpu.CompilerParams(vmem_limit_bytes=VMEM_LIMIT),
        cost_estimate=pl.CostEstimate(flops=flops, bytes_accessed=moved, transcendentals=0),
    )(*given)


def swap(first, second, axis):
    count = lax.axis_size(axis)
    results = []
    for parity, value in enumerate((first, second)):
        pairs = []
        for i in range(parity, count, 2):
            other = (i + 1) % count
            pairs += [(i, other), (other, i)]
        results.append(lax.ppermute(value, axis, pairs))
    return results


def local(rhs, skel1, elim1, update1, skel2, elim2, update2, skel3, elim3, update3):
    slabs, narrow = lax.axis_size("slab"), lax.axis_size("narrow")
    place = jnp.stack([lax.axis_index("slab"), lax.axis_index("narrow")]).astype(jnp.int32)

    solved1, skeleton, inner, edge, send_a, send_b = call(
        fine_kernel,
        place,
        [rhs.reshape(1024, 256), skel1, elim1, update1.reshape(648, 40)],
        [
            ((1024, 160), F32),
            ((4, 24, 1024), F32),
            ((4, 24, 1024), F32),
            ((2, 24, 1024), F32),
            ((24, 384), F32),
            ((24, 384), F32),
        ],
        [
            ((64, 128), F32),
            ((216, 384), F32),
            ((2, 256, 128), F32),
            ((4, 4, 128, 256), BF16),
            ((2, 160, 128), F32),
        ],
        flops=1 << 30,
    )
    got_a, got_b = swap(send_a, send_b, "narrow")
    operators = call(
        operators_kernel,
        None,
        [skel2, elim2, update2.reshape(1296, 144), skel3, elim3, update3.reshape(2592, 288)],
        [((192, 144), BF16)] * 2
        + [((1296, 144), BF16)] * 2
        + [((384, 288), BF16)] * 2
        + [((2592, 288), BF16)] * 2
        + [((256, 256), BF16), ((128, 256), BF16)],
    )
    solve2, update2, solve3, update3 = [operators[2 * i : 2 * i + 2] for i in range(4)]
    sort2, sort3 = operators[8:]

    plane_a, plane_b = swap(
        *call(
            functools.partial(fine_edge_kernel, narrow),
            place,
            [edge, got_a, got_b],
            [((24, 1024), F32)] * 2,
        ),
        "slab",
    )
    solved2, skeleton, inner, edge, send_a, send_b = call(
        functools.partial(mid_kernel, slabs, narrow),
        place,
        [skeleton, inner, got_a, got_b, plane_a, plane_b, sort2, *solve2, *update2],
        [
            ((128, 576), F32),
            ((48, 512), F32),
            ((48, 512), F32),
            ((48, 512), F32),
            ((48, 128), F32),
            ((48, 128), F32),
        ],
        [((16, 48, 256), BF16), ((192, 512), F32), ((1296, 512), F32), ((576, 128), F32)],
        flops=1 << 30,
    )
    got_a, got_b = swap(send_a, send_b, "narrow")
    plane_a, plane_b = swap(
        *call(
            functools.partial(mid_edge_kernel, narrow),
            place,
            [edge, got_a, got_b],
            [((48, 256), F32)] * 2,
        ),
        "slab",
    )
    solved3, rest, send_a, send_b = call(
        functools.partial(coarse_kernel, slabs, narrow),
        place,
        [skeleton, inner, got_a, got_b, plane_a, plane_b, sort3, *solve3, *update3],
        [((16, 1152), F32), ((96, 128), F32), ((96, 128), F32), ((96, 128), F32)],
        [((4, 96, 128), BF16), ((384, 128), F32), ((2592, 128), F32), ((1152, 128), F32)],
        flops=1 << 30,
    )
    plane_a, plane_b = swap(send_a, send_b, "slab")
    (mine,) = call(
        functools.partial(coarse_edge_kernel, slabs),
        place,
        [rest, plane_a, plane_b],
        [((24, 384), F32)],
        [((384, 128), F32)],
    )
    other = lax.ppermute(mine, "narrow", [(i, i ^ 1) for i in range(narrow)])
    (pair,) = call(pair_kernel, place, [mine, other], [((40, 384), F32)])
    pairs = narrow // 2
    blocks = [pair] + [
        lax.ppermute(pair, "narrow", [(i, i ^ (2 * d)) for i in range(narrow)])
        for d in range(1, pairs)
    ]
    (coarse,) = call(
        functools.partial(gather_kernel, pairs),
        place,
        blocks,
        [((pairs * 32, 384), F32)],
        [((pairs * 32 + 8, 384), F32)],
    )
    return (
        solved1.reshape(4, 16, 16, 160),
        solved2.reshape(2, 8, 8, 576),
        solved3.reshape(1, 4, 4, 1152),
        coarse.reshape(1, pairs * 8, 4, 384),
    )


def solution(mesh):
    return jax.shard_map(
        local,
        mesh=mesh,
        in_specs=(P("slab", "narrow", None, None), P(), P(), P(), P(), P(), P(), P(), P(), P()),
        out_specs=(
            P("slab", "narrow", None, None),
            P("slab", "narrow", None, None),
            P("slab", "narrow", None, None),
            P("slab", None, None, None),
        ),
        check_vma=False,
    )
```

profile of v0, /device:TPU:1, one launch (start us, length us, event | category | flops | bytes accessed | tf_op | source)
XLA Modules:
  0.0 69.6 jit_solution(6851557555197849618)
XLA Ops:
  0.7 1.2 %copy-done.7 = f32[4,16,16,256]{3,2,1,0:T(8,128)S(1)} copy-done((f32[4,16,16,256]{3,2,1,0:T(8,128)S(1)}, f32[4,16,16,256]{3,2,1,0:T(8,128)}, u32[]{:S(2)}) %copy-start.7) | copy-done | bytes 1048600
  1.9 1.0 %copy-done.8 = f32[27,24,40]{2,1,0:T(8,128)S(1)} copy-done((f32[27,24,40]{2,1,0:T(8,128)S(1)}, f32[27,24,40]{2,1,0:T(8,128)}, u32[]{:S(2)}) %copy-start.8) | copy-done | bytes 103704
  4.4 7.1 %shard_map.129 = (f32[1024,160]{1,0:T(8,128)}, f32[4,24,1024]{2,1,0:T(8,128)S(1)}, f32[4,24,1024]{2,1,0:T(8,128)S(1)}, f32[2,24,1024]{2,1,0:T(8,128)S(1)}, f32[24,384]{1,0:T(8,128)S(1)}, /*index=5*/f32[24,384]{1,0:T(8,128)S(1)}) custom-call(s32[2]{0:T(128)S(1)} %pad_add_fusion.place, f32[1024,256]{1,0:T(8,128)S(1)} %bitcast.9, f32[24,40]{1,0:T(8,128)S(1)} %copy-done.10, ...), custom_call_target="tpu_custom_call" | custom-call | flops 1073741824 | bytes 2874624 | tf_op jit(solution)/shard_map/pallas_call | solution.py:387
  11.4 3.2 %collective-permute-start = (f32[24,384]{1,0:T(8,128)S(1)}, f32[24,384]{1,0:T(8,128)S(1)}, u32[]{:S(2)}, u32[]{:S(2)}) collective-permute-start(f32[24,384]{1,0:T(8,128)S(1)} %get-tuple-element.37), channel_id=1, source_target_pairs={{0,1},{1,0},{2,3},{3,2},{4,5},{5,4},{6,7},{7,6},{8,9},{9,8},{10,11... | collective-permute-start | bytes 110600 | tf_op jit(solution)/shard_map/ppermute | solution.py:406
  14.7 0.9 %collective-permute-done.got_a = f32[24,384]{1,0:T(8,128)S(1)} collective-permute-done((f32[24,384]{1,0:T(8,128)S(1)}, f32[24,384]{1,0:T(8,128)S(1)}, u32[]{:S(2)}, u32[]{:S(2)}) %collective-permute-start) | collective-permute-done | bytes 36896 | tf_op jit(solution)/shard_map/ppermute | solution.py:406
  15.5 2.8 %collective-permute-done.1.got_b = f32[24,384]{1,0:T(8,128)S(1)} collective-permute-done((f32[24,384]{1,0:T(8,128)S(1)}, f32[24,384]{1,0:T(8,128)S(1)}, u32[]{:S(2)}, u32[]{:S(2)}) %collective-permute-start.1) | collective-permute-done | bytes 36896 | tf_op jit(solution)/shard_map/ppermute | solution.py:406
  19.1 7.0 %collective-permute-start.3 = (f32[24,1024]{1,0:T(8,128)S(1)}, f32[24,1024]{1,0:T(8,128)S(1)}, u32[]{:S(2)}, u32[]{:S(2)}) collective-permute-start(f32[24,1024]{1,0:T(8,128)S(1)} %get-tuple-element.41), channel_id=1, source_target_pairs={{8,16},{16,8},{24,32},{32,24},{40,48},{48,40},{56,64},{64,56},{72,... | collective-permute-start | bytes 294920 | tf_op jit(solution)/shard_map/ppermute | solution.py:406
  26.2 4.9 %shard_map.131 = (bf16[192,144]{1,0:T(8,128)(2,1)S(1)}, bf16[192,144]{1,0:T(8,128)(2,1)S(1)}, bf16[1296,144]{1,0:T(8,128)(2,1)S(1)}, bf16[1296,144]{1,0:T(8,128)...) custom-call(f32[48,144]{1,0:T(8,128)S(1)} %copy-done.6, ...), custom_call_target="tpu_custom_call" | custom-call | bytes 8767488 | tf_op jit(solution)/shard_map/pallas_call | solution.py:387
  31.1 3.9 %shard_map.132 = (f32[128,576]{1,0:T(8,128)}, f32[48,512]{1,0:T(8,128)S(1)}, f32[48,512]{1,0:T(8,128)S(1)}, f32[48,512]{1,0:T(8,128)S(1)}, f32[48,128]{1,0:T(8,128)S(1)}, /*index=5*/f32[48,128]{1,0:T(8,128)S(1)}) custom-call(s32[2]{0:T(128)S(1)} %pad_add_fusion.place, f32[4,24,1024]{2,1,0:T(8,128)S(1)} %get-tuple-element.35.skeleton1, ...), custom_call_target="tpu_custom_call" | custom-call | flops 1073741824 | bytes 2683904 | tf_op jit(solution)/shard_map/pallas_call | solution.py:387
  35.0 1.5 %collective-permute-start.4 = (f32[48,128]{1,0:T(8,128)S(1)}, f32[48,128]{1,0:T(8,128)S(1)}, u32[]{:S(2)}, u32[]{:S(2)}) collective-permute-start(f32[48,128]{1,0:T(8,128)S(1)} %get-tuple-element.50), channel_id=1, source_target_pairs={{0,1},{1,0},{2,3},{3,2},{4,5},{5,4},{6,7},{7,6},{8,9},{9,8},{10,11... | collective-permute-start | bytes 73736 | tf_op jit(solution)/shard_map/ppermute | solution.py:406
  36.5 0.8 %collective-permute-done.4.got_a = f32[48,128]{1,0:T(8,128)S(1)} collective-permute-done((f32[48,128]{1,0:T(8,128)S(1)}, f32[48,128]{1,0:T(8,128)S(1)}, u32[]{:S(2)}, u32[]{:S(2)}) %collective-permute-start.4) | collective-permute-done | bytes 24608 | tf_op jit(solution)/shard_map/ppermute | solution.py:406
  37.3 2.7 %collective-permute-done.5.got_b = f32[48,128]{1,0:T(8,128)S(1)} collective-permute-done((f32[48,128]{1,0:T(8,128)S(1)}, f32[48,128]{1,0:T(8,128)S(1)}, u32[]{:S(2)}, u32[]{:S(2)}) %collective-permute-start.5) | collective-permute-done | bytes 24608 | tf_op jit(solution)/shard_map/ppermute | solution.py:406
  40.8 3.0 %collective-permute-start.7 = (f32[48,256]{1,0:T(8,128)S(1)}, f32[48,256]{1,0:T(8,128)S(1)}, u32[]{:S(2)}, u32[]{:S(2)}) collective-permute-start(f32[48,256]{1,0:T(8,128)S(1)} %get-tuple-element.54), channel_id=1, source_target_pairs={{8,16},{16,8},{24,32},{32,24},{40,48},{48,40},{56,64},{64,56},{72,... | collective-permute-start | bytes 147464 | tf_op jit(solution)/shard_map/ppermute | solution.py:406
  43.8 3.6 %collective-permute-done.7.plane_b = f32[48,256]{1,0:T(8,128)S(1)} collective-permute-done((f32[48,256]{1,0:T(8,128)S(1)}, f32[48,256]{1,0:T(8,128)S(1)}, u32[]{:S(2)}, u32[]{:S(2)}) %collective-permute-start.7) | collective-permute-done | bytes 49184 | tf_op jit(solution)/shard_map/ppermute | solution.py:406
  47.4 2.8 %shard_map.134 = (f32[16,1152]{1,0:T(8,128)S(1)}, f32[96,128]{1,0:T(8,128)S(1)}, f32[96,128]{1,0:T(8,128)S(1)}, f32[96,128]{1,0:T(8,128)S(1)}) custom-call(s32[2]{0:T(128)S(1)} %pad_add_fusion.place, f32[48,512]{1,0:T(8,128)S(1)} %get-tuple-element.48.skeleton2, f32[48,512]{1,0:T(8,128)S(1)} %get-tuple-element.49.inner2, ...), custom_call_target="tpu_custom_call" | custom-call | flops 1073741824 | bytes 4059136 | tf_op jit(solution)/shard_map/pallas_call | solution.py:387
  50.3 2.8 %collective-permute-start.9 = (f32[96,128]{1,0:T(8,128)S(1)}, f32[96,128]{1,0:T(8,128)S(1)}, u32[]{:S(2)}, u32[]{:S(2)}) collective-permute-start(f32[96,128]{1,0:T(8,128)S(1)} %get-tuple-element.63), channel_id=1, source_target_pairs={{8,16},{16,8},{24,32},{32,24},{40,48},{48,40},{56,64},{64,56},{72,... | collective-permute-start | bytes 147464 | tf_op jit(solution)/shard_map/ppermute | solution.py:406
  53.2 3.4 %collective-permute-done.9.plane_b = f32[96,128]{1,0:T(8,128)S(1)} collective-permute-done((f32[96,128]{1,0:T(8,128)S(1)}, f32[96,128]{1,0:T(8,128)S(1)}, u32[]{:S(2)}, u32[]{:S(2)}) %collective-permute-start.9) | collective-permute-done | bytes 49184 | tf_op jit(solution)/shard_map/ppermute | solution.py:406
  56.7 0.8 %shard_map.135.own = f32[24,384]{1,0:T(8,128)S(1)} custom-call(s32[2]{0:T(128)S(1)} %pad_add_fusion.place, f32[96,128]{1,0:T(8,128)S(1)} %get-tuple-element.61.rest, f32[96,128]{1,0:T(8,128)S(1)} %collective-permute-done.8.plane_a, f32[96,128]{1,0:T(8,128)S(1)} %collective-permute-done.9.plane_b), custom_call_target="tpu_custom_call" | custom-call | bytes 184320 | tf_op jit(solution)/shard_map/pallas_call | solution.py:387
  57.4 3.3 %collective-permute-start.10 = (f32[24,384]{1,0:T(8,128)S(1)}, f32[24,384]{1,0:T(8,128)S(1)}, u32[]{:S(2)}, u32[]{:S(2)}) collective-permute-start(f32[24,384]{1,0:T(8,128)S(1)} %shard_map.135.own), channel_id=1, source_target_pairs={{0,1},{1,0},{2,3},{3,2},{4,5},{5,4},{6,7},{7,6},{8,9},{9,8},{10,11... | collective-permute-start | bytes 110600 | tf_op jit(solution)/shard_map/ppermute | solution.py:499
  60.7 0.9 %collective-permute-done.10.other = f32[24,384]{1,0:T(8,128)S(1)} collective-permute-done((f32[24,384]{1,0:T(8,128)S(1)}, f32[24,384]{1,0:T(8,128)S(1)}, u32[]{:S(2)}, u32[]{:S(2)}) %collective-permute-start.10) | collective-permute-done | bytes 36896 | tf_op jit(solution)/shard_map/ppermute | solution.py:499
  62.1 1.6 %collective-permute-start.13 = (f32[40,384]{1,0:T(8,128)S(1)}, f32[40,384]{1,0:T(8,128)S(1)}, u32[]{:S(2)}, u32[]{:S(2)}) collective-permute-start(f32[40,384]{1,0:T(8,128)S(1)} %shard_map.136.refs_0_), channel_id=1, source_target_pairs={{0,6},{1,7},{2,4},{3,5},{4,2},{5,3},{6,0},{7,1},{8,14},{9,15},{10,... | collective-permute-start | bytes 184328 | tf_op jit(solution)/shard_map/ppermute | solution.py:503
  63.7 1.8 %collective-permute-start.11 = (f32[40,384]{1,0:T(8,128)S(1)}, f32[40,384]{1,0:T(8,128)S(1)}, u32[]{:S(2)}, u32[]{:S(2)}) collective-permute-start(f32[40,384]{1,0:T(8,128)S(1)} %shard_map.136.refs_0_), channel_id=1, source_target_pairs={{0,2},{1,3},{2,0},{3,1},{4,6},{5,7},{6,4},{7,5},{8,10},{9,11},{10,... | collective-permute-start | bytes 184328 | tf_op jit(solution)/shard_map/ppermute | solution.py:503
  66.5 1.8 %collective-permute-done.12.refs_2_ = f32[40,384]{1,0:T(8,128)S(1)} collective-permute-done((f32[40,384]{1,0:T(8,128)S(1)}, f32[40,384]{1,0:T(8,128)S(1)}, u32[]{:S(2)}, u32[]{:S(2)}) %collective-permute-start.12) | collective-permute-done | bytes 61472 | tf_op jit(solution)/shard_map/ppermute | solution.py:503
  68.9 0.7 %reshape.39 = f32[1,32,4,384]{3,2,1,0:T(4,128)} reshape(f32[128,384]{1,0:T(8,128)S(1)} %shard_map.137) | data formatting | bytes 393216 | tf_op jit(solution)/shard_map/reshape | solution.py:517
  (38 shorter events, 5.6 us)
Async XLA Ops:
  0.7 1.2 %copy-start.7 = (f32[4,16,16,256]{3,2,1,0:T(8,128)S(1)}, f32[4,16,16,256]{3,2,1,0:T(8,128)}, u32[]{:S(2)}) copy-start(f32[4,16,16,256]{3,2,1,0:T(8,128)} %param.10) | copy-start | bytes 3145732
  1.9 1.0 %copy-start.8 = (f32[27,24,40]{2,1,0:T(8,128)S(1)}, f32[27,24,40]{2,1,0:T(8,128)}, u32[]{:S(2)}) copy-start(f32[27,24,40]{2,1,0:T(8,128)} %param.13) | copy-start | bytes 311044
  2.9 0.7 %copy-start.9 = (f32[40,40]{1,0:T(8,128)S(1)}, f32[40,40]{1,0:T(8,128)}, u32[]{:S(2)}) copy-start(f32[40,40]{1,0:T(8,128)} %elim.1) | copy-start | bytes 19204
  4.3 21.8 %copy-start.2 = (f32[27,48,144]{2,1,0:T(8,128)S(1)}, f32[27,48,144]{2,1,0:T(8,128)}, u32[]{:S(2)}) copy-start(f32[27,48,144]{2,1,0:T(8,128)} %param.16) | copy-start | bytes 2239492
  4.3 21.8 %copy-start.3 = (f32[288,288]{1,0:T(8,128)S(1)}, f32[288,288]{1,0:T(8,128)}, u32[]{:S(2)}) copy-start(f32[288,288]{1,0:T(8,128)} %elim3.1) | copy-start | bytes 995332
  4.3 21.8 %copy-start.4 = (f32[144,144]{1,0:T(8,128)S(1)}, f32[144,144]{1,0:T(8,128)}, u32[]{:S(2)}) copy-start(f32[144,144]{1,0:T(8,128)} %elim2.1) | copy-start | bytes 248836
  4.4 21.8 %copy-start.5 = (f32[96,288]{1,0:T(8,128)S(1)}, f32[96,288]{1,0:T(8,128)}, u32[]{:S(2)}) copy-start(f32[96,288]{1,0:T(8,128)} %skel3.1) | copy-start | bytes 331780
  4.4 21.8 %copy-start.6 = (f32[48,144]{1,0:T(8,128)S(1)}, f32[48,144]{1,0:T(8,128)}, u32[]{:S(2)}) copy-start(f32[48,144]{1,0:T(8,128)} %skel2.1) | copy-start | bytes 82948
  11.4 4.1 %collective-permute-start = (f32[24,384]{1,0:T(8,128)S(1)}, f32[24,384]{1,0:T(8,128)S(1)}, u32[]{:S(2)}, u32[]{:S(2)}) collective-permute-start(f32[24,384]{1,0:T(8,128)S(1)} %get-tuple-element.37), channel_id=1, source_target_pairs={{0,1},{1,0},{2,3},{3,2},{4,5},{5,4},{6,7},{7,6},{8,9},{9,8},{10,11... | collective-permute-start | bytes 110600 | tf_op jit(solution)/shard_map/ppermute | solution.py:406
  14.7 3.7 %collective-permute-start.1 = (f32[24,384]{1,0:T(8,128)S(1)}, f32[24,384]{1,0:T(8,128)S(1)}, u32[]{:S(2)}, u32[]{:S(2)}) collective-permute-start(f32[24,384]{1,0:T(8,128)S(1)} %get-tuple-element.38), channel_id=1, source_target_pairs={{1,2},{2,1},{3,4},{4,3},{5,6},{6,5},{7,0},{0,7},{9,10},{10,9},{11,... | collective-permute-start | bytes 110600 | tf_op jit(solution)/shard_map/ppermute | solution.py:406
  19.0 12.0 %collective-permute-start.2 = (f32[24,1024]{1,0:T(8,128)S(1)}, f32[24,1024]{1,0:T(8,128)S(1)}, u32[]{:S(2)}, u32[]{:S(2)}) collective-permute-start(f32[24,1024]{1,0:T(8,128)S(1)} %get-tuple-element.40), channel_id=1, source_target_pairs={{0,8},{8,0},{16,24},{24,16},{32,40},{40,32},{48,56},{56,48},{64,72... | collective-permute-start | bytes 294920 | tf_op jit(solution)/shard_map/ppermute | solution.py:406
  19.1 11.9 %collective-permute-start.3 = (f32[24,1024]{1,0:T(8,128)S(1)}, f32[24,1024]{1,0:T(8,128)S(1)}, u32[]{:S(2)}, u32[]{:S(2)}) collective-permute-start(f32[24,1024]{1,0:T(8,128)S(1)} %get-tuple-element.41), channel_id=1, source_target_pairs={{8,16},{16,8},{24,32},{32,24},{40,48},{48,40},{56,64},{64,56},{72,... | collective-permute-start | bytes 294920 | tf_op jit(solution)/shard_map/ppermute | solution.py:406
  31.1 16.3 %copy-start = (bf16[2592,288]{1,0:T(8,128)(2,1)S(1)}, bf16[2592,288]{1,0:T(8,128)(2,1)}, u32[]{:S(2)}) copy-start(bf16[2592,288]{1,0:T(8,128)(2,1)} %get-tuple-element.58.update_h) | copy-start | bytes 4478980
  31.1 16.3 %copy-start.1 = (bf16[2592,288]{1,0:T(8,128)(2,1)S(1)}, bf16[2592,288]{1,0:T(8,128)(2,1)}, u32[]{:S(2)}) copy-start(bf16[2592,288]{1,0:T(8,128)(2,1)} %get-tuple-element.59.update_l) | copy-start | bytes 4478980
  35.0 2.3 %collective-permute-start.4 = (f32[48,128]{1,0:T(8,128)S(1)}, f32[48,128]{1,0:T(8,128)S(1)}, u32[]{:S(2)}, u32[]{:S(2)}) collective-permute-start(f32[48,128]{1,0:T(8,128)S(1)} %get-tuple-element.50), channel_id=1, source_target_pairs={{0,1},{1,0},{2,3},{3,2},{4,5},{5,4},{6,7},{7,6},{8,9},{9,8},{10,11... | collective-permute-start | bytes 73736 | tf_op jit(solution)/shard_map/ppermute | solution.py:406
  36.5 3.5 %collective-permute-start.5 = (f32[48,128]{1,0:T(8,128)S(1)}, f32[48,128]{1,0:T(8,128)S(1)}, u32[]{:S(2)}, u32[]{:S(2)}) collective-permute-start(f32[48,128]{1,0:T(8,128)S(1)} %get-tuple-element.51), channel_id=1, source_target_pairs={{1,2},{2,1},{3,4},{4,3},{5,6},{6,5},{7,0},{0,7},{9,10},{10,9},{11,... | collective-permute-start | bytes 73736 | tf_op jit(solution)/shard_map/ppermute | solution.py:406
  40.7 3.1 %collective-permute-start.6 = (f32[48,256]{1,0:T(8,128)S(1)}, f32[48,256]{1,0:T(8,128)S(1)}, u32[]{:S(2)}, u32[]{:S(2)}) collective-permute-start(f32[48,256]{1,0:T(8,128)S(1)} %get-tuple-element.53), channel_id=1, source_target_pairs={{0,8},{8,0},{16,24},{24,16},{32,40},{40,32},{48,56},{56,48},{64,72... | collective-permute-start | bytes 147464 | tf_op jit(solution)/shard_map/ppermute | solution.py:406
  40.8 6.5 %collective-permute-start.7 = (f32[48,256]{1,0:T(8,128)S(1)}, f32[48,256]{1,0:T(8,128)S(1)}, u32[]{:S(2)}, u32[]{:S(2)}) collective-permute-start(f32[48,256]{1,0:T(8,128)S(1)} %get-tuple-element.54), channel_id=1, source_target_pairs={{8,16},{16,8},{24,32},{32,24},{40,48},{48,40},{56,64},{64,56},{72,... | collective-permute-start | bytes 147464 | tf_op jit(solution)/shard_map/ppermute | solution.py:406
  50.2 3.0 %collective-permute-start.8 = (f32[96,128]{1,0:T(8,128)S(1)}, f32[96,128]{1,0:T(8,128)S(1)}, u32[]{:S(2)}, u32[]{:S(2)}) collective-permute-start(f32[96,128]{1,0:T(8,128)S(1)} %get-tuple-element.62), channel_id=1, source_target_pairs={{0,8},{8,0},{16,24},{24,16},{32,40},{40,32},{48,56},{56,48},{64,72... | collective-permute-start | bytes 147464 | tf_op jit(solution)/shard_map/ppermute | solution.py:406
  50.3 6.3 %collective-permute-start.9 = (f32[96,128]{1,0:T(8,128)S(1)}, f32[96,128]{1,0:T(8,128)S(1)}, u32[]{:S(2)}, u32[]{:S(2)}) collective-permute-start(f32[96,128]{1,0:T(8,128)S(1)} %get-tuple-element.63), channel_id=1, source_target_pairs={{8,16},{16,8},{24,32},{32,24},{40,48},{48,40},{56,64},{64,56},{72,... | collective-permute-start | bytes 147464 | tf_op jit(solution)/shard_map/ppermute | solution.py:406
  57.4 4.2 %collective-permute-start.10 = (f32[24,384]{1,0:T(8,128)S(1)}, f32[24,384]{1,0:T(8,128)S(1)}, u32[]{:S(2)}, u32[]{:S(2)}) collective-permute-start(f32[24,384]{1,0:T(8,128)S(1)} %shard_map.135.own), channel_id=1, source_target_pairs={{0,1},{1,0},{2,3},{3,2},{4,5},{5,4},{6,7},{7,6},{8,9},{9,8},{10,11... | collective-permute-start | bytes 110600 | tf_op jit(solution)/shard_map/ppermute | solution.py:499
  62.1 4.4 %collective-permute-start.13 = (f32[40,384]{1,0:T(8,128)S(1)}, f32[40,384]{1,0:T(8,128)S(1)}, u32[]{:S(2)}, u32[]{:S(2)}) collective-permute-start(f32[40,384]{1,0:T(8,128)S(1)} %shard_map.136.refs_0_), channel_id=1, source_target_pairs={{0,6},{1,7},{2,4},{3,5},{4,2},{5,3},{6,0},{7,1},{8,14},{9,15},{10,... | collective-permute-start | bytes 184328 | tf_op jit(solution)/shard_map/ppermute | solution.py:503
  63.7 4.6 %collective-permute-start.12 = (f32[40,384]{1,0:T(8,128)S(1)}, f32[40,384]{1,0:T(8,128)S(1)}, u32[]{:S(2)}, u32[]{:S(2)}) collective-permute-start(f32[40,384]{1,0:T(8,128)S(1)} %shard_map.136.refs_0_), channel_id=1, source_target_pairs={{0,4},{1,5},{2,6},{3,7},{4,0},{5,1},{6,2},{7,3},{8,12},{9,13},{10,... | collective-permute-start | bytes 184328 | tf_op jit(solution)/shard_map/ppermute | solution.py:503
  63.7 4.6 %collective-permute-start.11 = (f32[40,384]{1,0:T(8,128)S(1)}, f32[40,384]{1,0:T(8,128)S(1)}, u32[]{:S(2)}, u32[]{:S(2)}) collective-permute-start(f32[40,384]{1,0:T(8,128)S(1)} %shard_map.136.refs_0_), channel_id=1, source_target_pairs={{0,2},{1,3},{2,0},{3,1},{4,6},{5,7},{6,4},{7,5},{8,10},{9,11},{10,... | collective-permute-start | bytes 184328 | tf_op jit(solution)/shard_map/ppermute | solution.py:503
  (1 other events, 0.7 us)
where the time goes:
time: 69.9 us; the launch traced here: 69.6 us
  starting transfers between devices  24.4 us (35%)
  Pallas kernels  22 us (31%)
  waiting for transfers between devices  17.4 us (25%)
  local copies, waits for them, and re-layouts  5.05 us (7%)
  between operations  0.76 us (1%)
    pallas_call x9, Pallas kernels, call(): pl.pallas_call(kernel, out_shape=out_shape, in_specs=specs, out_specs=[vm...  22 us
    ppermute x10, starting transfers between devices, swap(): results.append(lax.ppermute(value, axis, pairs))  17.7 us
    ppermute x10, waiting for transfers between devices, swap(): results.append(lax.ppermute(value, axis, pairs))  14.4 us
    unnamed x22, local copies, waits for them, and re-layouts  3.66 us
    ppermute x3, starting transfers between devices, local(): lax.ppermute(pair, 'narrow', [(i, i ^ 2 * d) for i in range(narrow)])  3.34 us
    ppermute x1, starting transfers between devices, local(): other = lax.ppermute(mine, 'narrow', [(i, i ^ 1) for i in range(narrow)])  3.29 us
    ppermute x3, waiting for transfers between devices, local(): lax.ppermute(pair, 'narrow', [(i, i ^ 2 * d) for i in range(narrow)])  2.16 us
  transfers between devices with their start and end apart: 14, of which 10 were waited for; matrix products, arithmetic and copies ran while one was open for 1% of the time, Pallas kernels for 7%

commit v1 on v0

v1 whole, which is shorter than its diff:
```python
import functools

import jax
import jax.numpy as jnp
from jax import lax
from jax.experimental import pallas as pl
from jax.experimental.pallas import tpu as pltpu
from jax.sharding import PartitionSpec as P

F32 = jnp.float32
BF16 = jnp.bfloat16
VMEM_LIMIT = 48 * 1024 * 1024


def dot(a, b):
    return lax.dot_general(a, b, (((1,), (0,)), ((), ())), preferred_element_type=F32)


def halves(x):
    high = x.astype(BF16)
    return high, (x - high.astype(F32)).astype(BF16)


def dot3(a_high, a_low, b):
    b_high, b_low = halves(b)
    return dot(a_high, b_high) + dot(a_low, b_high) + dot(a_high, b_low)


def lanes(shape):
    return lax.broadcasted_iota(jnp.int32, shape, len(shape) - 1)


def roll(x, shift):
    size = x.shape[1]
    shift = shift % size
    return x if shift == 0 else pltpu.roll(x, shift, 1)


def stacked(x):
    high = x.astype(BF16).astype(F32)
    zeros = jnp.zeros((8, x.shape[1]), F32)
    return jnp.concatenate([high, high, x - high, zeros], axis=0).astype(BF16)


def packed_left(ref, block, x):
    high = x.astype(BF16).astype(F32)
    base = block * 128
    ref[:, base : base + 40] = high
    ref[:, base + 40 : base + 80] = x - high
    ref[:, base + 80 : base + 120] = high


def to_partners(even, upward, downward):
    return jnp.where(even, upward, downward), jnp.where(even, downward, upward)


def from_partners(axis, count, first, second):
    index = lax.axis_index(axis)
    even = index % 2 == 0
    above = jnp.where(even, first, second)
    below = jnp.where(even, second, first)
    zeros = jnp.zeros_like(above)
    return jnp.where(index < count - 1, above, zeros), jnp.where(index > 0, below, zeros)


def fine_solve_kernel(
    rhs, skel, elim, update, solution_out, skeleton, cat, packed, send_a, send_b,
    planes, skel_in, elim_in, update_in, left_c, left_u, turned, sems,
):
    copies = [
        pltpu.make_async_copy(elim, elim_in, sems.at[0]),
        pltpu.make_async_copy(skel, skel_in, sems.at[1]),
    ]
    for x in range(4):
        here = pl.ds(x * 256, 256)
        copies.append(pltpu.make_async_copy(rhs.at[here], planes.at[here], sems.at[2 + x]))
    copies.append(pltpu.make_async_copy(update, update_in, sems.at[6]))
    for copy in copies:
        copy.start()
    left_c[...] = jnp.zeros_like(left_c)
    left_u[...] = jnp.zeros_like(left_u)
    copies[0].wait()
    copies[1].wait()
    packed_left(left_c, 0, jnp.concatenate([elim_in[...], skel_in[...]], axis=0))
    solve = left_c[...].astype(BF16)
    half = lanes((40, 128))
    ends = [[jnp.zeros((40, 128), F32)] * 3 for _ in range(2)]
    for x in range(4):
        copies[2 + x].wait()
        for part in range(2):
            turned[part] = planes[x * 256 + part * 128 : x * 256 + (part + 1) * 128, :].T
        for k in range(4):
            vector = jnp.concatenate(
                [turned[part, pl.ds(k, 64, stride=4), :] for part in range(2)], axis=1
            )
            product = dot(solve, stacked(vector[24:64]))
            skeleton[x, :, k * 256 : (k + 1) * 256] = vector[:24] - product[40:64]
            solution_vector = product[:40]
            solution_out[k, x] = solution_vector
            cat[k, x] = stacked(solution_vector)
            q, u = divmod(k * 6 + x, 8)
            first = roll(solution_vector[:, :128], 16 * u)
            last = roll(solution_vector[:, 128:], 16 * u + 16)
            ends[0][q] = jnp.where(half // 16 == u, first, ends[0][q])
            ends[1][q] = jnp.where(half // 16 == u, last, ends[1][q])
    copies[6].wait()
    for dx in range(3):
        packed_left(left_u, dx, update_in[dx * 216 : (dx + 1) * 216, :])
    operator = left_u[...].astype(BF16)
    packed[...] = operator
    z = lanes((24, 384)) % 16
    messages = []
    for end, base in ((0, 144), (1, 0)):
        boundary = jnp.concatenate(ends[end], axis=1)
        right = jnp.concatenate([stacked(roll(boundary, 16 * (2 - d))) for d in range(3)], axis=0)
        messages.append(along_z(dot(operator[base : base + 72], right), 24, z, 15))
    send_a[...], send_b[...] = to_partners(lax.axis_index("narrow") % 2 == 0, messages[1], messages[0])


def along_z(product, rows, z, last):
    minus, zero, plus = [product[d * rows : (d + 1) * rows] for d in range(3)]
    return (
        zero
        + jnp.where(z > 0, roll(minus, 1), 0.0)
        + jnp.where(z < last, roll(plus, -1), 0.0)
    )


def fine_plane(operator, cat, k, c):
    first = max(0, c - 2)
    last = min(3, c)
    columns = operator[:, (first - c + 2) * 128 : (last - c + 3) * 128]
    right = cat[k, first : last + 1].reshape((last + 1 - first) * 128, 256)
    product = dot(columns, right)
    lane = lanes((24, 256))
    sums = [along_z(product[dy * 72 : (dy + 1) * 72], 24, lane % 16, 15) for dy in range(3)]
    return (
        sums[1]
        + jnp.where(lane >= 16, roll(sums[0], 16), 0.0)
        + jnp.where(lane < 240, roll(sums[2], -16), 0.0)
    )


def fine_outside_kernel(cat, packed, edge):
    operator = packed[...]
    for k in range(4):
        for side, c in ((0, 0), (1, 5)):
            edge[side, :, k * 256 : (k + 1) * 256] = fine_plane(operator, cat, k, c)


def fine_inside_kernel(cat, packed, solution_in, after, skeleton, solved, rest, out_rows):
    operator = packed[...]
    for k in range(4):
        for x in range(4):
            here = slice(k * 256, (k + 1) * 256)
            rest[x, :, here] = skeleton[x, :, here] - fine_plane(operator, cat, k, x + 1)
    for x in range(4):
        for part in range(2):
            for k in range(4):
                out_rows[part, pl.ds(k, 40, stride=4), :] = solution_in[
                    k, x, :, part * 128 : (part + 1) * 128
                ]
            solved[x * 256 + part * 128 : x * 256 + (part + 1) * 128, :] = out_rows[part].T


def fine_border(above, below, slot):
    half = lanes((24, 128))
    q, u = divmod(slot, 8)
    here = slice(q * 128, (q + 1) * 128)
    start = jnp.where(half < 16, roll(below[:, here], -16 * u), 0.0)
    end = jnp.where(half >= 112, roll(above[:, here], -16 * u - 16), 0.0)
    return start, end


def fine_edge_kernel(narrow, edge, got_a, got_b, send_a, send_b):
    above, below = from_partners("narrow", narrow, got_a[...], got_b[...])
    even = lax.axis_index("slab") % 2 == 0
    for k in range(4):
        planes = []
        for side, c in ((0, 0), (1, 5)):
            start, end = fine_border(above, below, k * 6 + c)
            planes.append(
                (
                    edge[side, :, k * 256 : k * 256 + 128] + start,
                    edge[side, :, k * 256 + 128 : (k + 1) * 256] + end,
                )
            )
        for part in range(2):
            here = slice(k * 256 + part * 128, k * 256 + (part + 1) * 128)
            send_a[:, here], send_b[:, here] = to_partners(even, planes[1][part], planes[0][part])


def operators_mid_kernel(after, skel, elim, update, solve_h, solve_l, update_h, update_l, sort):
    solve_h[...], solve_l[...] = halves(jnp.concatenate([elim[...], skel[...]], axis=0))
    update_h[...], update_l[...] = halves(update[...])
    row = lax.broadcasted_iota(jnp.int32, (256, 256), 0)
    y, z = row // 16, row % 16
    goal = ((y % 2) * 2 + z % 2) * 64 + (y // 2) * 8 + z // 2
    sort[...] = jnp.where(goal == lanes((256, 256)), 1.0, 0.0).astype(BF16)


def operators_coarse_kernel(after, skel, elim, update, solve_h, solve_l, update_h, update_l, sort):
    solve_h[...], solve_l[...] = halves(jnp.concatenate([elim[...], skel[...]], axis=0))
    update_h[...], update_l[...] = halves(update[...])
    row = lax.broadcasted_iota(jnp.int32, (128, 256), 0)
    x, y, z = row // 64, row // 8 % 8, row % 8
    goal = ((x * 2 + y % 2) * 2 + z % 2) * 32 + (y // 2 + 2) * 4 + z // 2
    sort[...] = jnp.where(goal == lanes((128, 256)), 1.0, 0.0).astype(BF16)


def mid_solve_kernel(
    slabs, narrow, rest1, got_a, got_b, plane_a, plane_b, sort, solve_h, solve_l, update_h, update_l,
    solution_out, skeleton, send_a, send_b,
    parts, vector,
):
    above, below = from_partners("narrow", narrow, got_a[...], got_b[...])
    plane_above, plane_below = from_partners("slab", slabs, plane_a[...], plane_b[...])
    for k in range(4):
        for x in range(4):
            start, end = fine_border(above, below, k * 6 + x + 1)
            here = slice(k * 256, (k + 1) * 256)
            value = rest1[x, :, here] - jnp.concatenate([start, end], axis=1)
            if x == 0:
                value = value - plane_below[:, here]
            if x == 3:
                value = value - plane_above[:, here]
            top = value.astype(BF16).astype(F32)
            parts[k * 4 + x] = jnp.concatenate([top, value - top], axis=0).astype(BF16)
    arranged = dot(parts[...].reshape(16 * 48, 256), sort[...])
    half = lanes((24, 128))
    for k in range(4):
        for dx in range(2):
            pair = []
            for x in (dx, 2 + dx):
                base = (k * 4 + x) * 48
                pair.append(arranged[base : base + 24] + arranged[base + 24 : base + 48])
            for dy in range(2):
                first, second = [v[:, dy * 128 : (dy + 1) * 128] for v in pair]
                here = slice(k * 128, (k + 1) * 128)
                child = (dx * 2 + dy) * 2
                vector[child * 24 : child * 24 + 24, here] = jnp.where(
                    half < 64, first, roll(second, 64)
                )
                vector[child * 24 + 24 : child * 24 + 48, here] = jnp.where(
                    half < 64, roll(first, 64), second
                )
    result = dot3(solve_h[...], solve_l[...], vector[48:, :])
    solution_vector = result[:144]
    solution_out[...] = solution_vector
    skeleton[...] = vector[:48, :] - result[144:]

    j = lanes((144, 128)) // 8 % 8
    ends = []
    for end, wanted in enumerate((0, 7)):
        total = None
        for k in range(4):
            block = solution_vector[:, k * 128 : (k + 1) * 128]
            for x in range(2):
                u = k * 2 + x
                moved = roll(block, 8 * (u - wanted) - 64 * x + 64 * end)
                total = moved if total is None else jnp.where(j == u, moved, total)
        ends.append(total)
    spot = lanes((48, 128))
    l = spot % 8
    right = jnp.where(lanes((144, 128)) < 64, ends[0], ends[1])
    sums = [[], []]
    for dx in range(3):
        rows = []
        for dy in (2, 0):
            base = (dx * 9 + dy * 3) * 48
            rows.append(slice(base, base + 144))
        both = [dot3(update_h[r, :], update_l[r, :], right) for r in rows]
        for end in range(2):
            sums[end].append(along_z(both[end], 48, l, 7))
    x = spot // 8 % 2
    messages = []
    for end in range(2):
        minus, zero, plus = sums[end]
        inside = zero + jnp.where(x == 0, roll(plus, -8), roll(minus, 8))
        outside = jnp.where(x == 0, plus, minus)
        if end == 0:
            messages.append(jnp.where(spot < 64, inside, roll(outside, 64)))
        else:
            messages.append(jnp.where(spot < 64, roll(inside, 64), outside))
    send_a[...], send_b[...] = to_partners(lax.axis_index("narrow") % 2 == 0, messages[1], messages[0])


def mid_update_kernel(solution_in, skeleton, update_h, update_l, rest, edge, product):
    product[...] = dot3(update_h[...], update_l[...], solution_in[...])
    lane = lanes((48, 128))
    i, j, l = lane // 64, lane // 8 % 8, lane % 8
    for k in range(4):
        here = slice(k * 128, (k + 1) * 128)
        totals = []
        for dx in range(3):
            sums = []
            for dy in range(3):
                base = (dx * 9 + dy * 3) * 48
                sums.append(along_z(product[base : base + 144, here], 48, l, 7))
            totals.append(
                sums[1]
                + jnp.where(j > 0, roll(sums[0], 8), 0.0)
                + jnp.where(j < 7, roll(sums[2], -8), 0.0)
            )
        minus, zero, plus = totals
        inside = zero + jnp.where(i == 0, roll(plus, 64), roll(minus, 64))
        rest[:, here] = skeleton[:, here] - inside
        edge[:, here] = jnp.where(i == 0, plus, minus)


def mid_border(above, below, k, a):
    lane = lanes((48, 128))
    j = lane // 8 % 8
    total = jnp.zeros((48, 128), F32)
    for x in range(2):
        start = a * 64 + (k * 2 + x) * 8
        here = lane // 64 == x
        total = jnp.where(here & (j == 0), roll(below, x * 64 - start), total)
        total = jnp.where(here & (j == 7), roll(above, x * 64 + 56 - start), total)
    return total


def mid_edge_kernel(narrow, edge, got_a, got_b, send_a, send_b):
    above, below = from_partners("narrow", narrow, got_a[...], got_b[...])
    even = lax.axis_index("slab") % 2 == 0
    half = lanes((48, 128))
    for p in range(2):
        pair = []
        for k in (2 * p, 2 * p + 1):
            pair.append(edge[:, k * 128 : (k + 1) * 128] + mid_border(above, below, k, 1))
        moved = roll(pair[0], 64)
        low = jnp.where(half >= 64, moved, pair[1])
        high = jnp.where(half < 64, moved, pair[1])
        here = slice(p * 128, (p + 1) * 128)
        send_a[:, here], send_b[:, here] = to_partners(even, high, low)


def mid_solved_kernel(after, solution_in, solved, out_rows):
    for k in range(4):
        out_rows[pl.ds(k, 144, stride=4), :] = solution_in[:, k * 128 : (k + 1) * 128]
    solved[...] = out_rows[...].T


def coarse_solve_kernel(
    slabs, narrow, rest2, got_a, got_b, plane_a, plane_b, sort, solve_h, solve_l, update_h, update_l,
    solution_out, skeleton, send_a, send_b,
    parts, vector,
):
    above, below = from_partners("narrow", narrow, got_a[...], got_b[...])
    plane_above, plane_below = from_partners("slab", slabs, plane_a[...], plane_b[...])
    half = lanes((48, 128))
    for k in range(4):
        here = slice(k * 128, (k + 1) * 128)
        pack = slice(k // 2 * 128, (k // 2 + 1) * 128)
        up, down = plane_above[:, pack], plane_below[:, pack]
        if k % 2 == 1:
            up, down = roll(up, 64), roll(down, 64)
        value = rest2[:, here] - mid_border(above, below, k, 0) - jnp.where(half < 64, down, up)
        top = value.astype(BF16).astype(F32)
        parts[k] = jnp.concatenate([top, value - top], axis=0).astype(BF16)
    arranged = dot(parts[...].reshape(4 * 96, 128), sort[...])
    for child in range(8):
        total = None
        for k in range(4):
            from_columns = slice(child // 4 * 128, (child // 4 + 1) * 128)
            value = (
                arranged[k * 96 : k * 96 + 48, from_columns]
                + arranged[k * 96 + 48 : k * 96 + 96, from_columns]
            )
            moved = roll(value, 32 * (k - child % 4))
            total = moved if total is None else jnp.where(half // 32 == k, moved, total)
        vector[child * 48 : (child + 1) * 48, :] = total
    result = dot3(solve_h[...], solve_l[...], vector[96:, :])
    solution_vector = result[:288]
    solution_out[...] = solution_vector
    skeleton[...] = vector[:96, :] - result[288:]
    low = coarse_plane(update_h, update_l, solution_vector, 2)
    high = coarse_plane(update_h, update_l, solution_vector, 0)
    send_a[...], send_b[...] = to_partners(lax.axis_index("slab") % 2 == 0, high, low)


def coarse_plane(update_h, update_l, solution_vector, dx):
    sol_h, sol_l = halves(solution_vector)
    rows = slice(dx * 864, (dx + 1) * 864)
    both = dot(update_h[rows, :], jnp.concatenate([sol_h, sol_l], axis=1))
    product = both[:, :128] + both[:, 128:] + dot(update_l[rows, :], sol_h)
    l = lanes((96, 128)) % 4
    total = None
    for dz in range(3):
        column = None
        for dy in range(3):
            base = (dy * 3 + dz) * 96
            moved = roll(product[base : base + 96, :], -((dy - 1) * 4 + dz - 1))
            column = moved if column is None else column + moved
        if dz == 0:
            column = jnp.where(l > 0, column, 0.0)
        if dz == 2:
            column = jnp.where(l < 3, column, 0.0)
        total = column if total is None else total + column
    return total


def coarse_update_kernel(after, solution_in, skeleton, update_h, update_l, solved, rest, out_rows):
    solution_vector = solution_in[...]
    rest[...] = skeleton[...] - coarse_plane(update_h, update_l, solution_vector, 1)
    for k in range(4):
        out_rows[pl.ds(k, 288, stride=4), :] = roll(solution_vector, -32 * k)
    columns = out_rows[...].T
    for y in range(4):
        solved[y] = columns[8 + y * 4 : 12 + y * 4, :]


def coarse_edge_kernel(slabs, rest, plane_a, plane_b, out, rows):
    above, below = from_partners("slab", slabs, plane_a[...], plane_b[...])
    value = rest[...] - above - below
    for k in range(4):
        rows[pl.ds(k, 96, stride=4), :] = roll(value, -32 * k)
    out[...] = rows[...].T[4:28, :]


def pair_kernel(own, other, out):
    even = lax.axis_index("narrow") % 2 == 0
    first = jnp.where(even, own[...], other[...])
    second = jnp.where(even, other[...], own[...])
    out[0:16, :] = first[0:16]
    out[16:24, :] = first[16:24] + second[0:8]
    out[24:40, :] = second[8:24]


def gather_kernel(pairs, *refs):
    blocks, out, rows = refs[:pairs], refs[pairs], refs[pairs + 1]
    mine = lax.axis_index("narrow") // 2
    rows[...] = jnp.zeros_like(rows)
    for distance in range(pairs):
        base = pl.multiple_of((mine ^ distance) * 32, 8)
        rows[pl.ds(base, 40), :] = rows[pl.ds(base, 40), :] + blocks[distance][...]
    for y in range(pairs * 8):
        out[y] = rows[4 + y * 4 : 8 + y * 4, :]


def call(kernel, operands, outs, scratch=(), flops=0, unread=(), where=pltpu.VMEM, sems=0):
    vmem = pl.BlockSpec(memory_space=pltpu.VMEM)
    out_shape = [jax.ShapeDtypeStruct(shape, dtype) for shape, dtype in outs]
    moved = sum(
        x.size * x.dtype.itemsize
        for x in [v for i, v in enumerate(operands) if i not in unread] + out_shape
    )
    specs = [
        pl.BlockSpec(memory_space=pl.ANY if i in unread else where) for i in range(len(operands))
    ]
    scratch_shapes = [pltpu.VMEM(shape, dtype) for shape, dtype in scratch]
    if sems:
        scratch_shapes.append(pltpu.SemaphoreType.DMA((sems,)))
    return pl.pallas_call(
        kernel,
        out_shape=out_shape,
        in_specs=specs,
        out_specs=[vmem] * len(outs),
        scratch_shapes=scratch_shapes,
        compiler_params=pltpu.CompilerParams(vmem_limit_bytes=VMEM_LIMIT),
        cost_estimate=pl.CostEstimate(flops=flops, bytes_accessed=moved, transcendentals=0),
    )(*operands)


def swap(first, second, axis):
    count = lax.axis_size(axis)
    results = []
    for parity, value in enumerate((first, second)):
        pairs = []
        for i in range(parity, count, 2):
            other = (i + 1) % count
            pairs += [(i, other), (other, i)]
        results.append(lax.ppermute(value, axis, pairs))
    return results


def local(rhs, skel1, elim1, update1, skel2, elim2, update2, skel3, elim3, update3):
    slabs, narrow = lax.axis_size("slab"), lax.axis_size("narrow")

    solution1, skeleton, cat, packed, send_a, send_b = call(
        fine_solve_kernel,
        [rhs.reshape(1024, 256), skel1, elim1, update1.reshape(648, 40)],
        [
            ((4, 4, 40, 256), F32),
            ((4, 24, 1024), F32),
            ((4, 4, 128, 256), BF16),
            ((216, 384), BF16),
            ((24, 384), F32),
            ((24, 384), F32),
        ],
        [
            ((1024, 256), F32),
            ((24, 40), F32),
            ((40, 40), F32),
            ((648, 40), F32),
            ((64, 128), F32),
            ((216, 384), F32),
            ((2, 256, 128), F32),
        ],
        flops=1 << 29,
        where=pltpu.HBM,
        sems=7,
    )
    got_a, got_b = swap(send_a, send_b, "narrow")
    (edge,) = call(fine_outside_kernel, [cat, packed], [((2, 24, 1024), F32)], flops=1 << 30)
    send_a, send_b = call(
        functools.partial(fine_edge_kernel, narrow),
        [edge, got_a, got_b],
        [((24, 1024), F32)] * 2,
    )
    plane_a, plane_b = swap(send_a, send_b, "slab")
    solved1, rest = call(
        fine_inside_kernel,
        [cat, packed, solution1, send_a, skeleton],
        [((1024, 160), F32), ((4, 24, 1024), F32)],
        [((2, 160, 128), F32)],
        flops=1 << 30,
        unread=(3,),
    )
    *solve2, update2_h, update2_l, sort2 = call(
        operators_mid_kernel,
        [send_a, skel2, elim2, update2.reshape(1296, 144)],
        [((192, 144), BF16)] * 2 + [((1296, 144), BF16)] * 2 + [((256, 256), BF16)],
        unread=(0,),
    )

    solution2, skeleton, send_a, send_b = call(
        functools.partial(mid_solve_kernel, slabs, narrow),
        [rest, got_a, got_b, plane_a, plane_b, sort2, *solve2, update2_h, update2_l],
        [((144, 512), F32), ((48, 512), F32), ((48, 128), F32), ((48, 128), F32)],
        [((16, 48, 256), BF16), ((192, 512), F32)],
        flops=1 << 29,
    )
    got_a, got_b = swap(send_a, send_b, "narrow")
    rest, edge = call(
        mid_update_kernel,
        [solution2, skeleton, update2_h, update2_l],
        [((48, 512), F32), ((48, 512), F32)],
        [((1296, 512), F32)],
        flops=1 << 30,
    )
    send_a, send_b = call(
        functools.partial(mid_edge_kernel, narrow),
        [edge, got_a, got_b],
        [((48, 256), F32)] * 2,
    )
    plane_a, plane_b = swap(send_a, send_b, "slab")
    (solved2,) = call(
        mid_solved_kernel,
        [send_a, solution2],
        [((128, 576), F32)],
        [((576, 128), F32)],
        unread=(0,),
    )
    *solve3, update3_h, update3_l, sort3 = call(
        operators_coarse_kernel,
        [send_a, skel3, elim3, update3.reshape(2592, 288)],
        [((384, 288), BF16)] * 2 + [((2592, 288), BF16)] * 2 + [((128, 256), BF16)],
        unread=(0,),
    )

    solution3, skeleton, send_a, send_b = call(
        functools.partial(coarse_solve_kernel, slabs, narrow),
        [rest, got_a, got_b, plane_a, plane_b, sort3, *solve3, update3_h, update3_l],
        [((288, 128), F32), ((96, 128), F32), ((96, 128), F32), ((96, 128), F32)],
        [((4, 96, 128), BF16), ((384, 128), F32)],
        flops=1 << 29,
    )
    plane_a, plane_b = swap(send_a, send_b, "slab")
    solved3, rest = call(
        coarse_update_kernel,
        [send_a, solution3, skeleton, update3_h, update3_l],
        [((4, 4, 1152), F32), ((96, 128), F32)],
        [((1152, 128), F32)],
        flops=1 << 29,
        unread=(0,),
    )
    (mine,) = call(
        functools.partial(coarse_edge_kernel, slabs),
        [rest, plane_a, plane_b],
        [((24, 384), F32)],
        [((384, 128), F32)],
    )
    other = lax.ppermute(mine, "narrow", [(i, i ^ 1) for i in range(narrow)])
    (pair,) = call(pair_kernel, [mine, other], [((40, 384), F32)])
    pairs = narrow // 2
    blocks = [pair] + [
        lax.ppermute(pair, "narrow", [(i, i ^ (2 * d)) for i in range(narrow)])
        for d in range(1, pairs)
    ]
    (coarse,) = call(
        functools.partial(gather_kernel, pairs),
        blocks,
        [((pairs * 8, 4, 384), F32)],
        [((pairs * 32 + 8, 384), F32)],
    )
    return (
        solved1.reshape(4, 16, 16, 160),
        solved2.reshape(2, 8, 8, 576),
        solved3.reshape(1, 4, 4, 1152),
        coarse.reshape(1, pairs * 8, 4, 384),
    )


def solution(mesh):
    return jax.shard_map(
        local,
        mesh=mesh,
        in_specs=(P("slab", "narrow", None, None), P(), P(), P(), P(), P(), P(), P(), P(), P()),
        out_specs=(
            P("slab", "narrow", None, None),
            P("slab", "narrow", None, None),
            P("slab", "narrow", None, None),
            P("slab", None, None, None),
        ),
        check_vma=False,
    )
```

time: 69.9 us -> 57.8 us (0.83)
  waiting for transfers between devices: 17.4 us -> 9.74 us
  Pallas kernels: 22 us -> 17.6 us
  local copies, waits for them, and re-layouts: 5.05 us -> 3.64 us
  starting transfers between devices: 24.4 us -> 25.7 us
    ppermute x10, waiting for transfers between devices: 14.4 us -> 7.16 us  [swap(): results.append(lax.ppermute(value, axis, pairs))]
    pallas_call x9 -> x15, Pallas kernels: 22 us -> 17.6 us  [call(): pl.pallas_call(kernel, out_shape=out_shape, in_specs=specs, out_specs=[vm...]
    reshape x2 -> x0, local copies, waits for them, and re-layouts: 1.39 us -> none  [the longest x1 0.73 us: local(): coarse.reshape(1, pairs * 8, 4, 384)]
    ppermute x10, starting transfers between devices: 17.7 us -> 18.7 us  [swap(): results.append(lax.ppermute(value, axis, pairs))]
    unnamed x22 -> x18, local copies, waits for them, and re-layouts: 3.66 us -> 3.64 us
  transfers between devices with their start and end apart: 14 -> 14, of which waited for: 10 -> 9; matrix products, arithmetic and copies ran while one was open for 1% -> 0% of each run, Pallas kernels for 7% -> 18%
where the time goes in v1:
time: 57.8 us; the launch traced here: 57.5 us
  starting transfers between devices  25.7 us (44%)
  Pallas kernels  17.6 us (30%)
  waiting for transfers between devices  9.74 us (17%)
  local copies, waits for them, and re-layouts  3.64 us (6%)
  between operations  0.74 us (1%)
    ppermute x10, starting transfers between devices, swap(): results.append(lax.ppermute(value, axis, pairs))  18.7 us
    pallas_call x15, Pallas kernels, call(): pl.pallas_call(kernel, out_shape=out_shape, in_specs=specs, out_specs=[vm...  17.6 us
    ppermute x10, waiting for transfers between devices, swap(): results.append(lax.ppermute(value, axis, pairs))  7.16 us
    ppermute x1, starting transfers between devices, local(): other = lax.ppermute(mine, 'narrow', [(i, i ^ 1) for i in range(narrow)])  3.68 us
    unnamed x18, local copies, waits for them, and re-layouts  3.64 us
    ppermute x3, starting transfers between devices, local(): lax.ppermute(pair, 'narrow', [(i, i ^ 2 * d) for i in range(narrow)])  3.34 us
    ppermute x3, waiting for transfers between devices, local(): lax.ppermute(pair, 'narrow', [(i, i ^ 2 * d) for i in range(narrow)])  1.72 us
  transfers between devices with their start and end apart: 14, of which 9 were waited for; matrix products, arithmetic and copies ran while one was open for 0% of the time, Pallas kernels for 18%

profile of v1, /device:TPU:1, one launch (start us, length us, event | category | flops | bytes accessed | tf_op | source)
XLA Modules:
  0.0 57.5 jit_solution(2662529186440842993)
XLA Ops:
  0.6 1.2 %copy-done.5 = f32[4,16,16,256]{3,2,1,0:T(8,128)S(1)} copy-done((f32[4,16,16,256]{3,2,1,0:T(8,128)S(1)}, f32[4,16,16,256]{3,2,1,0:T(8,128)}, u32[]{:S(2)}) %copy-start.5) | copy-done | bytes 1048600
  1.9 1.0 %copy-done.6 = f32[27,24,40]{2,1,0:T(8,128)S(1)} copy-done((f32[27,24,40]{2,1,0:T(8,128)S(1)}, f32[27,24,40]{2,1,0:T(8,128)}, u32[]{:S(2)}) %copy-start.6) | copy-done | bytes 103704
  4.3 2.4 %shard_map.129 = (f32[4,4,40,256]{3,2,1,0:T(8,128)S(1)}, f32[4,24,1024]{2,1,0:T(8,128)S(1)}, bf16[4,4,128,256]{3,2,1,0:T(8,128)(2,1)S(1)}, bf16[216,384]{1,0:T(8...) custom-call(f32[1024,256]{1,0:T(8,128)S(1)} %bitcast.9, f32[24,40]{1,0:T(8,128)S(1)} %copy-done.8, ...), custom_call_target="tpu_custom_call" | custom-call | flops 536870912 | bytes 3499264 | tf_op jit(solution)/shard_map/pallas_call | solution.py:454
  6.7 3.3 %collective-permute-start = (f32[24,384]{1,0:T(8,128)S(1)}, f32[24,384]{1,0:T(8,128)S(1)}, u32[]{:S(2)}, u32[]{:S(2)}) collective-permute-start(f32[24,384]{1,0:T(8,128)S(1)} %get-tuple-element.41), channel_id=1, source_target_pairs={{0,1},{1,0},{2,3},{3,2},{4,5},{5,4},{6,7},{7,6},{8,9},{9,8},{10,11... | collective-permute-start | bytes 110600 | tf_op jit(solution)/shard_map/ppermute | solution.py:473
  10.9 2.5 %collective-permute-done.1.got_b = f32[24,384]{1,0:T(8,128)S(1)} collective-permute-done((f32[24,384]{1,0:T(8,128)S(1)}, f32[24,384]{1,0:T(8,128)S(1)}, u32[]{:S(2)}, u32[]{:S(2)}) %collective-permute-start.1) | collective-permute-done | bytes 36896 | tf_op jit(solution)/shard_map/ppermute | solution.py:473
  13.5 6.4 %collective-permute-start.3 = (f32[24,1024]{1,0:T(8,128)S(1)}, f32[24,1024]{1,0:T(8,128)S(1)}, u32[]{:S(2)}, u32[]{:S(2)}) collective-permute-start(f32[24,1024]{1,0:T(8,128)S(1)} %get-tuple-element.47), channel_id=1, source_target_pairs={{8,16},{16,8},{24,32},{32,24},{40,48},{48,40},{56,64},{64,56},{72,... | collective-permute-start | bytes 294920 | tf_op jit(solution)/shard_map/ppermute | solution.py:473
  20.2 2.5 %shard_map.132 = (f32[1024,160]{1,0:T(8,128)}, f32[4,24,1024]{2,1,0:T(8,128)S(1)}) custom-call(bf16[4,4,128,256]{3,2,1,0:T(8,128)(2,1)S(1)} %get-tuple-element.38.cat, bf16[216,384]{1,0:T(8,128)(2,1)S(1)} %get-tuple-element.39.packed, f32[4,4,40,256]{3,2,1,0:T(8,128)S(1)} %get-tuple-element.40.solution_in, f32[24,1024]{1,0:T(8,128)S(1)} %get-tuple-element.43.after, ...), custom_call_target="tpu_custom_call" | custom-call | flops 1073741824 | bytes 3311616 | tf_op jit(solution)/shard_map/pallas_call | solution.py:454
  22.7 0.9 %collective-permute-done.2.plane_a = f32[24,1024]{1,0:T(8,128)S(1)} collective-permute-done((f32[24,1024]{1,0:T(8,128)S(1)}, f32[24,1024]{1,0:T(8,128)S(1)}, u32[]{:S(2)}, u32[]{:S(2)}) %collective-permute-start.2) | collective-permute-done | bytes 98336 | tf_op jit(solution)/shard_map/ppermute | solution.py:473
  23.6 1.8 %shard_map.134 = (f32[144,512]{1,0:T(8,128)S(1)}, f32[48,512]{1,0:T(8,128)S(1)}, f32[48,128]{1,0:T(8,128)S(1)}, f32[48,128]{1,0:T(8,128)S(1)}) custom-call(f32[4,24,1024]{2,1,0:T(8,128)S(1)} %get-tuple-element.46.rest1, f32[24,384]{1,0:T(8,128)S(1)} %collective-permute-done.got_a, f32[24,384]{1,0:T(8,128)S(1)} %collective-permute-done.1.got_b, ...), custom_call_target="tpu_custom_call" | custom-call | flops 536870912 | bytes 2094080 | tf_op jit(solution)/shard_map/pallas_call | solution.py:454
  25.5 2.5 %collective-permute-start.4 = (f32[48,128]{1,0:T(8,128)S(1)}, f32[48,128]{1,0:T(8,128)S(1)}, u32[]{:S(2)}, u32[]{:S(2)}) collective-permute-start(f32[48,128]{1,0:T(8,128)S(1)} %get-tuple-element.56), channel_id=1, source_target_pairs={{0,1},{1,0},{2,3},{3,2},{4,5},{5,4},{6,7},{7,6},{8,9},{9,8},{10,11... | collective-permute-start | bytes 73736 | tf_op jit(solution)/shard_map/ppermute | solution.py:473
  28.2 1.6 %shard_map.135 = (f32[48,512]{1,0:T(8,128)S(1)}, f32[48,512]{1,0:T(8,128)S(1)}) custom-call(f32[144,512]{1,0:T(8,128)S(1)} %get-tuple-element.53.solution_in, f32[48,512]{1,0:T(8,128)S(1)} %get-tuple-element.54.skeleton, bf16[1296,144]{1,0:T(8,128)(2,1)S(1)} %get-tuple-element.51.update_h, bf16[1296,144]{1,0:T(8,128)(2,1)S(1)} %get-tuple-element.52.update_l), custom_call_target="tpu_custom_call" | custom-call | flops 1073741824 | bytes 1336320 | tf_op jit(solution)/shard_map/pallas_call | solution.py:454
  29.9 1.4 %collective-permute-done.5.got_b = f32[48,128]{1,0:T(8,128)S(1)} collective-permute-done((f32[48,128]{1,0:T(8,128)S(1)}, f32[48,128]{1,0:T(8,128)S(1)}, u32[]{:S(2)}, u32[]{:S(2)}) %collective-permute-start.5) | collective-permute-done | bytes 24608 | tf_op jit(solution)/shard_map/ppermute | solution.py:473
  31.4 3.1 %collective-permute-start.7 = (f32[48,256]{1,0:T(8,128)S(1)}, f32[48,256]{1,0:T(8,128)S(1)}, u32[]{:S(2)}, u32[]{:S(2)}) collective-permute-start(f32[48,256]{1,0:T(8,128)S(1)} %get-tuple-element.60), channel_id=1, source_target_pairs={{8,16},{16,8},{24,32},{32,24},{40,48},{48,40},{56,64},{64,56},{72,... | collective-permute-start | bytes 147464 | tf_op jit(solution)/shard_map/ppermute | solution.py:473
  34.6 2.9 %shard_map.138 = (bf16[384,288]{1,0:T(8,128)(2,1)S(1)}, bf16[384,288]{1,0:T(8,128)(2,1)S(1)}, bf16[2592,288]{1,0:T(8,128)(2,1)S(1)}, bf16[2592,288]{1,0:T(8,128)(2,1)S(1)}, bf16[128,256]{1,0:T(8,128)(2,1)S(1)}) custom-call(f32[48,256]{1,0:T(8,128)S(1)} %get-tuple-element.58.after, f32[96,288]{1,0:T(8,128)S(1)} %copy-done.3, f32[288,288]{1,0:T(8,128)S(1)} %copy-done.1, ...), custom_call_target="tpu_custom_call" | custom-call | bytes 6922240 | tf_op jit(solution)/shard_map/pallas_call | solution.py:454
  37.8 1.9 %shard_map.139 = (f32[288,128]{1,0:T(8,128)S(1)}, f32[96,128]{1,0:T(8,128)S(1)}, f32[96,128]{1,0:T(8,128)S(1)}, f32[96,128]{1,0:T(8,128)S(1)}) custom-call(f32[48,512]{1,0:T(8,128)S(1)} %get-tuple-element.59.rest2, f32[48,128]{1,0:T(8,128)S(1)} %collective-permute-done.4.got_a, f32[48,128]{1,0:T(8,128)S(1)} %collective-permute-done.5.got_b, ...), custom_call_target="tpu_custom_call" | custom-call | flops 536870912 | bytes 4034560 | tf_op jit(solution)/shard_map/pallas_call | solution.py:454
  39.6 3.1 %collective-permute-start.9 = (f32[96,128]{1,0:T(8,128)S(1)}, f32[96,128]{1,0:T(8,128)S(1)}, u32[]{:S(2)}, u32[]{:S(2)}) collective-permute-start(f32[96,128]{1,0:T(8,128)S(1)} %get-tuple-element.71), channel_id=1, source_target_pairs={{8,16},{16,8},{24,32},{32,24},{40,48},{48,40},{56,64},{64,56},{72,... | collective-permute-start | bytes 147464 | tf_op jit(solution)/shard_map/ppermute | solution.py:473
  42.8 1.3 %shard_map.140 = (f32[4,4,1152]{2,1,0:T(4,128)}, f32[96,128]{1,0:T(8,128)S(1)}) custom-call(f32[96,128]{1,0:T(8,128)S(1)} %get-tuple-element.66.after, f32[288,128]{1,0:T(8,128)S(1)} %get-tuple-element.67.solution_in, f32[96,128]{1,0:T(8,128)S(1)} %get-tuple-element.68.skeleton, bf16[2592,288]{1,0:T(8,128)(2,1)S(1)} %get-tuple-element.64.update_h, ...), custom_call_target="tpu_custom_call" | custom-call | flops 536870912 | bytes 3305472 | tf_op jit(solution)/shard_map/pallas_call | solution.py:454
  44.1 1.9 %collective-permute-done.9.plane_b = f32[96,128]{1,0:T(8,128)S(1)} collective-permute-done((f32[96,128]{1,0:T(8,128)S(1)}, f32[96,128]{1,0:T(8,128)S(1)}, u32[]{:S(2)}, u32[]{:S(2)}) %collective-permute-start.9) | collective-permute-done | bytes 49184 | tf_op jit(solution)/shard_map/ppermute | solution.py:473
  46.2 3.7 %collective-permute-start.10 = (f32[24,384]{1,0:T(8,128)S(1)}, f32[24,384]{1,0:T(8,128)S(1)}, u32[]{:S(2)}, u32[]{:S(2)}) collective-permute-start(f32[24,384]{1,0:T(8,128)S(1)} %shard_map.141.own), channel_id=1, source_target_pairs={{0,1},{1,0},{2,3},{3,2},{4,5},{5,4},{6,7},{7,6},{8,9},{9,8},{10,11... | collective-permute-start | bytes 110600 | tf_op jit(solution)/shard_map/ppermute | solution.py:584
  49.9 0.9 %collective-permute-done.10.other = f32[24,384]{1,0:T(8,128)S(1)} collective-permute-done((f32[24,384]{1,0:T(8,128)S(1)}, f32[24,384]{1,0:T(8,128)S(1)}, u32[]{:S(2)}, u32[]{:S(2)}) %collective-permute-start.10) | collective-permute-done | bytes 36896 | tf_op jit(solution)/shard_map/ppermute | solution.py:584
  50.8 1.4 %collective-permute-start.13 = (f32[40,384]{1,0:T(8,128)S(1)}, f32[40,384]{1,0:T(8,128)S(1)}, u32[]{:S(2)}, u32[]{:S(2)}) collective-permute-start(f32[40,384]{1,0:T(8,128)S(1)} %shard_map.142.refs_0_), channel_id=1, source_target_pairs={{0,6},{1,7},{2,4},{3,5},{4,2},{5,3},{6,0},{7,1},{8,14},{9,15},{10,... | collective-permute-start | bytes 184328 | tf_op jit(solution)/shard_map/ppermute | solution.py:588
  52.2 2.0 %collective-permute-start.11 = (f32[40,384]{1,0:T(8,128)S(1)}, f32[40,384]{1,0:T(8,128)S(1)}, u32[]{:S(2)}, u32[]{:S(2)}) collective-permute-start(f32[40,384]{1,0:T(8,128)S(1)} %shard_map.142.refs_0_), channel_id=1, source_target_pairs={{0,2},{1,3},{2,0},{3,1},{4,6},{5,7},{6,4},{7,5},{8,10},{9,11},{10,... | collective-permute-start | bytes 184328 | tf_op jit(solution)/shard_map/ppermute | solution.py:588
  54.1 0.9 %shard_map.137 = f32[128,576]{1,0:T(8,128)} custom-call(f32[48,256]{1,0:T(8,128)S(1)} %get-tuple-element.58.after, f32[144,512]{1,0:T(8,128)S(1)} %get-tuple-element.53.solution_in), custom_call_target="tpu_custom_call" | custom-call | bytes 589824 | tf_op jit(solution)/shard_map/pallas_call | solution.py:454
  55.1 1.6 %collective-permute-done.12.refs_2_ = f32[40,384]{1,0:T(8,128)S(1)} collective-permute-done((f32[40,384]{1,0:T(8,128)S(1)}, f32[40,384]{1,0:T(8,128)S(1)}, u32[]{:S(2)}, u32[]{:S(2)}) %collective-permute-start.12) | collective-permute-done | bytes 61472 | tf_op jit(solution)/shard_map/ppermute | solution.py:588
  (37 shorter events, 4.5 us)
Async XLA Ops:
  0.6 1.2 %copy-start.5 = (f32[4,16,16,256]{3,2,1,0:T(8,128)S(1)}, f32[4,16,16,256]{3,2,1,0:T(8,128)}, u32[]{:S(2)}) copy-start(f32[4,16,16,256]{3,2,1,0:T(8,128)} %param.10) | copy-start | bytes 3145732
  1.9 1.0 %copy-start.6 = (f32[27,24,40]{2,1,0:T(8,128)S(1)}, f32[27,24,40]{2,1,0:T(8,128)}, u32[]{:S(2)}) copy-start(f32[27,24,40]{2,1,0:T(8,128)} %param.13) | copy-start | bytes 311044
  2.8 0.7 %copy-start.7 = (f32[40,40]{1,0:T(8,128)S(1)}, f32[40,40]{1,0:T(8,128)}, u32[]{:S(2)}) copy-start(f32[40,40]{1,0:T(8,128)} %elim.3) | copy-start | bytes 19204
  3.6 0.7 %copy-start.8 = (f32[24,40]{1,0:T(8,128)S(1)}, f32[24,40]{1,0:T(8,128)}, u32[]{:S(2)}) copy-start(f32[24,40]{1,0:T(8,128)} %skel.3) | copy-start | bytes 11524
  6.7 4.2 %collective-permute-start = (f32[24,384]{1,0:T(8,128)S(1)}, f32[24,384]{1,0:T(8,128)S(1)}, u32[]{:S(2)}, u32[]{:S(2)}) collective-permute-start(f32[24,384]{1,0:T(8,128)S(1)} %get-tuple-element.41), channel_id=1, source_target_pairs={{0,1},{1,0},{2,3},{3,2},{4,5},{5,4},{6,7},{7,6},{8,9},{9,8},{10,11... | collective-permute-start | bytes 110600 | tf_op jit(solution)/shard_map/ppermute | solution.py:473
  10.0 3.4 %collective-permute-start.1 = (f32[24,384]{1,0:T(8,128)S(1)}, f32[24,384]{1,0:T(8,128)S(1)}, u32[]{:S(2)}, u32[]{:S(2)}) collective-permute-start(f32[24,384]{1,0:T(8,128)S(1)} %get-tuple-element.42), channel_id=1, source_target_pairs={{1,2},{2,1},{3,4},{4,3},{5,6},{6,5},{7,0},{0,7},{9,10},{10,9},{11,... | collective-permute-start | bytes 110600 | tf_op jit(solution)/shard_map/ppermute | solution.py:473
  10.0 9.9 %copy-start = (f32[27,48,144]{2,1,0:T(8,128)S(1)}, f32[27,48,144]{2,1,0:T(8,128)}, u32[]{:S(2)}) copy-start(f32[27,48,144]{2,1,0:T(8,128)} %param.16) | copy-start | bytes 2239492
  10.0 9.9 %copy-start.2 = (f32[144,144]{1,0:T(8,128)S(1)}, f32[144,144]{1,0:T(8,128)}, u32[]{:S(2)}) copy-start(f32[144,144]{1,0:T(8,128)} %elim.4) | copy-start | bytes 248836
  10.0 9.9 %copy-start.4 = (f32[48,144]{1,0:T(8,128)S(1)}, f32[48,144]{1,0:T(8,128)}, u32[]{:S(2)}) copy-start(f32[48,144]{1,0:T(8,128)} %skel.4) | copy-start | bytes 82948
  13.5 9.2 %collective-permute-start.3 = (f32[24,1024]{1,0:T(8,128)S(1)}, f32[24,1024]{1,0:T(8,128)S(1)}, u32[]{:S(2)}, u32[]{:S(2)}) collective-permute-start(f32[24,1024]{1,0:T(8,128)S(1)} %get-tuple-element.47), channel_id=1, source_target_pairs={{8,16},{16,8},{24,32},{32,24},{40,48},{48,40},{56,64},{64,56},{72,... | collective-permute-start | bytes 294920 | tf_op jit(solution)/shard_map/ppermute | solution.py:473
  19.9 3.8 %collective-permute-start.2 = (f32[24,1024]{1,0:T(8,128)S(1)}, f32[24,1024]{1,0:T(8,128)S(1)}, u32[]{:S(2)}, u32[]{:S(2)}) collective-permute-start(f32[24,1024]{1,0:T(8,128)S(1)} %get-tuple-element.43.after), channel_id=1, source_target_pairs={{0,8},{8,0},{16,24},{24,16},{32,40},{40,32},{48,56},{56,48},{64,72... | collective-permute-start | bytes 294920 | tf_op jit(solution)/shard_map/ppermute | solution.py:473
  25.5 4.4 %collective-permute-start.4 = (f32[48,128]{1,0:T(8,128)S(1)}, f32[48,128]{1,0:T(8,128)S(1)}, u32[]{:S(2)}, u32[]{:S(2)}) collective-permute-start(f32[48,128]{1,0:T(8,128)S(1)} %get-tuple-element.56), channel_id=1, source_target_pairs={{0,1},{1,0},{2,3},{3,2},{4,5},{5,4},{6,7},{7,6},{8,9},{9,8},{10,11... | collective-permute-start | bytes 73736 | tf_op jit(solution)/shard_map/ppermute | solution.py:473
  28.0 3.3 %collective-permute-start.5 = (f32[48,128]{1,0:T(8,128)S(1)}, f32[48,128]{1,0:T(8,128)S(1)}, u32[]{:S(2)}, u32[]{:S(2)}) collective-permute-start(f32[48,128]{1,0:T(8,128)S(1)} %get-tuple-element.57), channel_id=1, source_target_pairs={{1,2},{2,1},{3,4},{4,3},{5,6},{6,5},{7,0},{0,7},{9,10},{10,9},{11,... | collective-permute-start | bytes 73736 | tf_op jit(solution)/shard_map/ppermute | solution.py:473
  28.2 6.4 %copy-start.1 = (f32[288,288]{1,0:T(8,128)S(1)}, f32[288,288]{1,0:T(8,128)}, u32[]{:S(2)}) copy-start(f32[288,288]{1,0:T(8,128)} %elim.5) | copy-start | bytes 995332
  28.2 6.4 %copy-start.3 = (f32[96,288]{1,0:T(8,128)S(1)}, f32[96,288]{1,0:T(8,128)}, u32[]{:S(2)}) copy-start(f32[96,288]{1,0:T(8,128)} %skel.5) | copy-start | bytes 331780
  31.4 6.3 %collective-permute-start.7 = (f32[48,256]{1,0:T(8,128)S(1)}, f32[48,256]{1,0:T(8,128)S(1)}, u32[]{:S(2)}, u32[]{:S(2)}) collective-permute-start(f32[48,256]{1,0:T(8,128)S(1)} %get-tuple-element.60), channel_id=1, source_target_pairs={{8,16},{16,8},{24,32},{32,24},{40,48},{48,40},{56,64},{64,56},{72,... | collective-permute-start | bytes 147464 | tf_op jit(solution)/shard_map/ppermute | solution.py:473
  34.5 3.2 %collective-permute-start.6 = (f32[48,256]{1,0:T(8,128)S(1)}, f32[48,256]{1,0:T(8,128)S(1)}, u32[]{:S(2)}, u32[]{:S(2)}) collective-permute-start(f32[48,256]{1,0:T(8,128)S(1)} %get-tuple-element.58.after), channel_id=1, source_target_pairs={{0,8},{8,0},{16,24},{24,16},{32,40},{40,32},{48,56},{56,48},{64,72... | collective-permute-start | bytes 147464 | tf_op jit(solution)/shard_map/ppermute | solution.py:473
  39.6 6.3 %collective-permute-start.9 = (f32[96,128]{1,0:T(8,128)S(1)}, f32[96,128]{1,0:T(8,128)S(1)}, u32[]{:S(2)}, u32[]{:S(2)}) collective-permute-start(f32[96,128]{1,0:T(8,128)S(1)} %get-tuple-element.71), channel_id=1, source_target_pairs={{8,16},{16,8},{24,32},{32,24},{40,48},{48,40},{56,64},{64,56},{72,... | collective-permute-start | bytes 147464 | tf_op jit(solution)/shard_map/ppermute | solution.py:473
  42.8 3.2 %collective-permute-start.8 = (f32[96,128]{1,0:T(8,128)S(1)}, f32[96,128]{1,0:T(8,128)S(1)}, u32[]{:S(2)}, u32[]{:S(2)}) collective-permute-start(f32[96,128]{1,0:T(8,128)S(1)} %get-tuple-element.66.after), channel_id=1, source_target_pairs={{0,8},{8,0},{16,24},{24,16},{32,40},{40,32},{48,56},{56,48},{64,72... | collective-permute-start | bytes 147464 | tf_op jit(solution)/shard_map/ppermute | solution.py:473
  46.2 4.5 %collective-permute-start.10 = (f32[24,384]{1,0:T(8,128)S(1)}, f32[24,384]{1,0:T(8,128)S(1)}, u32[]{:S(2)}, u32[]{:S(2)}) collective-permute-start(f32[24,384]{1,0:T(8,128)S(1)} %shard_map.141.own), channel_id=1, source_target_pairs={{0,1},{1,0},{2,3},{3,2},{4,5},{5,4},{6,7},{7,6},{8,9},{9,8},{10,11... | collective-permute-start | bytes 110600 | tf_op jit(solution)/shard_map/ppermute | solution.py:584
  50.8 4.4 %collective-permute-start.13 = (f32[40,384]{1,0:T(8,128)S(1)}, f32[40,384]{1,0:T(8,128)S(1)}, u32[]{:S(2)}, u32[]{:S(2)}) collective-permute-start(f32[40,384]{1,0:T(8,128)S(1)} %shard_map.142.refs_0_), channel_id=1, source_target_pairs={{0,6},{1,7},{2,4},{3,5},{4,2},{5,3},{6,0},{7,1},{8,14},{9,15},{10,... | collective-permute-start | bytes 184328 | tf_op jit(solution)/shard_map/ppermute | solution.py:588
  52.2 4.6 %collective-permute-start.12 = (f32[40,384]{1,0:T(8,128)S(1)}, f32[40,384]{1,0:T(8,128)S(1)}, u32[]{:S(2)}, u32[]{:S(2)}) collective-permute-start(f32[40,384]{1,0:T(8,128)S(1)} %shard_map.142.refs_0_), channel_id=1, source_target_pairs={{0,4},{1,5},{2,6},{3,7},{4,0},{5,1},{6,2},{7,3},{8,12},{9,13},{10,... | collective-permute-start | bytes 184328 | tf_op jit(solution)/shard_map/ppermute | solution.py:588
  52.2 4.6 %collective-permute-start.11 = (f32[40,384]{1,0:T(8,128)S(1)}, f32[40,384]{1,0:T(8,128)S(1)}, u32[]{:S(2)}, u32[]{:S(2)}) collective-permute-start(f32[40,384]{1,0:T(8,128)S(1)} %shard_map.142.refs_0_), channel_id=1, source_target_pairs={{0,2},{1,3},{2,0},{3,1},{4,6},{5,7},{6,4},{7,5},{8,10},{9,11},{10,... | collective-permute-start | bytes 184328 | tf_op jit(solution)/shard_map/ppermute | solution.py:588

commit v2 on v1

--- a/solution.py
+++ b/solution.py
@@ -9,7 +9,7 @@
 
 F32 = jnp.float32
 BF16 = jnp.bfloat16
-VMEM_LIMIT = 48 * 1024 * 1024
+VMEM_LIMIT = 20 * 1024 * 1024
 
 
 def dot(a, b):
@@ -63,8 +63,20 @@
     return jnp.where(index < count - 1, above, zeros), jnp.where(index > 0, below, zeros)
 
 
+def fine_ends_kernel(rhs, send_a, send_b, sems):
+    upward = jnp.where(lax.axis_index("narrow") % 2 == 0, 15, 0)
+    copies = [
+        pltpu.make_async_copy(rhs.at[:, upward], send_a, sems.at[0]),
+        pltpu.make_async_copy(rhs.at[:, 15 - upward], send_b, sems.at[1]),
+    ]
+    for copy in copies:
+        copy.start()
+    for copy in copies:
+        copy.wait()
+
+
 def fine_solve_kernel(
-    rhs, skel, elim, update, solution_out, skeleton, cat, packed, send_a, send_b,
+    rhs, skel, elim, update, solution_out, skeleton, cat, packed, solver,
     planes, skel_in, elim_in, update_in, left_c, left_u, turned, sems,
 ):
     copies = [
@@ -83,8 +95,7 @@
     copies[1].wait()
     packed_left(left_c, 0, jnp.concatenate([elim_in[...], skel_in[...]], axis=0))
     solve = left_c[...].astype(BF16)
-    half = lanes((40, 128))
-    ends = [[jnp.zeros((40, 128), F32)] * 3 for _ in range(2)]
+    solver[...] = solve
     for x in range(4):
         copies[2 + x].wait()
         for part in range(2):
@@ -98,23 +109,10 @@
             solution_vector = product[:40]
             solution_out[k, x] = solution_vector
             cat[k, x] = stacked(solution_vector)
-            q, u = divmod(k * 6 + x, 8)
-            first = roll(solution_vector[:, :128], 16 * u)
-            last = roll(solution_vector[:, 128:], 16 * u + 16)
-            ends[0][q] = jnp.where(half // 16 == u, first, ends[0][q])
-            ends[1][q] = jnp.where(half // 16 == u, last, ends[1][q])
     copies[6].wait()
     for dx in range(3):
         packed_left(left_u, dx, update_in[dx * 216 : (dx + 1) * 216, :])
-    operator = left_u[...].astype(BF16)
-    packed[...] = operator
-    z = lanes((24, 384)) % 16
-    messages = []
-    for end, base in ((0, 144), (1, 0)):
-        boundary = jnp.concatenate(ends[end], axis=1)
-        right = jnp.concatenate([stacked(roll(boundary, 16 * (2 - d))) for d in range(3)], axis=0)
-        messages.append(along_z(dot(operator[base : base + 72], right), 24, z, 15))
-    send_a[...], send_b[...] = to_partners(lax.axis_index("narrow") % 2 == 0, messages[1], messages[0])
+    packed[...] = left_u[...].astype(BF16)
 
 
 def along_z(product, rows, z, last):
@@ -163,22 +161,44 @@
             solved[x * 256 + part * 128 : x * 256 + (part + 1) * 128, :] = out_rows[part].T
 
 
-def fine_border(above, below, slot):
+def fine_border(above, below, k, c):
     half = lanes((24, 128))
-    q, u = divmod(slot, 8)
-    here = slice(q * 128, (q + 1) * 128)
-    start = jnp.where(half < 16, roll(below[:, here], -16 * u), 0.0)
-    end = jnp.where(half >= 112, roll(above[:, here], -16 * u - 16), 0.0)
+    here = slice(k * 128, (k + 1) * 128)
+    start = jnp.where(half < 16, roll(below[:, here], -16 * c), 0.0)
+    end = jnp.where(half >= 112, roll(above[:, here], 112 - 16 * c), 0.0)
     return start, end
 
 
-def fine_edge_kernel(narrow, edge, got_a, got_b, send_a, send_b):
+def fine_edge_kernel(
+    narrow, edge, packed, solver, got_a, got_b, sum_above, sum_below, send_a, send_b, turned
+):
     above, below = from_partners("narrow", narrow, got_a[...], got_b[...])
+    turned[...] = jnp.concatenate([below, above], axis=0).T
+    vectors = [turned[pl.ds(k, 64, stride=4), :][24:64] for k in range(4)]
+    solution_vector = dot(solver[...], stacked(jnp.concatenate(vectors, axis=1)))[:40]
+    operator = packed[...]
+    half = lanes((40, 128))
+    z = lanes((24, 512)) % 16
+    sums = []
+    for side, base in ((0, 0), (1, 144)):
+        blocks = []
+        for k in range(4):
+            block = roll(solution_vector[:, k * 128 : (k + 1) * 128], 64 * side)
+            blocks.append(jnp.where(half < 64, block, 0.0))
+        right = []
+        for d in range(3):
+            moved = [roll(block, 16 * (2 - d)) for block in blocks]
+            right.append(stacked(jnp.concatenate(moved, axis=1)))
+        product = dot(operator[base : base + 72], jnp.concatenate(right, axis=0))
+        sums.append(along_z(product, 24, z, 15))
+    below, above = sums
+    sum_below[...] = below
+    sum_above[...] = above
     even = lax.axis_index("slab") % 2 == 0
     for k in range(4):
         planes = []
         for side, c in ((0, 0), (1, 5)):
-            start, end = fine_border(above, below, k * 6 + c)
+            start, end = fine_border(above, below, k, c)
             planes.append(
                 (
                     edge[side, :, k * 256 : k * 256 + 128] + start,
@@ -209,15 +229,14 @@
 
 
 def mid_solve_kernel(
-    slabs, narrow, rest1, got_a, got_b, plane_a, plane_b, sort, solve_h, solve_l, update_h, update_l,
+    slabs, rest1, above, below, plane_a, plane_b, sort, solve_h, solve_l, update_h, update_l,
     solution_out, skeleton, send_a, send_b,
     parts, vector,
 ):
-    above, below = from_partners("narrow", narrow, got_a[...], got_b[...])
     plane_above, plane_below = from_partners("slab", slabs, plane_a[...], plane_b[...])
     for k in range(4):
         for x in range(4):
-            start, end = fine_border(above, below, k * 6 + x + 1)
+            start, end = fine_border(above, below, k, x + 1)
             here = slice(k * 256, (k + 1) * 256)
             value = rest1[x, :, here] - jnp.concatenate([start, end], axis=1)
             if x == 0:
@@ -418,23 +437,20 @@
     out[...] = rows[...].T[4:28, :]
 
 
-def pair_kernel(own, other, out):
-    even = lax.axis_index("narrow") % 2 == 0
-    first = jnp.where(even, own[...], other[...])
-    second = jnp.where(even, other[...], own[...])
-    out[0:16, :] = first[0:16]
-    out[16:24, :] = first[16:24] + second[0:8]
-    out[24:40, :] = second[8:24]
-
-
-def gather_kernel(pairs, *refs):
-    blocks, out, rows = refs[:pairs], refs[pairs], refs[pairs + 1]
-    mine = lax.axis_index("narrow") // 2
+def join_kernel(*refs):
+    for i, block in enumerate(refs[:-1]):
+        refs[-1][i * 24 : (i + 1) * 24, :] = block[...]
+
+
+def gather_kernel(chips, own, other, out, rows):
+    mine = lax.axis_index("narrow")
     rows[...] = jnp.zeros_like(rows)
-    for distance in range(pairs):
-        base = pl.multiple_of((mine ^ distance) * 32, 8)
-        rows[pl.ds(base, 40), :] = rows[pl.ds(base, 40), :] + blocks[distance][...]
-    for y in range(pairs * 8):
+    for distance in range(chips):
+        for parity, blocks in enumerate((own, other)):
+            base = pl.multiple_of((mine ^ (distance * 2 + parity)) * 16, 8)
+            here = pl.ds(base, 24)
+            rows[here, :] = rows[here, :] + blocks[distance * 24 : (distance + 1) * 24, :]
+    for y in range(chips * 8):
         out[y] = rows[4 + y * 4 : 8 + y * 4, :]
 
 
@@ -462,31 +478,45 @@
     )(*operands)
 
 
-def swap(first, second, axis):
-    count = lax.axis_size(axis)
+def swap_narrow(first, second):
+    count = lax.axis_size("narrow")
+    pairs = [[(i, (i + 1 if i % 2 == parity else i - 1) % count) for i in range(count)] for parity in (0, 1)]
+    return [lax.ppermute(value, "narrow", pair) for value, pair in zip((first, second), pairs)]
+
+
+def swap_slab(first, second):
+    slabs, narrow = lax.axis_size("slab"), lax.axis_size("narrow")
     results = []
     for parity, value in enumerate((first, second)):
         pairs = []
-        for i in range(parity, count, 2):
-            other = (i + 1) % count
-            pairs += [(i, other), (other, i)]
-        results.append(lax.ppermute(value, axis, pairs))
+        for i in range(slabs):
+            j = i + 1 if i % 2 == parity else i - 1
+            for n in range(narrow):
+                other = j * narrow + n if 0 <= j < slabs else i * narrow + (n ^ 1)
+                pairs.append((i * narrow + n, other))
+        results.append(lax.ppermute(value, ("slab", "narrow"), pairs))
     return results
 
 
 def local(rhs, skel1, elim1, update1, skel2, elim2, update2, skel3, elim3, update3):
     slabs, narrow = lax.axis_size("slab"), lax.axis_size("narrow")
 
-    solution1, skeleton, cat, packed, send_a, send_b = call(
+    in_hbm = [
+        pltpu.with_memory_space_constraint(x, pltpu.HBM)
+        for x in (rhs, rhs.reshape(1024, 256), skel1, elim1, update1.reshape(648, 40))
+    ]
+    got_a, got_b = swap_narrow(
+        *call(fine_ends_kernel, in_hbm[:1], [((4, 16, 256), F32)] * 2, where=pltpu.HBM, sems=2)
+    )
+    solution1, skeleton, cat, packed, solver = call(
         fine_solve_kernel,
-        [rhs.reshape(1024, 256), skel1, elim1, update1.reshape(648, 40)],
+        in_hbm[1:],
         [
             ((4, 4, 40, 256), F32),
             ((4, 24, 1024), F32),
             ((4, 4, 128, 256), BF16),
             ((216, 384), BF16),
-            ((24, 384), F32),
-            ((24, 384), F32),
+            ((64, 128), BF16),
         ],
         [
             ((1024, 256), F32),
@@ -501,14 +531,15 @@
         where=pltpu.HBM,
         sems=7,
     )
-    got_a, got_b = swap(send_a, send_b, "narrow")
     (edge,) = call(fine_outside_kernel, [cat, packed], [((2, 24, 1024), F32)], flops=1 << 30)
-    send_a, send_b = call(
+    above, below, send_a, send_b = call(
         functools.partial(fine_edge_kernel, narrow),
-        [edge, got_a, got_b],
-        [((24, 1024), F32)] * 2,
-    )
-    plane_a, plane_b = swap(send_a, send_b, "slab")
+        [edge, packed, solver, got_a.reshape(64, 256), got_b.reshape(64, 256)],
+        [((24, 512), F32)] * 2 + [((24, 1024), F32)] * 2,
+        [((256, 128), F32)],
+    )
+    after = send_a
+    plane_a, plane_b = swap_slab(send_a, send_b)
     solved1, rest = call(
         fine_inside_kernel,
         [cat, packed, solution1, send_a, skeleton],
@@ -525,13 +556,13 @@
     )
 
     solution2, skeleton, send_a, send_b = call(
-        functools.partial(mid_solve_kernel, slabs, narrow),
-        [rest, got_a, got_b, plane_a, plane_b, sort2, *solve2, update2_h, update2_l],
+        functools.partial(mid_solve_kernel, slabs),
+        [rest, above, below, plane_a, plane_b, sort2, *solve2, update2_h, update2_l],
         [((144, 512), F32), ((48, 512), F32), ((48, 128), F32), ((48, 128), F32)],
         [((16, 48, 256), BF16), ((192, 512), F32)],
         flops=1 << 29,
     )
-    got_a, got_b = swap(send_a, send_b, "narrow")
+    got_a, got_b = swap_narrow(send_a, send_b)
     rest, edge = call(
         mid_update_kernel,
         [solution2, skeleton, update2_h, update2_l],
@@ -544,7 +575,7 @@
         [edge, got_a, got_b],
         [((48, 256), F32)] * 2,
     )
-    plane_a, plane_b = swap(send_a, send_b, "slab")
+    plane_a, plane_b = swap_slab(send_a, send_b)
     (solved2,) = call(
         mid_solved_kernel,
         [send_a, solution2],
@@ -554,7 +585,7 @@
     )
     *solve3, update3_h, update3_l, sort3 = call(
         operators_coarse_kernel,
-        [send_a, skel3, elim3, update3.reshape(2592, 288)],
+        [after, skel3, elim3, update3.reshape(2592, 288)],
         [((384, 288), BF16)] * 2 + [((2592, 288), BF16)] * 2 + [((128, 256), BF16)],
         unread=(0,),
     )
@@ -566,7 +597,7 @@
         [((4, 96, 128), BF16), ((384, 128), F32)],
         flops=1 << 29,
     )
-    plane_a, plane_b = swap(send_a, send_b, "slab")
+    plane_a, plane_b = swap_slab(send_a, send_b)
     solved3, rest = call(
         coarse_update_kernel,
         [send_a, solution3, skeleton, update3_h, update3_l],
@@ -581,24 +612,24 @@
         [((24, 384), F32)],
         [((384, 128), F32)],
     )
-    other = lax.ppermute(mine, "narrow", [(i, i ^ 1) for i in range(narrow)])
-    (pair,) = call(pair_kernel, [mine, other], [((40, 384), F32)])
-    pairs = narrow // 2
-    blocks = [pair] + [
-        lax.ppermute(pair, "narrow", [(i, i ^ (2 * d)) for i in range(narrow)])
-        for d in range(1, pairs)
+    chips = narrow // 2
+    blocks = [mine] + [
+        lax.ppermute(mine, "narrow", [(i, i ^ (2 * d)) for i in range(narrow)])
+        for d in range(1, chips)
     ]
+    (own,) = call(join_kernel, blocks, [((chips * 24, 384), F32)])
+    other = lax.ppermute(own, "narrow", [(i, i ^ 1) for i in range(narrow)])
     (coarse,) = call(
-        functools.partial(gather_kernel, pairs),
-        blocks,
-        [((pairs * 8, 4, 384), F32)],
-        [((pairs * 32 + 8, 384), F32)],
+        functools.partial(gather_kernel, chips),
+        [own, other],
+        [((chips * 8, 4, 384), F32)],
+        [((chips * 32 + 8, 384), F32)],
     )
     return (
         solved1.reshape(4, 16, 16, 160),
         solved2.reshape(2, 8, 8, 576),
         solved3.reshape(1, 4, 4, 1152),
-        coarse.reshape(1, pairs * 8, 4, 384),
+        coarse.reshape(1, chips * 8, 4, 384),
     )
 
 

time: 57.8 us -> 50 us (0.87)
  the two profiles are of different devices: /device:TPU:1 before, /device:TPU:25 now
where the time goes in v2:
time: 50 us; the launch traced here: 49.7 us
  starting transfers between devices  21.1 us (42%)
  Pallas kernels  17.3 us (35%)
  waiting for transfers between devices  10.5 us (21%)
  between operations  0.78 us (2%)
    pallas_call x16, Pallas kernels, call(): pl.pallas_call(kernel, out_shape=out_shape, in_specs=specs, out_specs=[vm...  17.3 us
    ppermute x6, starting transfers between devices, swap_slab(): results.append(lax.ppermute(value, ('slab', 'narrow'), pairs))  9.68 us
    ppermute x6, waiting for transfers between devices, swap_slab(): results.append(lax.ppermute(value, ('slab', 'narrow'), pairs))  5.2 us
    ppermute x4, starting transfers between devices, swap_narrow(): lax.ppermute(value, 'narrow', pair)  4.83 us
    ppermute x3, waiting for transfers between devices, local(): lax.ppermute(mine, 'narrow', [(i, i ^ 2 * d) for i in range(narrow)])  3.64 us
    ppermute x3, starting transfers between devices, local(): lax.ppermute(mine, 'narrow', [(i, i ^ 2 * d) for i in range(narrow)])  3.49 us
    ppermute x1, starting transfers between devices, local(): other = lax.ppermute(own, 'narrow', [(i, i ^ 1) for i in range(narrow)])  3.06 us
    ppermute x4, waiting for transfers between devices, swap_narrow(): lax.ppermute(value, 'narrow', pair)  1.6 us
  transfers between devices with their start and end apart: 14, of which 7 were waited for; matrix products, arithmetic and copies ran while one was open for 0% of the time, Pallas kernels for 22%

profile of v2, /device:TPU:25, one launch (start us, length us, event | category | flops | bytes accessed | tf_op | source)
XLA Modules:
  0.0 49.7 jit_solution(309566700684113955)
XLA Ops:
  0.6 0.9 %shard_map.131 = (f32[4,16,256]{2,1,0:T(8,128)S(1)}, f32[4,16,256]{2,1,0:T(8,128)S(1)}) custom-call(f32[4,16,16,256]{3,2,1,0:T(8,128)} %rhs.1), custom_call_target="tpu_custom_call" | custom-call | bytes 1179648 | tf_op jit(solution)/shard_map/pallas_call | solution.py:470
  1.5 0.8 %collective-permute-start = (f32[4,16,256]{2,1,0:T(8,128)S(1)}, f32[4,16,256]{2,1,0:T(8,128)S(1)}, u32[]{:S(2)}, u32[]{:S(2)}) collective-permute-start(f32[4,16,256]{2,1,0:T(8,128)S(1)} %get-tuple-element.45), channel_id=1, source_target_pairs={{0,1},{1,0},{2,3},{3,2},{4,5},{5,4},{6,7},{7,6},{8,9},{9,8},{10,11... | collective-permute-start | bytes 196616 | tf_op jit(solution)/shard_map/ppermute | solution.py:484
  2.3 1.2 %collective-permute-start.1 = (f32[4,16,256]{2,1,0:T(8,128)S(1)}, f32[4,16,256]{2,1,0:T(8,128)S(1)}, u32[]{:S(2)}, u32[]{:S(2)}) collective-permute-start(f32[4,16,256]{2,1,0:T(8,128)S(1)} %get-tuple-element.46), channel_id=1, source_target_pairs={{0,7},{1,2},{2,1},{3,4},{4,3},{5,6},{6,5},{7,0},{8,15},{9,10},{10,... | collective-permute-start | bytes 196616 | tf_op jit(solution)/shard_map/ppermute | solution.py:484
  3.5 2.5 %shard_map.129 = (f32[4,4,40,256]{3,2,1,0:T(8,128)S(1)}, f32[4,24,1024]{2,1,0:T(8,128)S(1)}, bf16[4,4,128,256]{3,2,1,0:T(8,128)(2,1)S(1)}, bf16[216,384]{1,0:T(8,128)(2,1)S(1)}, bf16[64,128]{1,0:T(8,128)(2,1)S(1)}) custom-call(f32[1024,256]{1,0:T(8,128)} %bitcast.14, f32[24,40]{1,0:T(8,128)} %skel.3, f32[40,40]{1,0:T(8,128)} %elim.3, f32[648,40]{1,0:T(8,128)} %bitcast.17), custom_call_target="tpu_custom_call" | custom-call | flops 536870912 | bytes 3441920 | tf_op jit(solution)/shard_map/pallas_call | solution.py:470
  6.8 0.8 %shard_map.132 = (f32[24,512]{1,0:T(8,128)S(1)}, f32[24,512]{1,0:T(8,128)S(1)}, f32[24,1024]{1,0:T(8,128)S(1)}, f32[24,1024]{1,0:T(8,128)S(1)}) custom-call(f32[2,24,1024]{2,1,0:T(8,128)S(1)} %shard_map.130.edge, bf16[216,384]{1,0:T(8,128)(2,1)S(1)} %get-tuple-element.42.packed, bf16[64,128]{1,0:T(8,128)(2,1)S(1)} %get-tuple-element.44.solver, ...), custom_call_target="tpu_custom_call" | custom-call | bytes 804864 | tf_op jit(solution)/shard_map/pallas_call | solution.py:470
  7.6 5.8 %collective-permute-start.3 = (f32[24,1024]{1,0:T(8,128)S(1)}, f32[24,1024]{1,0:T(8,128)S(1)}, u32[]{:S(2)}, u32[]{:S(2)}) collective-permute-start(f32[24,1024]{1,0:T(8,128)S(1)} %get-tuple-element.53), channel_id=1, source_target_pairs={{0,1},{1,0},{2,3},{3,2},{4,5},{5,4},{6,7},{7,6},{8,16},{9,17},{10,... | collective-permute-start | bytes 294920 | tf_op jit(solution)/shard_map/ppermute | solution.py:497
  13.8 2.5 %shard_map.133 = (f32[1024,160]{1,0:T(8,128)}, f32[4,24,1024]{2,1,0:T(8,128)S(1)}) custom-call(bf16[4,4,128,256]{3,2,1,0:T(8,128)(2,1)S(1)} %get-tuple-element.41.cat, bf16[216,384]{1,0:T(8,128)(2,1)S(1)} %get-tuple-element.42.packed, f32[4,4,40,256]{3,2,1,0:T(8,128)S(1)} %get-tuple-element.43.solution_in, f32[24,1024]{1,0:T(8,128)S(1)} %get-tuple-element.47.after, ...), custom_call_target="tpu_custom_call" | custom-call | flops 1073741824 | bytes 3311616 | tf_op jit(solution)/shard_map/pallas_call | solution.py:470
  16.3 0.9 %collective-permute-done.2.plane_a = f32[24,1024]{1,0:T(8,128)S(1)} collective-permute-done((f32[24,1024]{1,0:T(8,128)S(1)}, f32[24,1024]{1,0:T(8,128)S(1)}, u32[]{:S(2)}, u32[]{:S(2)}) %collective-permute-start.2) | collective-permute-done | bytes 98336 | tf_op jit(solution)/shard_map/ppermute | solution.py:497
  17.2 1.8 %shard_map.135 = (f32[144,512]{1,0:T(8,128)S(1)}, f32[48,512]{1,0:T(8,128)S(1)}, f32[48,128]{1,0:T(8,128)S(1)}, f32[48,128]{1,0:T(8,128)S(1)}) custom-call(f32[4,24,1024]{2,1,0:T(8,128)S(1)} %get-tuple-element.50.rest1, f32[24,512]{1,0:T(8,128)S(1)} %get-tuple-element.51.above, f32[24,512]{1,0:T(8,128)S(1)} %get-tuple-element.52.below, ...), custom_call_target="tpu_custom_call" | custom-call | flops 536870912 | bytes 2118656 | tf_op jit(solution)/shard_map/pallas_call | solution.py:470
  19.0 2.9 %collective-permute-start.4 = (f32[48,128]{1,0:T(8,128)S(1)}, f32[48,128]{1,0:T(8,128)S(1)}, u32[]{:S(2)}, u32[]{:S(2)}) collective-permute-start(f32[48,128]{1,0:T(8,128)S(1)} %get-tuple-element.62), channel_id=1, source_target_pairs={{0,1},{1,0},{2,3},{3,2},{4,5},{5,4},{6,7},{7,6},{8,9},{9,8},{10,11... | collective-permute-start | bytes 73736 | tf_op jit(solution)/shard_map/ppermute | solution.py:484
  21.9 1.6 %shard_map.136 = (f32[48,512]{1,0:T(8,128)S(1)}, f32[48,512]{1,0:T(8,128)S(1)}) custom-call(f32[144,512]{1,0:T(8,128)S(1)} %get-tuple-element.59.solution_in, f32[48,512]{1,0:T(8,128)S(1)} %get-tuple-element.60.skeleton, bf16[1296,144]{1,0:T(8,128)(2,1)S(1)} %get-tuple-element.57.update_h, bf16[1296,144]{1,0:T(8,128)(2,1)S(1)} %get-tuple-element.58.update_l), custom_call_target="tpu_custom_call" | custom-call | flops 1073741824 | bytes 1336320 | tf_op jit(solution)/shard_map/pallas_call | solution.py:470
  23.6 1.6 %collective-permute-done.5.got_b = f32[48,128]{1,0:T(8,128)S(1)} collective-permute-done((f32[48,128]{1,0:T(8,128)S(1)}, f32[48,128]{1,0:T(8,128)S(1)}, u32[]{:S(2)}, u32[]{:S(2)}) %collective-permute-start.5) | collective-permute-done | bytes 24608 | tf_op jit(solution)/shard_map/ppermute | solution.py:484
  25.4 1.9 %collective-permute-start.7 = (f32[48,256]{1,0:T(8,128)S(1)}, f32[48,256]{1,0:T(8,128)S(1)}, u32[]{:S(2)}, u32[]{:S(2)}) collective-permute-start(f32[48,256]{1,0:T(8,128)S(1)} %get-tuple-element.66), channel_id=1, source_target_pairs={{0,1},{1,0},{2,3},{3,2},{4,5},{5,4},{6,7},{7,6},{8,16},{9,17},{10,... | collective-permute-start | bytes 147464 | tf_op jit(solution)/shard_map/ppermute | solution.py:497
  27.3 0.8 %shard_map.139 = (bf16[384,288]{1,0:T(8,128)(2,1)S(1)}, bf16[384,288]{1,0:T(8,128)(2,1)S(1)}, bf16[2592,288]{1,0:T(8,128)(2,1)S(1)}, bf16[2592,288]{1,0:T(8,128)(2,1)S(1)}, bf16[128,256]{1,0:T(8,128)(2,1)S(1)}) custom-call(f32[24,1024]{1,0:T(8,128)S(1)} %get-tuple-element.47.after, f32[96,288]{1,0:T(8,128)S(1)} %copy-done.4, f32[288,288]{1,0:T(8,128)S(1)} %copy-done.2, ...), custom_call_target="tpu_custom_call" | custom-call | bytes 6922240 | tf_op jit(solution)/shard_map/pallas_call | solution.py:470
  28.1 2.4 %collective-permute-done.7.plane_b = f32[48,256]{1,0:T(8,128)S(1)} collective-permute-done((f32[48,256]{1,0:T(8,128)S(1)}, f32[48,256]{1,0:T(8,128)S(1)}, u32[]{:S(2)}, u32[]{:S(2)}) %collective-permute-start.7) | collective-permute-done | bytes 49184 | tf_op jit(solution)/shard_map/ppermute | solution.py:497
  30.5 1.9 %shard_map.140 = (f32[288,128]{1,0:T(8,128)S(1)}, f32[96,128]{1,0:T(8,128)S(1)}, f32[96,128]{1,0:T(8,128)S(1)}, f32[96,128]{1,0:T(8,128)S(1)}) custom-call(f32[48,512]{1,0:T(8,128)S(1)} %get-tuple-element.65.rest2, f32[48,128]{1,0:T(8,128)S(1)} %collective-permute-done.4.got_a, f32[48,128]{1,0:T(8,128)S(1)} %collective-permute-done.5.got_b, ...), custom_call_target="tpu_custom_call" | custom-call | flops 536870912 | bytes 4034560 | tf_op jit(solution)/shard_map/pallas_call | solution.py:470
  32.4 1.9 %collective-permute-start.9 = (f32[96,128]{1,0:T(8,128)S(1)}, f32[96,128]{1,0:T(8,128)S(1)}, u32[]{:S(2)}, u32[]{:S(2)}) collective-permute-start(f32[96,128]{1,0:T(8,128)S(1)} %get-tuple-element.77), channel_id=1, source_target_pairs={{0,1},{1,0},{2,3},{3,2},{4,5},{5,4},{6,7},{7,6},{8,16},{9,17},{10,... | collective-permute-start | bytes 147464 | tf_op jit(solution)/shard_map/ppermute | solution.py:497
  34.3 1.3 %shard_map.141 = (f32[4,4,1152]{2,1,0:T(4,128)}, f32[96,128]{1,0:T(8,128)S(1)}) custom-call(f32[96,128]{1,0:T(8,128)S(1)} %get-tuple-element.72.after, f32[288,128]{1,0:T(8,128)S(1)} %get-tuple-element.73.solution_in, f32[96,128]{1,0:T(8,128)S(1)} %get-tuple-element.74.skeleton, bf16[2592,288]{1,0:T(8,128)(2,1)S(1)} %get-tuple-element.70.update_h, ...), custom_call_target="tpu_custom_call" | custom-call | flops 536870912 | bytes 3305472 | tf_op jit(solution)/shard_map/pallas_call | solution.py:470
  35.6 1.9 %collective-permute-done.9.plane_b = f32[96,128]{1,0:T(8,128)S(1)} collective-permute-done((f32[96,128]{1,0:T(8,128)S(1)}, f32[96,128]{1,0:T(8,128)S(1)}, u32[]{:S(2)}, u32[]{:S(2)}) %collective-permute-start.9) | collective-permute-done | bytes 49184 | tf_op jit(solution)/shard_map/ppermute | solution.py:497
  37.7 2.8 %collective-permute-start.12 = (f32[24,384]{1,0:T(8,128)S(1)}, f32[24,384]{1,0:T(8,128)S(1)}, u32[]{:S(2)}, u32[]{:S(2)}) collective-permute-start(f32[24,384]{1,0:T(8,128)S(1)} %shard_map.142.refs_0_), channel_id=1, source_target_pairs={{0,6},{1,7},{2,4},{3,5},{4,2},{5,3},{6,0},{7,1},{8,14},{9,15},{10,... | collective-permute-start | bytes 110600 | tf_op jit(solution)/shard_map/ppermute | solution.py:617
  41.9 3.0 %collective-permute-done.11.refs_2_ = f32[24,384]{1,0:T(8,128)S(1)} collective-permute-done((f32[24,384]{1,0:T(8,128)S(1)}, f32[24,384]{1,0:T(8,128)S(1)}, u32[]{:S(2)}, u32[]{:S(2)}) %collective-permute-start.11) | collective-permute-done | bytes 36896 | tf_op jit(solution)/shard_map/ppermute | solution.py:617
  44.9 3.1 %collective-permute-start.13 = (f32[96,384]{1,0:T(8,128)S(1)}, f32[96,384]{1,0:T(8,128)S(1)}, u32[]{:S(2)}, u32[]{:S(2)}) collective-permute-start(f32[96,384]{1,0:T(8,128)S(1)} %shard_map.143.own), channel_id=1, source_target_pairs={{0,1},{1,0},{2,3},{3,2},{4,5},{5,4},{6,7},{7,6},{8,9},{9,8},{10,11... | collective-permute-start | bytes 442376 | tf_op jit(solution)/shard_map/ppermute | solution.py:621
  47.9 0.9 %shard_map.138 = f32[128,576]{1,0:T(8,128)} custom-call(f32[48,256]{1,0:T(8,128)S(1)} %get-tuple-element.64.after, f32[144,512]{1,0:T(8,128)S(1)} %get-tuple-element.59.solution_in), custom_call_target="tpu_custom_call" | custom-call | bytes 589824 | tf_op jit(solution)/shard_map/pallas_call | solution.py:470
  48.9 0.8 %shard_map.144 = f32[32,4,384]{2,1,0:T(4,128)} custom-call(f32[96,384]{1,0:T(8,128)S(1)} %shard_map.143.own, f32[96,384]{1,0:T(8,128)S(1)} %collective-permute-done.13.other), custom_call_target="tpu_custom_call" | custom-call | bytes 491520 | tf_op jit(solution)/shard_map/pallas_call | solution.py:470
  (32 shorter events, 2.9 us)
Async XLA Ops:
  1.5 5.2 %collective-permute-start = (f32[4,16,256]{2,1,0:T(8,128)S(1)}, f32[4,16,256]{2,1,0:T(8,128)S(1)}, u32[]{:S(2)}, u32[]{:S(2)}) collective-permute-start(f32[4,16,256]{2,1,0:T(8,128)S(1)} %get-tuple-element.45), channel_id=1, source_target_pairs={{0,1},{1,0},{2,3},{3,2},{4,5},{5,4},{6,7},{7,6},{8,9},{9,8},{10,11... | collective-permute-start | bytes 196616 | tf_op jit(solution)/shard_map/ppermute | solution.py:484
  2.3 4.5 %collective-permute-start.1 = (f32[4,16,256]{2,1,0:T(8,128)S(1)}, f32[4,16,256]{2,1,0:T(8,128)S(1)}, u32[]{:S(2)}, u32[]{:S(2)}) collective-permute-start(f32[4,16,256]{2,1,0:T(8,128)S(1)} %get-tuple-element.46), channel_id=1, source_target_pairs={{0,7},{1,2},{2,1},{3,4},{4,3},{5,6},{6,5},{7,0},{8,15},{9,10},{10,... | collective-permute-start | bytes 196616 | tf_op jit(solution)/shard_map/ppermute | solution.py:484
  6.0 7.4 %copy-start.1 = (f32[27,48,144]{2,1,0:T(8,128)S(1)}, f32[27,48,144]{2,1,0:T(8,128)}, u32[]{:S(2)}) copy-start(f32[27,48,144]{2,1,0:T(8,128)} %param.16) | copy-start | bytes 2239492
  6.1 7.4 %copy-start.3 = (f32[144,144]{1,0:T(8,128)S(1)}, f32[144,144]{1,0:T(8,128)}, u32[]{:S(2)}) copy-start(f32[144,144]{1,0:T(8,128)} %elim.4) | copy-start | bytes 248836
  6.1 7.4 %copy-start.5 = (f32[48,144]{1,0:T(8,128)S(1)}, f32[48,144]{1,0:T(8,128)}, u32[]{:S(2)}) copy-start(f32[48,144]{1,0:T(8,128)} %skel.4) | copy-start | bytes 82948
  7.6 8.7 %collective-permute-start.3 = (f32[24,1024]{1,0:T(8,128)S(1)}, f32[24,1024]{1,0:T(8,128)S(1)}, u32[]{:S(2)}, u32[]{:S(2)}) collective-permute-start(f32[24,1024]{1,0:T(8,128)S(1)} %get-tuple-element.53), channel_id=1, source_target_pairs={{0,1},{1,0},{2,3},{3,2},{4,5},{5,4},{6,7},{7,6},{8,16},{9,17},{10,... | collective-permute-start | bytes 294920 | tf_op jit(solution)/shard_map/ppermute | solution.py:497
  13.5 3.8 %collective-permute-start.2 = (f32[24,1024]{1,0:T(8,128)S(1)}, f32[24,1024]{1,0:T(8,128)S(1)}, u32[]{:S(2)}, u32[]{:S(2)}) collective-permute-start(f32[24,1024]{1,0:T(8,128)S(1)} %get-tuple-element.47.after), channel_id=1, source_target_pairs={{0,8},{1,9},{2,10},{3,11},{4,12},{5,13},{6,14},{7,15},{8,0},{9,1},... | collective-permute-start | bytes 294920 | tf_op jit(solution)/shard_map/ppermute | solution.py:497
  17.2 10.0 %copy-start.2 = (f32[288,288]{1,0:T(8,128)S(1)}, f32[288,288]{1,0:T(8,128)}, u32[]{:S(2)}) copy-start(f32[288,288]{1,0:T(8,128)} %elim.5) | copy-start | bytes 995332
  19.0 4.5 %collective-permute-start.4 = (f32[48,128]{1,0:T(8,128)S(1)}, f32[48,128]{1,0:T(8,128)S(1)}, u32[]{:S(2)}, u32[]{:S(2)}) collective-permute-start(f32[48,128]{1,0:T(8,128)S(1)} %get-tuple-element.62), channel_id=1, source_target_pairs={{0,1},{1,0},{2,3},{3,2},{4,5},{5,4},{6,7},{7,6},{8,9},{9,8},{10,11... | collective-permute-start | bytes 73736 | tf_op jit(solution)/shard_map/ppermute | solution.py:484
  21.9 3.3 %collective-permute-start.5 = (f32[48,128]{1,0:T(8,128)S(1)}, f32[48,128]{1,0:T(8,128)S(1)}, u32[]{:S(2)}, u32[]{:S(2)}) collective-permute-start(f32[48,128]{1,0:T(8,128)S(1)} %get-tuple-element.63), channel_id=1, source_target_pairs={{0,7},{1,2},{2,1},{3,4},{4,3},{5,6},{6,5},{7,0},{8,15},{9,10},{10,... | collective-permute-start | bytes 73736 | tf_op jit(solution)/shard_map/ppermute | solution.py:484
  21.9 5.4 %copy-start = (f32[27,96,288]{2,1,0:T(8,128)S(1)}, f32[27,96,288]{2,1,0:T(8,128)}, u32[]{:S(2)}) copy-start(f32[27,96,288]{2,1,0:T(8,128)} %param.19) | copy-start | bytes 8957956
  21.9 5.4 %copy-start.4 = (f32[96,288]{1,0:T(8,128)S(1)}, f32[96,288]{1,0:T(8,128)}, u32[]{:S(2)}) copy-start(f32[96,288]{1,0:T(8,128)} %skel.5) | copy-start | bytes 331780
  25.4 5.1 %collective-permute-start.7 = (f32[48,256]{1,0:T(8,128)S(1)}, f32[48,256]{1,0:T(8,128)S(1)}, u32[]{:S(2)}, u32[]{:S(2)}) collective-permute-start(f32[48,256]{1,0:T(8,128)S(1)} %get-tuple-element.66), channel_id=1, source_target_pairs={{0,1},{1,0},{2,3},{3,2},{4,5},{5,4},{6,7},{7,6},{8,16},{9,17},{10,... | collective-permute-start | bytes 147464 | tf_op jit(solution)/shard_map/ppermute | solution.py:497
  27.3 3.2 %collective-permute-start.6 = (f32[48,256]{1,0:T(8,128)S(1)}, f32[48,256]{1,0:T(8,128)S(1)}, u32[]{:S(2)}, u32[]{:S(2)}) collective-permute-start(f32[48,256]{1,0:T(8,128)S(1)} %get-tuple-element.64.after), channel_id=1, source_target_pairs={{0,8},{1,9},{2,10},{3,11},{4,12},{5,13},{6,14},{7,15},{8,0},{9,1},... | collective-permute-start | bytes 147464 | tf_op jit(solution)/shard_map/ppermute | solution.py:497
  32.4 5.1 %collective-permute-start.9 = (f32[96,128]{1,0:T(8,128)S(1)}, f32[96,128]{1,0:T(8,128)S(1)}, u32[]{:S(2)}, u32[]{:S(2)}) collective-permute-start(f32[96,128]{1,0:T(8,128)S(1)} %get-tuple-element.77), channel_id=1, source_target_pairs={{0,1},{1,0},{2,3},{3,2},{4,5},{5,4},{6,7},{7,6},{8,16},{9,17},{10,... | collective-permute-start | bytes 147464 | tf_op jit(solution)/shard_map/ppermute | solution.py:497
  34.3 3.2 %collective-permute-start.8 = (f32[96,128]{1,0:T(8,128)S(1)}, f32[96,128]{1,0:T(8,128)S(1)}, u32[]{:S(2)}, u32[]{:S(2)}) collective-permute-start(f32[96,128]{1,0:T(8,128)S(1)} %get-tuple-element.72.after), channel_id=1, source_target_pairs={{0,8},{1,9},{2,10},{3,11},{4,12},{5,13},{6,14},{7,15},{8,0},{9,1},... | collective-permute-start | bytes 147464 | tf_op jit(solution)/shard_map/ppermute | solution.py:497
  37.7 4.2 %collective-permute-start.12 = (f32[24,384]{1,0:T(8,128)S(1)}, f32[24,384]{1,0:T(8,128)S(1)}, u32[]{:S(2)}, u32[]{:S(2)}) collective-permute-start(f32[24,384]{1,0:T(8,128)S(1)} %shard_map.142.refs_0_), channel_id=1, source_target_pairs={{0,6},{1,7},{2,4},{3,5},{4,2},{5,3},{6,0},{7,1},{8,14},{9,15},{10,... | collective-permute-start | bytes 110600 | tf_op jit(solution)/shard_map/ppermute | solution.py:617
  40.5 4.3 %collective-permute-start.11 = (f32[24,384]{1,0:T(8,128)S(1)}, f32[24,384]{1,0:T(8,128)S(1)}, u32[]{:S(2)}, u32[]{:S(2)}) collective-permute-start(f32[24,384]{1,0:T(8,128)S(1)} %shard_map.142.refs_0_), channel_id=1, source_target_pairs={{0,4},{1,5},{2,6},{3,7},{4,0},{5,1},{6,2},{7,3},{8,12},{9,13},{10,... | collective-permute-start | bytes 110600 | tf_op jit(solution)/shard_map/ppermute | solution.py:617
  40.6 4.3 %collective-permute-start.10 = (f32[24,384]{1,0:T(8,128)S(1)}, f32[24,384]{1,0:T(8,128)S(1)}, u32[]{:S(2)}, u32[]{:S(2)}) collective-permute-start(f32[24,384]{1,0:T(8,128)S(1)} %shard_map.142.refs_0_), channel_id=1, source_target_pairs={{0,2},{1,3},{2,0},{3,1},{4,6},{5,7},{6,4},{7,5},{8,10},{9,11},{10,... | collective-permute-start | bytes 110600 | tf_op jit(solution)/shard_map/ppermute | solution.py:617
  44.9 4.1 %collective-permute-start.13 = (f32[96,384]{1,0:T(8,128)S(1)}, f32[96,384]{1,0:T(8,128)S(1)}, u32[]{:S(2)}, u32[]{:S(2)}) collective-permute-start(f32[96,384]{1,0:T(8,128)S(1)} %shard_map.143.own), channel_id=1, source_target_pairs={{0,1},{1,0},{2,3},{3,2},{4,5},{5,4},{6,7},{7,6},{8,9},{9,8},{10,11... | collective-permute-start | bytes 442376 | tf_op jit(solution)/shard_map/ppermute | solution.py:621

commit v3 on v2

--- a/solution.py
+++ b/solution.py
@@ -76,28 +76,14 @@
 
 
 def fine_solve_kernel(
-    rhs, skel, elim, update, solution_out, skeleton, cat, packed, solver,
-    planes, skel_in, elim_in, update_in, left_c, left_u, turned, sems,
+    planes, skel, elim, update, solution_out, skeleton, cat, packed, solver, left_c, left_u, turned
 ):
-    copies = [
-        pltpu.make_async_copy(elim, elim_in, sems.at[0]),
-        pltpu.make_async_copy(skel, skel_in, sems.at[1]),
-    ]
-    for x in range(4):
-        here = pl.ds(x * 256, 256)
-        copies.append(pltpu.make_async_copy(rhs.at[here], planes.at[here], sems.at[2 + x]))
-    copies.append(pltpu.make_async_copy(update, update_in, sems.at[6]))
-    for copy in copies:
-        copy.start()
     left_c[...] = jnp.zeros_like(left_c)
     left_u[...] = jnp.zeros_like(left_u)
-    copies[0].wait()
-    copies[1].wait()
-    packed_left(left_c, 0, jnp.concatenate([elim_in[...], skel_in[...]], axis=0))
+    packed_left(left_c, 0, jnp.concatenate([elim[...], skel[...]], axis=0))
     solve = left_c[...].astype(BF16)
     solver[...] = solve
     for x in range(4):
-        copies[2 + x].wait()
         for part in range(2):
             turned[part] = planes[x * 256 + part * 128 : x * 256 + (part + 1) * 128, :].T
         for k in range(4):
@@ -109,9 +95,8 @@
             solution_vector = product[:40]
             solution_out[k, x] = solution_vector
             cat[k, x] = stacked(solution_vector)
-    copies[6].wait()
     for dx in range(3):
-        packed_left(left_u, dx, update_in[dx * 216 : (dx + 1) * 216, :])
+        packed_left(left_u, dx, update[dx * 216 : (dx + 1) * 216, :])
     packed[...] = left_u[...].astype(BF16)
 
 
@@ -501,16 +486,19 @@
 def local(rhs, skel1, elim1, update1, skel2, elim2, update2, skel3, elim3, update3):
     slabs, narrow = lax.axis_size("slab"), lax.axis_size("narrow")
 
-    in_hbm = [
-        pltpu.with_memory_space_constraint(x, pltpu.HBM)
-        for x in (rhs, rhs.reshape(1024, 256), skel1, elim1, update1.reshape(648, 40))
-    ]
     got_a, got_b = swap_narrow(
-        *call(fine_ends_kernel, in_hbm[:1], [((4, 16, 256), F32)] * 2, where=pltpu.HBM, sems=2)
+        *call(
+            fine_ends_kernel,
+            [pltpu.with_memory_space_constraint(rhs, pltpu.HBM)],
+            [((4, 16, 256), F32)] * 2,
+            flops=1 << 31,
+            where=pltpu.HBM,
+            sems=2,
+        )
     )
     solution1, skeleton, cat, packed, solver = call(
         fine_solve_kernel,
-        in_hbm[1:],
+        [rhs.reshape(1024, 256), skel1, elim1, update1.reshape(648, 40)],
         [
             ((4, 4, 40, 256), F32),
             ((4, 24, 1024), F32),
@@ -519,17 +507,11 @@
             ((64, 128), BF16),
         ],
         [
-            ((1024, 256), F32),
-            ((24, 40), F32),
-            ((40, 40), F32),
-            ((648, 40), F32),
             ((64, 128), F32),
             ((216, 384), F32),
             ((2, 256, 128), F32),
         ],
         flops=1 << 29,
-        where=pltpu.HBM,
-        sems=7,
     )
     (edge,) = call(fine_outside_kernel, [cat, packed], [((2, 24, 1024), F32)], flops=1 << 30)
     above, below, send_a, send_b = call(

time: 50 us -> 49.4 us (0.988)
  Pallas kernels: 17.3 us -> 15.5 us
  waiting for transfers between devices: 10.5 us -> 11.4 us
    pallas_call x16, Pallas kernels: 17.3 us -> 15.5 us  [call(): pl.pallas_call(kernel, out_shape=out_shape, in_specs=specs, out_specs=[vm...]
    ppermute x4, waiting for transfers between devices: 1.6 us -> 2.71 us  [swap_narrow(): lax.ppermute(value, 'narrow', pair)]
    ppermute x3, starting transfers between devices: 3.49 us -> 4.11 us  [local(): lax.ppermute(mine, 'narrow', [(i, i ^ 2 * d) for i in range(narrow)])]
  transfers between devices with their start and end apart: 14 -> 14, of which waited for: 7 -> 8; matrix products, arithmetic and copies ran while one was open for 0% -> 0% of each run, Pallas kernels for 22% -> 18%
where the time goes in v3:
time: 49.4 us; the launch traced here: 49.3 us
  starting transfers between devices  21.5 us (44%)
  Pallas kernels  15.5 us (31%)
  waiting for transfers between devices  11.4 us (23%)
  between operations  0.81 us (2%)
    pallas_call x16, Pallas kernels, call(): pl.pallas_call(kernel, out_shape=out_shape, in_specs=specs, out_specs=[vm...  15.5 us
    ppermute x6, starting transfers between devices, swap_slab(): results.append(lax.ppermute(value, ('slab', 'narrow'), pairs))  9.67 us
    ppermute x6, waiting for transfers between devices, swap_slab(): results.append(lax.ppermute(value, ('slab', 'narrow'), pairs))  4.96 us
    ppermute x4, starting transfers between devices, swap_narrow(): lax.ppermute(value, 'narrow', pair)  4.65 us
    ppermute x3, starting transfers between devices, local(): lax.ppermute(mine, 'narrow', [(i, i ^ 2 * d) for i in range(narrow)])  4.11 us
    ppermute x3, waiting for transfers between devices, local(): lax.ppermute(mine, 'narrow', [(i, i ^ 2 * d) for i in range(narrow)])  3.64 us
    ppermute x1, starting transfers between devices, local(): other = lax.ppermute(own, 'narrow', [(i, i ^ 1) for i in range(narrow)])  3.06 us
    ppermute x4, waiting for transfers between devices, swap_narrow(): lax.ppermute(value, 'narrow', pair)  2.71 us
  transfers between devices with their start and end apart: 14, of which 8 were waited for; matrix products, arithmetic and copies ran while one was open for 0% of the time, Pallas kernels for 18%

profile of v3, /device:TPU:25, one launch (start us, length us, event | category | flops | bytes accessed | tf_op | source)
XLA Modules:
  0.0 49.3 jit_solution(14267635189460744422)
XLA Ops:
  0.7 1.0 %shard_map.131 = (f32[4,16,256]{2,1,0:T(8,128)S(1)}, f32[4,16,256]{2,1,0:T(8,128)S(1)}) custom-call(f32[4,16,16,256]{3,2,1,0:T(8,128)} %rhs.1), custom_call_target="tpu_custom_call" | custom-call | flops 2147483648 | bytes 1179648 | tf_op jit(solution)/shard_map/pallas_call | solution.py:455
  1.7 0.8 %collective-permute-start = (f32[4,16,256]{2,1,0:T(8,128)S(1)}, f32[4,16,256]{2,1,0:T(8,128)S(1)}, u32[]{:S(2)}, u32[]{:S(2)}) collective-permute-start(f32[4,16,256]{2,1,0:T(8,128)S(1)} %get-tuple-element.45), channel_id=1, source_target_pairs={{0,1},{1,0},{2,3},{3,2},{4,5},{5,4},{6,7},{7,6},{8,9},{9,8},{10,11... | collective-permute-start | bytes 196616 | tf_op jit(solution)/shard_map/ppermute | solution.py:469
  2.4 1.2 %collective-permute-start.1 = (f32[4,16,256]{2,1,0:T(8,128)S(1)}, f32[4,16,256]{2,1,0:T(8,128)S(1)}, u32[]{:S(2)}, u32[]{:S(2)}) collective-permute-start(f32[4,16,256]{2,1,0:T(8,128)S(1)} %get-tuple-element.46), channel_id=1, source_target_pairs={{0,7},{1,2},{2,1},{3,4},{4,3},{5,6},{6,5},{7,0},{8,15},{9,10},{10,... | collective-permute-start | bytes 196616 | tf_op jit(solution)/shard_map/ppermute | solution.py:469
  3.7 0.7 %shard_map.129 = (f32[4,4,40,256]{3,2,1,0:T(8,128)S(1)}, f32[4,24,1024]{2,1,0:T(8,128)S(1)}, bf16[4,4,128,256]{3,2,1,0:T(8,128)(2,1)S(1)}, bf16[216,384]{1,0:T(8,128)(2,1)S(1)}, bf16[64,128]{1,0:T(8,128)(2,1)S(1)}) custom-call(f32[1024,256]{1,0:T(8,128)S(1)} %bitcast.14, f32[24,40]{1,0:T(8,128)S(1)} %copy-done.9, f32[40,40]{1,0:T(8,128)S(1)} %copy-done.8, ...), custom_call_target="tpu_custom_call" | custom-call | flops 536870912 | bytes 3441920 | tf_op jit(solution)/shard_map/pallas_call | solution.py:455
  5.1 1.3 %collective-permute-done.1 = f32[4,16,256]{2,1,0:T(8,128)S(1)} collective-permute-done((f32[4,16,256]{2,1,0:T(8,128)S(1)}, f32[4,16,256]{2,1,0:T(8,128)S(1)}, u32[]{:S(2)}, u32[]{:S(2)}) %collective-permute-start.1) | collective-permute-done | bytes 65568 | tf_op jit(solution)/shard_map/ppermute | solution.py:469
  6.4 0.8 %shard_map.132 = (f32[24,512]{1,0:T(8,128)S(1)}, f32[24,512]{1,0:T(8,128)S(1)}, f32[24,1024]{1,0:T(8,128)S(1)}, f32[24,1024]{1,0:T(8,128)S(1)}) custom-call(f32[2,24,1024]{2,1,0:T(8,128)S(1)} %shard_map.130.edge, bf16[216,384]{1,0:T(8,128)(2,1)S(1)} %get-tuple-element.42.packed, bf16[64,128]{1,0:T(8,128)(2,1)S(1)} %get-tuple-element.44.solver, ...), custom_call_target="tpu_custom_call" | custom-call | bytes 804864 | tf_op jit(solution)/shard_map/pallas_call | solution.py:455
  7.3 5.8 %collective-permute-start.3 = (f32[24,1024]{1,0:T(8,128)S(1)}, f32[24,1024]{1,0:T(8,128)S(1)}, u32[]{:S(2)}, u32[]{:S(2)}) collective-permute-start(f32[24,1024]{1,0:T(8,128)S(1)} %get-tuple-element.53), channel_id=1, source_target_pairs={{0,1},{1,0},{2,3},{3,2},{4,5},{5,4},{6,7},{7,6},{8,16},{9,17},{10,... | collective-permute-start | bytes 294920 | tf_op jit(solution)/shard_map/ppermute | solution.py:482
  13.4 2.5 %shard_map.133 = (f32[1024,160]{1,0:T(8,128)}, f32[4,24,1024]{2,1,0:T(8,128)S(1)}) custom-call(bf16[4,4,128,256]{3,2,1,0:T(8,128)(2,1)S(1)} %get-tuple-element.41.cat, bf16[216,384]{1,0:T(8,128)(2,1)S(1)} %get-tuple-element.42.packed, f32[4,4,40,256]{3,2,1,0:T(8,128)S(1)} %get-tuple-element.43.solution_in, f32[24,1024]{1,0:T(8,128)S(1)} %get-tuple-element.47.after, ...), custom_call_target="tpu_custom_call" | custom-call | flops 1073741824 | bytes 3311616 | tf_op jit(solution)/shard_map/pallas_call | solution.py:455
  16.6 1.8 %shard_map.135 = (f32[144,512]{1,0:T(8,128)S(1)}, f32[48,512]{1,0:T(8,128)S(1)}, f32[48,128]{1,0:T(8,128)S(1)}, f32[48,128]{1,0:T(8,128)S(1)}) custom-call(f32[4,24,1024]{2,1,0:T(8,128)S(1)} %get-tuple-element.50.rest1, f32[24,512]{1,0:T(8,128)S(1)} %get-tuple-element.51.above, f32[24,512]{1,0:T(8,128)S(1)} %get-tuple-element.52.below, ...), custom_call_target="tpu_custom_call" | custom-call | flops 536870912 | bytes 2118656 | tf_op jit(solution)/shard_map/pallas_call | solution.py:455
  18.4 2.5 %collective-permute-start.4 = (f32[48,128]{1,0:T(8,128)S(1)}, f32[48,128]{1,0:T(8,128)S(1)}, u32[]{:S(2)}, u32[]{:S(2)}) collective-permute-start(f32[48,128]{1,0:T(8,128)S(1)} %get-tuple-element.62), channel_id=1, source_target_pairs={{0,1},{1,0},{2,3},{3,2},{4,5},{5,4},{6,7},{7,6},{8,9},{9,8},{10,11... | collective-permute-start | bytes 73736 | tf_op jit(solution)/shard_map/ppermute | solution.py:469
  21.1 1.6 %shard_map.136 = (f32[48,512]{1,0:T(8,128)S(1)}, f32[48,512]{1,0:T(8,128)S(1)}) custom-call(f32[144,512]{1,0:T(8,128)S(1)} %get-tuple-element.59.solution_in, f32[48,512]{1,0:T(8,128)S(1)} %get-tuple-element.60.skeleton, bf16[1296,144]{1,0:T(8,128)(2,1)S(1)} %get-tuple-element.57.update_h, bf16[1296,144]{1,0:T(8,128)(2,1)S(1)} %get-tuple-element.58.update_l), custom_call_target="tpu_custom_call" | custom-call | flops 1073741824 | bytes 1336320 | tf_op jit(solution)/shard_map/pallas_call | solution.py:455
  22.8 1.4 %collective-permute-done.5.got_b = f32[48,128]{1,0:T(8,128)S(1)} collective-permute-done((f32[48,128]{1,0:T(8,128)S(1)}, f32[48,128]{1,0:T(8,128)S(1)}, u32[]{:S(2)}, u32[]{:S(2)}) %collective-permute-start.5) | collective-permute-done | bytes 24608 | tf_op jit(solution)/shard_map/ppermute | solution.py:469
  24.3 1.9 %collective-permute-start.7 = (f32[48,256]{1,0:T(8,128)S(1)}, f32[48,256]{1,0:T(8,128)S(1)}, u32[]{:S(2)}, u32[]{:S(2)}) collective-permute-start(f32[48,256]{1,0:T(8,128)S(1)} %get-tuple-element.66), channel_id=1, source_target_pairs={{0,1},{1,0},{2,3},{3,2},{4,5},{5,4},{6,7},{7,6},{8,16},{9,17},{10,... | collective-permute-start | bytes 147464 | tf_op jit(solution)/shard_map/ppermute | solution.py:482
  26.3 0.8 %shard_map.139 = (bf16[384,288]{1,0:T(8,128)(2,1)S(1)}, bf16[384,288]{1,0:T(8,128)(2,1)S(1)}, bf16[2592,288]{1,0:T(8,128)(2,1)S(1)}, bf16[2592,288]{1,0:T(8,128)(2,1)S(1)}, bf16[128,256]{1,0:T(8,128)(2,1)S(1)}) custom-call(f32[24,1024]{1,0:T(8,128)S(1)} %get-tuple-element.47.after, f32[96,288]{1,0:T(8,128)S(1)} %copy-done.4, f32[288,288]{1,0:T(8,128)S(1)} %copy-done.2, ...), custom_call_target="tpu_custom_call" | custom-call | bytes 6922240 | tf_op jit(solution)/shard_map/pallas_call | solution.py:455
  27.1 2.4 %collective-permute-done.7.plane_b = f32[48,256]{1,0:T(8,128)S(1)} collective-permute-done((f32[48,256]{1,0:T(8,128)S(1)}, f32[48,256]{1,0:T(8,128)S(1)}, u32[]{:S(2)}, u32[]{:S(2)}) %collective-permute-start.7) | collective-permute-done | bytes 49184 | tf_op jit(solution)/shard_map/ppermute | solution.py:482
  29.5 1.9 %shard_map.140 = (f32[288,128]{1,0:T(8,128)S(1)}, f32[96,128]{1,0:T(8,128)S(1)}, f32[96,128]{1,0:T(8,128)S(1)}, f32[96,128]{1,0:T(8,128)S(1)}) custom-call(f32[48,512]{1,0:T(8,128)S(1)} %get-tuple-element.65.rest2, f32[48,128]{1,0:T(8,128)S(1)} %collective-permute-done.4.got_a, f32[48,128]{1,0:T(8,128)S(1)} %collective-permute-done.5.got_b, ...), custom_call_target="tpu_custom_call" | custom-call | flops 536870912 | bytes 4034560 | tf_op jit(solution)/shard_map/pallas_call | solution.py:455
  31.3 1.9 %collective-permute-start.9 = (f32[96,128]{1,0:T(8,128)S(1)}, f32[96,128]{1,0:T(8,128)S(1)}, u32[]{:S(2)}, u32[]{:S(2)}) collective-permute-start(f32[96,128]{1,0:T(8,128)S(1)} %get-tuple-element.77), channel_id=1, source_target_pairs={{0,1},{1,0},{2,3},{3,2},{4,5},{5,4},{6,7},{7,6},{8,16},{9,17},{10,... | collective-permute-start | bytes 147464 | tf_op jit(solution)/shard_map/ppermute | solution.py:482
  33.3 1.3 %shard_map.141 = (f32[4,4,1152]{2,1,0:T(4,128)}, f32[96,128]{1,0:T(8,128)S(1)}) custom-call(f32[96,128]{1,0:T(8,128)S(1)} %get-tuple-element.72.after, f32[288,128]{1,0:T(8,128)S(1)} %get-tuple-element.73.solution_in, f32[96,128]{1,0:T(8,128)S(1)} %get-tuple-element.74.skeleton, bf16[2592,288]{1,0:T(8,128)(2,1)S(1)} %get-tuple-element.70.update_h, ...), custom_call_target="tpu_custom_call" | custom-call | flops 536870912 | bytes 3305472 | tf_op jit(solution)/shard_map/pallas_call | solution.py:455
  34.6 1.9 %collective-permute-done.9.plane_b = f32[96,128]{1,0:T(8,128)S(1)} collective-permute-done((f32[96,128]{1,0:T(8,128)S(1)}, f32[96,128]{1,0:T(8,128)S(1)}, u32[]{:S(2)}, u32[]{:S(2)}) %collective-permute-start.9) | collective-permute-done | bytes 49184 | tf_op jit(solution)/shard_map/ppermute | solution.py:482
  36.7 3.4 %collective-permute-start.12 = (f32[24,384]{1,0:T(8,128)S(1)}, f32[24,384]{1,0:T(8,128)S(1)}, u32[]{:S(2)}, u32[]{:S(2)}) collective-permute-start(f32[24,384]{1,0:T(8,128)S(1)} %shard_map.142.refs_0_), channel_id=1, source_target_pairs={{0,6},{1,7},{2,4},{3,5},{4,2},{5,3},{6,0},{7,1},{8,14},{9,15},{10,... | collective-permute-start | bytes 110600 | tf_op jit(solution)/shard_map/ppermute | solution.py:599
  41.5 3.0 %collective-permute-done.11.refs_2_ = f32[24,384]{1,0:T(8,128)S(1)} collective-permute-done((f32[24,384]{1,0:T(8,128)S(1)}, f32[24,384]{1,0:T(8,128)S(1)}, u32[]{:S(2)}, u32[]{:S(2)}) %collective-permute-start.11) | collective-permute-done | bytes 36896 | tf_op jit(solution)/shard_map/ppermute | solution.py:599
  44.5 3.1 %collective-permute-start.13 = (f32[96,384]{1,0:T(8,128)S(1)}, f32[96,384]{1,0:T(8,128)S(1)}, u32[]{:S(2)}, u32[]{:S(2)}) collective-permute-start(f32[96,384]{1,0:T(8,128)S(1)} %shard_map.143.own), channel_id=1, source_target_pairs={{0,1},{1,0},{2,3},{3,2},{4,5},{5,4},{6,7},{7,6},{8,9},{9,8},{10,11... | collective-permute-start | bytes 442376 | tf_op jit(solution)/shard_map/ppermute | solution.py:603
  47.5 0.9 %shard_map.138 = f32[128,576]{1,0:T(8,128)} custom-call(f32[48,256]{1,0:T(8,128)S(1)} %get-tuple-element.64.after, f32[144,512]{1,0:T(8,128)S(1)} %get-tuple-element.59.solution_in), custom_call_target="tpu_custom_call" | custom-call | bytes 589824 | tf_op jit(solution)/shard_map/pallas_call | solution.py:455
  48.5 0.8 %shard_map.144 = f32[32,4,384]{2,1,0:T(4,128)} custom-call(f32[96,384]{1,0:T(8,128)S(1)} %shard_map.143.own, f32[96,384]{1,0:T(8,128)S(1)} %collective-permute-done.13.other), custom_call_target="tpu_custom_call" | custom-call | bytes 491520 | tf_op jit(solution)/shard_map/pallas_call | solution.py:455
  (40 shorter events, 3.8 us)
Async XLA Ops:
  0.6 3.0 %copy-start.6 = (f32[4,16,16,256]{3,2,1,0:T(8,128)S(1)}, f32[4,16,16,256]{3,2,1,0:T(8,128)}, u32[]{:S(2)}) copy-start(f32[4,16,16,256]{3,2,1,0:T(8,128)} %rhs.1) | copy-start | bytes 3145732
  0.6 3.0 %copy-start.7 = (f32[27,24,40]{2,1,0:T(8,128)S(1)}, f32[27,24,40]{2,1,0:T(8,128)}, u32[]{:S(2)}) copy-start(f32[27,24,40]{2,1,0:T(8,128)} %param.13) | copy-start | bytes 311044
  0.7 3.0 %copy-start.8 = (f32[40,40]{1,0:T(8,128)S(1)}, f32[40,40]{1,0:T(8,128)}, u32[]{:S(2)}) copy-start(f32[40,40]{1,0:T(8,128)} %elim.3) | copy-start | bytes 19204
  0.7 3.0 %copy-start.9 = (f32[24,40]{1,0:T(8,128)S(1)}, f32[24,40]{1,0:T(8,128)}, u32[]{:S(2)}) copy-start(f32[24,40]{1,0:T(8,128)} %skel.3) | copy-start | bytes 11524
  1.7 3.4 %collective-permute-start = (f32[4,16,256]{2,1,0:T(8,128)S(1)}, f32[4,16,256]{2,1,0:T(8,128)S(1)}, u32[]{:S(2)}, u32[]{:S(2)}) collective-permute-start(f32[4,16,256]{2,1,0:T(8,128)S(1)} %get-tuple-element.45), channel_id=1, source_target_pairs={{0,1},{1,0},{2,3},{3,2},{4,5},{5,4},{6,7},{7,6},{8,9},{9,8},{10,11... | collective-permute-start | bytes 196616 | tf_op jit(solution)/shard_map/ppermute | solution.py:469
  2.4 4.0 %collective-permute-start.1 = (f32[4,16,256]{2,1,0:T(8,128)S(1)}, f32[4,16,256]{2,1,0:T(8,128)S(1)}, u32[]{:S(2)}, u32[]{:S(2)}) collective-permute-start(f32[4,16,256]{2,1,0:T(8,128)S(1)} %get-tuple-element.46), channel_id=1, source_target_pairs={{0,7},{1,2},{2,1},{3,4},{4,3},{5,6},{6,5},{7,0},{8,15},{9,10},{10,... | collective-permute-start | bytes 196616 | tf_op jit(solution)/shard_map/ppermute | solution.py:469
  4.4 8.8 %copy-start.1 = (f32[27,48,144]{2,1,0:T(8,128)S(1)}, f32[27,48,144]{2,1,0:T(8,128)}, u32[]{:S(2)}) copy-start(f32[27,48,144]{2,1,0:T(8,128)} %param.16) | copy-start | bytes 2239492
  4.4 8.7 %copy-start.3 = (f32[144,144]{1,0:T(8,128)S(1)}, f32[144,144]{1,0:T(8,128)}, u32[]{:S(2)}) copy-start(f32[144,144]{1,0:T(8,128)} %elim.4) | copy-start | bytes 248836
  4.4 8.7 %copy-start.5 = (f32[48,144]{1,0:T(8,128)S(1)}, f32[48,144]{1,0:T(8,128)}, u32[]{:S(2)}) copy-start(f32[48,144]{1,0:T(8,128)} %skel.4) | copy-start | bytes 82948
  7.3 8.7 %collective-permute-start.3 = (f32[24,1024]{1,0:T(8,128)S(1)}, f32[24,1024]{1,0:T(8,128)S(1)}, u32[]{:S(2)}, u32[]{:S(2)}) collective-permute-start(f32[24,1024]{1,0:T(8,128)S(1)} %get-tuple-element.53), channel_id=1, source_target_pairs={{0,1},{1,0},{2,3},{3,2},{4,5},{5,4},{6,7},{7,6},{8,16},{9,17},{10,... | collective-permute-start | bytes 294920 | tf_op jit(solution)/shard_map/ppermute | solution.py:482
  13.1 3.5 %collective-permute-start.2 = (f32[24,1024]{1,0:T(8,128)S(1)}, f32[24,1024]{1,0:T(8,128)S(1)}, u32[]{:S(2)}, u32[]{:S(2)}) collective-permute-start(f32[24,1024]{1,0:T(8,128)S(1)} %get-tuple-element.47.after), channel_id=1, source_target_pairs={{0,8},{1,9},{2,10},{3,11},{4,12},{5,13},{6,14},{7,15},{8,0},{9,1},... | collective-permute-start | bytes 294920 | tf_op jit(solution)/shard_map/ppermute | solution.py:482
  16.6 9.7 %copy-start.2 = (f32[288,288]{1,0:T(8,128)S(1)}, f32[288,288]{1,0:T(8,128)}, u32[]{:S(2)}) copy-start(f32[288,288]{1,0:T(8,128)} %elim.5) | copy-start | bytes 995332
  18.4 4.4 %collective-permute-start.4 = (f32[48,128]{1,0:T(8,128)S(1)}, f32[48,128]{1,0:T(8,128)S(1)}, u32[]{:S(2)}, u32[]{:S(2)}) collective-permute-start(f32[48,128]{1,0:T(8,128)S(1)} %get-tuple-element.62), channel_id=1, source_target_pairs={{0,1},{1,0},{2,3},{3,2},{4,5},{5,4},{6,7},{7,6},{8,9},{9,8},{10,11... | collective-permute-start | bytes 73736 | tf_op jit(solution)/shard_map/ppermute | solution.py:469
  20.9 3.3 %collective-permute-start.5 = (f32[48,128]{1,0:T(8,128)S(1)}, f32[48,128]{1,0:T(8,128)S(1)}, u32[]{:S(2)}, u32[]{:S(2)}) collective-permute-start(f32[48,128]{1,0:T(8,128)S(1)} %get-tuple-element.63), channel_id=1, source_target_pairs={{0,7},{1,2},{2,1},{3,4},{4,3},{5,6},{6,5},{7,0},{8,15},{9,10},{10,... | collective-permute-start | bytes 73736 | tf_op jit(solution)/shard_map/ppermute | solution.py:469
  21.1 5.2 %copy-start = (f32[27,96,288]{2,1,0:T(8,128)S(1)}, f32[27,96,288]{2,1,0:T(8,128)}, u32[]{:S(2)}) copy-start(f32[27,96,288]{2,1,0:T(8,128)} %param.19) | copy-start | bytes 8957956
  21.1 5.2 %copy-start.4 = (f32[96,288]{1,0:T(8,128)S(1)}, f32[96,288]{1,0:T(8,128)}, u32[]{:S(2)}) copy-start(f32[96,288]{1,0:T(8,128)} %skel.5) | copy-start | bytes 331780
  24.3 5.1 %collective-permute-start.7 = (f32[48,256]{1,0:T(8,128)S(1)}, f32[48,256]{1,0:T(8,128)S(1)}, u32[]{:S(2)}, u32[]{:S(2)}) collective-permute-start(f32[48,256]{1,0:T(8,128)S(1)} %get-tuple-element.66), channel_id=1, source_target_pairs={{0,1},{1,0},{2,3},{3,2},{4,5},{5,4},{6,7},{7,6},{8,16},{9,17},{10,... | collective-permute-start | bytes 147464 | tf_op jit(solution)/shard_map/ppermute | solution.py:482
  26.3 3.2 %collective-permute-start.6 = (f32[48,256]{1,0:T(8,128)S(1)}, f32[48,256]{1,0:T(8,128)S(1)}, u32[]{:S(2)}, u32[]{:S(2)}) collective-permute-start(f32[48,256]{1,0:T(8,128)S(1)} %get-tuple-element.64.after), channel_id=1, source_target_pairs={{0,8},{1,9},{2,10},{3,11},{4,12},{5,13},{6,14},{7,15},{8,0},{9,1},... | collective-permute-start | bytes 147464 | tf_op jit(solution)/shard_map/ppermute | solution.py:482
  31.3 5.1 %collective-permute-start.9 = (f32[96,128]{1,0:T(8,128)S(1)}, f32[96,128]{1,0:T(8,128)S(1)}, u32[]{:S(2)}, u32[]{:S(2)}) collective-permute-start(f32[96,128]{1,0:T(8,128)S(1)} %get-tuple-element.77), channel_id=1, source_target_pairs={{0,1},{1,0},{2,3},{3,2},{4,5},{5,4},{6,7},{7,6},{8,16},{9,17},{10,... | collective-permute-start | bytes 147464 | tf_op jit(solution)/shard_map/ppermute | solution.py:482
  33.3 3.2 %collective-permute-start.8 = (f32[96,128]{1,0:T(8,128)S(1)}, f32[96,128]{1,0:T(8,128)S(1)}, u32[]{:S(2)}, u32[]{:S(2)}) collective-permute-start(f32[96,128]{1,0:T(8,128)S(1)} %get-tuple-element.72.after), channel_id=1, source_target_pairs={{0,8},{1,9},{2,10},{3,11},{4,12},{5,13},{6,14},{7,15},{8,0},{9,1},... | collective-permute-start | bytes 147464 | tf_op jit(solution)/shard_map/ppermute | solution.py:482
  36.7 4.8 %collective-permute-start.12 = (f32[24,384]{1,0:T(8,128)S(1)}, f32[24,384]{1,0:T(8,128)S(1)}, u32[]{:S(2)}, u32[]{:S(2)}) collective-permute-start(f32[24,384]{1,0:T(8,128)S(1)} %shard_map.142.refs_0_), channel_id=1, source_target_pairs={{0,6},{1,7},{2,4},{3,5},{4,2},{5,3},{6,0},{7,1},{8,14},{9,15},{10,... | collective-permute-start | bytes 110600 | tf_op jit(solution)/shard_map/ppermute | solution.py:599
  40.1 4.3 %collective-permute-start.11 = (f32[24,384]{1,0:T(8,128)S(1)}, f32[24,384]{1,0:T(8,128)S(1)}, u32[]{:S(2)}, u32[]{:S(2)}) collective-permute-start(f32[24,384]{1,0:T(8,128)S(1)} %shard_map.142.refs_0_), channel_id=1, source_target_pairs={{0,4},{1,5},{2,6},{3,7},{4,0},{5,1},{6,2},{7,3},{8,12},{9,13},{10,... | collective-permute-start | bytes 110600 | tf_op jit(solution)/shard_map/ppermute | solution.py:599
  40.1 4.3 %collective-permute-start.10 = (f32[24,384]{1,0:T(8,128)S(1)}, f32[24,384]{1,0:T(8,128)S(1)}, u32[]{:S(2)}, u32[]{:S(2)}) collective-permute-start(f32[24,384]{1,0:T(8,128)S(1)} %shard_map.142.refs_0_), channel_id=1, source_target_pairs={{0,2},{1,3},{2,0},{3,1},{4,6},{5,7},{6,4},{7,5},{8,10},{9,11},{10,... | collective-permute-start | bytes 110600 | tf_op jit(solution)/shard_map/ppermute | solution.py:599
  44.5 4.1 %collective-permute-start.13 = (f32[96,384]{1,0:T(8,128)S(1)}, f32[96,384]{1,0:T(8,128)S(1)}, u32[]{:S(2)}, u32[]{:S(2)}) collective-permute-start(f32[96,384]{1,0:T(8,128)S(1)} %shard_map.143.own), channel_id=1, source_target_pairs={{0,1},{1,0},{2,3},{3,2},{4,5},{5,4},{6,7},{7,6},{8,9},{9,8},{10,11... | collective-permute-start | bytes 442376 | tf_op jit(solution)/shard_map/ppermute | solution.py:603

commit v4 on v3

--- a/solution.py
+++ b/solution.py
@@ -64,10 +64,10 @@
 
 
 def fine_ends_kernel(rhs, send_a, send_b, sems):
-    upward = jnp.where(lax.axis_index("narrow") % 2 == 0, 15, 0)
+    upward = jnp.where(lax.axis_index("narrow") % 2 == 0, 13, 0)
     copies = [
-        pltpu.make_async_copy(rhs.at[:, upward], send_a, sems.at[0]),
-        pltpu.make_async_copy(rhs.at[:, 15 - upward], send_b, sems.at[1]),
+        pltpu.make_async_copy(rhs.at[:, pl.ds(upward, 3)], send_a, sems.at[0]),
+        pltpu.make_async_copy(rhs.at[:, pl.ds(13 - upward, 3)], send_b, sems.at[1]),
     ]
     for copy in copies:
         copy.start()
@@ -131,7 +131,80 @@
             edge[side, :, k * 256 : (k + 1) * 256] = fine_plane(operator, cat, k, c)
 
 
-def fine_inside_kernel(cat, packed, solution_in, after, skeleton, solved, rest, out_rows):
+def strip_columns():
+    return lanes((24, 512)) // 16 % 8
+
+
+def strip_outer(j):
+    return (j == 1) | (j == 2) | (j == 5) | (j == 6)
+
+
+def strip_plane(operator, strips, c):
+    first = max(0, c - 2)
+    last = min(3, c)
+    columns = operator[:, (first - c + 2) * 128 : (last - c + 3) * 128]
+    right = strips[first : last + 1].reshape((last + 1 - first) * 128, 512)
+    product = dot(columns, right)
+    z = lanes((24, 512)) % 16
+    sums = [along_z(product[dy * 72 : (dy + 1) * 72], 24, z, 15) for dy in range(3)]
+    j = strip_columns()
+    inner = (j > 0) & (j < 7)
+    return (
+        jnp.where(strip_outer(j), sums[1], 0.0)
+        + jnp.where(inner & (j != 4), roll(sums[0], 16), 0.0)
+        + jnp.where(inner & (j != 3), roll(sums[2], -16), 0.0)
+    )
+
+
+def strip_ends(strip, k):
+    half = lanes((24, 128))
+    here = strip[:, k * 128 : (k + 1) * 128]
+    return (
+        jnp.where(half < 16, roll(here, -48), 0.0),
+        jnp.where(half >= 112, roll(here, 48), 0.0),
+    )
+
+
+def fine_edge_kernel(
+    narrow, after, edge, packed, solver, solution_in, got_a, got_b, strips, skeleton, send_a, send_b, turned
+):
+    above, below = from_partners("narrow", narrow, got_a[...], got_b[...])
+    j = lanes((40, 512)) // 16 % 8
+    for x in range(4):
+        here = slice(x * 48, (x + 1) * 48)
+        rows = [below[here], jnp.zeros((32, 256), F32), above[here]]
+        turned[...] = jnp.concatenate(rows, axis=0).T
+        vectors = [turned[pl.ds(k, 64, stride=4), :] for k in range(4)]
+        vector = jnp.concatenate(vectors, axis=1)
+        product = dot(solver[...], stacked(vector[24:64]))
+        skeleton[x] = vector[:24] - product[40:64]
+        own = [solution_in[k, x] for k in range(4)]
+        starts = jnp.concatenate([roll(v[:, :128], 48) for v in own], axis=1)
+        ends = jnp.concatenate([roll(v[:, 128:], -48) for v in own], axis=1)
+        strips[x] = stacked(jnp.where(j == 3, starts, jnp.where(j == 4, ends, product[:40])))
+    operator = packed[...]
+    even = lax.axis_index("slab") % 2 == 0
+    outer = strip_outer(lanes((24, 128)) // 16)
+    sides = [strip_plane(operator, strips, c) for c in (0, 5)]
+    for k in range(4):
+        for part in range(2):
+            here = slice(k * 256 + part * 128, k * 256 + (part + 1) * 128)
+            low, high = [edge[i, :, here] + strip_ends(sides[i], k)[part] for i in range(2)]
+            send_a[:, here], send_b[:, here] = to_partners(even, high, low)
+    for p in range(2):
+        low, high = [
+            jnp.where(
+                outer,
+                v[:, p * 256 : p * 256 + 128],
+                roll(v[:, p * 256 + 128 : (p + 1) * 256], 32),
+            )
+            for v in sides
+        ]
+        here = slice(1024 + p * 128, 1152 + p * 128)
+        send_a[:, here], send_b[:, here] = to_partners(even, high, low)
+
+
+def fine_inside_kernel(cat, packed, solution_in, skeleton, solved, rest, out_rows):
     operator = packed[...]
     for k in range(4):
         for x in range(4):
@@ -146,62 +219,31 @@
             solved[x * 256 + part * 128 : x * 256 + (part + 1) * 128, :] = out_rows[part].T
 
 
-def fine_border(above, below, k, c):
-    half = lanes((24, 128))
-    here = slice(k * 128, (k + 1) * 128)
-    start = jnp.where(half < 16, roll(below[:, here], -16 * c), 0.0)
-    end = jnp.where(half >= 112, roll(above[:, here], 112 - 16 * c), 0.0)
-    return start, end
-
-
-def fine_edge_kernel(
-    narrow, edge, packed, solver, got_a, got_b, sum_above, sum_below, send_a, send_b, turned
+def fine_strip_kernel(packed, after, inner, strips, strip_skeleton, rest, strip_rest):
+    operator = packed[...]
+    for x in range(4):
+        strip = strip_plane(operator, strips, x + 1)
+        strip_rest[x] = strip_skeleton[x] - strip
+        for k in range(4):
+            here = slice(k * 256, (k + 1) * 256)
+            rest[x, :, here] = inner[x, :, here] - jnp.concatenate(strip_ends(strip, k), axis=1)
+
+
+def operators_mid_kernel(
+    after, skel, elim, update, solve_h, solve_l, update_h, update_l, sort, sort_strip
 ):
-    above, below = from_partners("narrow", narrow, got_a[...], got_b[...])
-    turned[...] = jnp.concatenate([below, above], axis=0).T
-    vectors = [turned[pl.ds(k, 64, stride=4), :][24:64] for k in range(4)]
-    solution_vector = dot(solver[...], stacked(jnp.concatenate(vectors, axis=1)))[:40]
-    operator = packed[...]
-    half = lanes((40, 128))
-    z = lanes((24, 512)) % 16
-    sums = []
-    for side, base in ((0, 0), (1, 144)):
-        blocks = []
-        for k in range(4):
-            block = roll(solution_vector[:, k * 128 : (k + 1) * 128], 64 * side)
-            blocks.append(jnp.where(half < 64, block, 0.0))
-        right = []
-        for d in range(3):
-            moved = [roll(block, 16 * (2 - d)) for block in blocks]
-            right.append(stacked(jnp.concatenate(moved, axis=1)))
-        product = dot(operator[base : base + 72], jnp.concatenate(right, axis=0))
-        sums.append(along_z(product, 24, z, 15))
-    below, above = sums
-    sum_below[...] = below
-    sum_above[...] = above
-    even = lax.axis_index("slab") % 2 == 0
-    for k in range(4):
-        planes = []
-        for side, c in ((0, 0), (1, 5)):
-            start, end = fine_border(above, below, k, c)
-            planes.append(
-                (
-                    edge[side, :, k * 256 : k * 256 + 128] + start,
-                    edge[side, :, k * 256 + 128 : (k + 1) * 256] + end,
-                )
-            )
-        for part in range(2):
-            here = slice(k * 256 + part * 128, k * 256 + (part + 1) * 128)
-            send_a[:, here], send_b[:, here] = to_partners(even, planes[1][part], planes[0][part])
-
-
-def operators_mid_kernel(after, skel, elim, update, solve_h, solve_l, update_h, update_l, sort):
     solve_h[...], solve_l[...] = halves(jnp.concatenate([elim[...], skel[...]], axis=0))
     update_h[...], update_l[...] = halves(update[...])
     row = lax.broadcasted_iota(jnp.int32, (256, 256), 0)
     y, z = row // 16, row % 16
     goal = ((y % 2) * 2 + z % 2) * 64 + (y // 2) * 8 + z // 2
     sort[...] = jnp.where(goal == lanes((256, 256)), 1.0, 0.0).astype(BF16)
+    row = lax.broadcasted_iota(jnp.int32, (128, 512), 0)
+    j, z = row // 16, row % 16
+    goal = (((j + 1) % 2) * 2 + z % 2) * 128 + j // 4 * 64 + z // 2
+    goal = jnp.where(strip_outer(j) & (j < 4), ((j - 1) * 2 + z % 2) * 128 + z // 2, goal)
+    wanted = strip_outer(j) & (goal == lanes((128, 512)))
+    sort_strip[...] = jnp.where(wanted, 1.0, 0.0).astype(BF16)
 
 
 def operators_coarse_kernel(after, skel, elim, update, solve_h, solve_l, update_h, update_l, sort):
@@ -214,23 +256,47 @@
 
 
 def mid_solve_kernel(
-    slabs, rest1, above, below, plane_a, plane_b, sort, solve_h, solve_l, update_h, update_l,
-    solution_out, skeleton, send_a, send_b,
-    parts, vector,
+    slabs, narrow, rest1, strip_rest, plane_a, plane_b, sort, sort_strip,
+    solve_h, solve_l, update_h, update_l,
+    solution_out, skeleton, sum_above, sum_below,
+    parts, strip_parts, vector,
 ):
     plane_above, plane_below = from_partners("slab", slabs, plane_a[...], plane_b[...])
+    index = lax.axis_index("narrow")
+    column = lanes((24, 128)) // 16
+    first, end = jnp.where(index > 0, 0, 4), jnp.where(index < narrow - 1, 8, 4)
+    there = strip_outer(column) & (column >= first) & (column < end)
     for k in range(4):
         for x in range(4):
-            start, end = fine_border(above, below, k, x + 1)
             here = slice(k * 256, (k + 1) * 256)
-            value = rest1[x, :, here] - jnp.concatenate([start, end], axis=1)
-            if x == 0:
-                value = value - plane_below[:, here]
-            if x == 3:
-                value = value - plane_above[:, here]
+            value = rest1[x, :, here]
+            strip = strip_rest[x, :, k * 128 : (k + 1) * 128]
+            if x in (0, 3):
+                plane = plane_below if x == 0 else plane_above
+                value = value - plane[:, here]
+                outside = plane[:, 1024 + k // 2 * 128 : 1152 + k // 2 * 128]
+                strip = strip - (roll(outside, -32) if k % 2 == 1 else outside)
+            strip = jnp.where(there, strip, 0.0)
             top = value.astype(BF16).astype(F32)
             parts[k * 4 + x] = jnp.concatenate([top, value - top], axis=0).astype(BF16)
+            top = strip.astype(BF16).astype(F32)
+            strip_parts[k * 4 + x] = jnp.concatenate([top, strip - top], axis=0).astype(BF16)
     arranged = dot(parts[...].reshape(16 * 48, 256), sort[...])
+    strip_arranged = dot(strip_parts[...].reshape(16 * 48, 128), sort_strip[...])
+    for child in range(2, 8):
+        dx, group = divmod(child, 4)
+        total = None
+        for k in range(4):
+            for i in range(2):
+                base = (k * 4 + i * 2 + dx) * 48
+                columns = slice(group * 128, (group + 1) * 128)
+                piece = (
+                    strip_arranged[base : base + 24, columns]
+                    + strip_arranged[base + 24 : base + 48, columns]
+                )
+                moved = roll(piece, (k * 2 + i) * 8)
+                total = moved if total is None else total + moved
+        vector[child * 24 : child * 24 + 24, 512:] = total
     half = lanes((24, 128))
     for k in range(4):
         for dx in range(2):
@@ -249,28 +315,15 @@
                     half < 64, roll(first, 64), second
                 )
     result = dot3(solve_h[...], solve_l[...], vector[48:, :])
-    solution_vector = result[:144]
-    solution_out[...] = solution_vector
-    skeleton[...] = vector[:48, :] - result[144:]
-
-    j = lanes((144, 128)) // 8 % 8
-    ends = []
-    for end, wanted in enumerate((0, 7)):
-        total = None
-        for k in range(4):
-            block = solution_vector[:, k * 128 : (k + 1) * 128]
-            for x in range(2):
-                u = k * 2 + x
-                moved = roll(block, 8 * (u - wanted) - 64 * x + 64 * end)
-                total = moved if total is None else jnp.where(j == u, moved, total)
-        ends.append(total)
+    solution_out[...] = result[:144, :512]
+    skeleton[...] = vector[:48, :512] - result[144:, :512]
+    right = result[:144, 512:]
     spot = lanes((48, 128))
     l = spot % 8
-    right = jnp.where(lanes((144, 128)) < 64, ends[0], ends[1])
     sums = [[], []]
     for dx in range(3):
         rows = []
-        for dy in (2, 0):
+        for dy in (0, 2):
             base = (dx * 9 + dy * 3) * 48
             rows.append(slice(base, base + 144))
         both = [dot3(update_h[r, :], update_l[r, :], right) for r in rows]
@@ -286,30 +339,53 @@
             messages.append(jnp.where(spot < 64, inside, roll(outside, 64)))
         else:
             messages.append(jnp.where(spot < 64, roll(inside, 64), outside))
-    send_a[...], send_b[...] = to_partners(lax.axis_index("narrow") % 2 == 0, messages[1], messages[0])
-
-
-def mid_update_kernel(solution_in, skeleton, update_h, update_l, rest, edge, product):
-    product[...] = dot3(update_h[...], update_l[...], solution_in[...])
+    sum_below[...], sum_above[...] = messages
+
+
+def mid_plane(update_h, update_l, solution_vector, dx, product):
+    rows = slice(dx * 432, (dx + 1) * 432)
+    product[...] = dot3(update_h[rows, :], update_l[rows, :], solution_vector)
     lane = lanes((48, 128))
-    i, j, l = lane // 64, lane // 8 % 8, lane % 8
+    j, l = lane // 8 % 8, lane % 8
+    totals = []
     for k in range(4):
         here = slice(k * 128, (k + 1) * 128)
-        totals = []
-        for dx in range(3):
-            sums = []
-            for dy in range(3):
-                base = (dx * 9 + dy * 3) * 48
-                sums.append(along_z(product[base : base + 144, here], 48, l, 7))
-            totals.append(
-                sums[1]
-                + jnp.where(j > 0, roll(sums[0], 8), 0.0)
-                + jnp.where(j < 7, roll(sums[2], -8), 0.0)
-            )
-        minus, zero, plus = totals
-        inside = zero + jnp.where(i == 0, roll(plus, 64), roll(minus, 64))
-        rest[:, here] = skeleton[:, here] - inside
-        edge[:, here] = jnp.where(i == 0, plus, minus)
+        sums = [along_z(product[dy * 144 : (dy + 1) * 144, here], 48, l, 7) for dy in range(3)]
+        totals.append(
+            sums[1]
+            + jnp.where(j > 0, roll(sums[0], 8), 0.0)
+            + jnp.where(j < 7, roll(sums[2], -8), 0.0)
+        )
+    return totals
+
+
+def mid_outside_kernel(
+    solution_in, skeleton, above, below, update_h, update_l, partial, send_a, send_b, product
+):
+    minus = mid_plane(update_h, update_l, solution_in[...], 0, product.at[0])
+    plus = mid_plane(update_h, update_l, solution_in[...], 2, product.at[1])
+    half = lanes((48, 128))
+    edges = []
+    for k in range(4):
+        here = slice(k * 128, (k + 1) * 128)
+        partial[:, here] = skeleton[:, here] - jnp.where(
+            half < 64, roll(plus[k], 64), roll(minus[k], 64)
+        )
+        edges.append(jnp.where(half < 64, plus[k], minus[k]) + mid_border(above, below, k, 1))
+    even = lax.axis_index("slab") % 2 == 0
+    for p in range(2):
+        moved = roll(edges[2 * p], 64)
+        low = jnp.where(half >= 64, moved, edges[2 * p + 1])
+        high = jnp.where(half < 64, moved, edges[2 * p + 1])
+        here = slice(p * 128, (p + 1) * 128)
+        send_a[:, here], send_b[:, here] = to_partners(even, high, low)
+
+
+def mid_inside_kernel(after, solution_in, partial, above, below, update_h, update_l, rest, product):
+    zero = mid_plane(update_h, update_l, solution_in[...], 1, product)
+    for k in range(4):
+        here = slice(k * 128, (k + 1) * 128)
+        rest[:, here] = partial[:, here] - zero[k] - mid_border(above, below, k, 0)
 
 
 def mid_border(above, below, k, a):
@@ -319,24 +395,9 @@
     for x in range(2):
         start = a * 64 + (k * 2 + x) * 8
         here = lane // 64 == x
-        total = jnp.where(here & (j == 0), roll(below, x * 64 - start), total)
-        total = jnp.where(here & (j == 7), roll(above, x * 64 + 56 - start), total)
+        total = jnp.where(here & (j == 0), roll(below[...], x * 64 - start), total)
+        total = jnp.where(here & (j == 7), roll(above[...], x * 64 + 56 - start), total)
     return total
-
-
-def mid_edge_kernel(narrow, edge, got_a, got_b, send_a, send_b):
-    above, below = from_partners("narrow", narrow, got_a[...], got_b[...])
-    even = lax.axis_index("slab") % 2 == 0
-    half = lanes((48, 128))
-    for p in range(2):
-        pair = []
-        for k in (2 * p, 2 * p + 1):
-            pair.append(edge[:, k * 128 : (k + 1) * 128] + mid_border(above, below, k, 1))
-        moved = roll(pair[0], 64)
-        low = jnp.where(half >= 64, moved, pair[1])
-        high = jnp.where(half < 64, moved, pair[1])
-        here = slice(p * 128, (p + 1) * 128)
-        send_a[:, here], send_b[:, here] = to_partners(even, high, low)
 
 
 def mid_solved_kernel(after, solution_in, solved, out_rows):
@@ -346,11 +407,10 @@
 
 
 def coarse_solve_kernel(
-    slabs, narrow, rest2, got_a, got_b, plane_a, plane_b, sort, solve_h, solve_l, update_h, update_l,
+    slabs, rest2, plane_a, plane_b, sort, solve_h, solve_l, update_h, update_l,
     solution_out, skeleton, send_a, send_b,
     parts, vector,
 ):
-    above, below = from_partners("narrow", narrow, got_a[...], got_b[...])
     plane_above, plane_below = from_partners("slab", slabs, plane_a[...], plane_b[...])
     half = lanes((48, 128))
     for k in range(4):
@@ -359,7 +419,7 @@
         up, down = plane_above[:, pack], plane_below[:, pack]
         if k % 2 == 1:
             up, down = roll(up, 64), roll(down, 64)
-        value = rest2[:, here] - mid_border(above, below, k, 0) - jnp.where(half < 64, down, up)
+        value = rest2[:, here] - jnp.where(half < 64, down, up)
         top = value.astype(BF16).astype(F32)
         parts[k] = jnp.concatenate([top, value - top], axis=0).astype(BF16)
     arranged = dot(parts[...].reshape(4 * 96, 128), sort[...])
@@ -490,7 +550,7 @@
         *call(
             fine_ends_kernel,
             [pltpu.with_memory_space_constraint(rhs, pltpu.HBM)],
-            [((4, 16, 256), F32)] * 2,
+            [((4, 3, 16, 256), F32)] * 2,
             flops=1 << 31,
             where=pltpu.HBM,
             sems=2,
@@ -514,50 +574,61 @@
         flops=1 << 29,
     )
     (edge,) = call(fine_outside_kernel, [cat, packed], [((2, 24, 1024), F32)], flops=1 << 30)
-    above, below, send_a, send_b = call(
-        functools.partial(fine_edge_kernel, narrow),
-        [edge, packed, solver, got_a.reshape(64, 256), got_b.reshape(64, 256)],
-        [((24, 512), F32)] * 2 + [((24, 1024), F32)] * 2,
-        [((256, 128), F32)],
-    )
-    after = send_a
-    plane_a, plane_b = swap_slab(send_a, send_b)
-    solved1, rest = call(
+    solved1, inner = call(
         fine_inside_kernel,
-        [cat, packed, solution1, send_a, skeleton],
+        [cat, packed, solution1, skeleton],
         [((1024, 160), F32), ((4, 24, 1024), F32)],
         [((2, 160, 128), F32)],
         flops=1 << 30,
-        unread=(3,),
-    )
-    *solve2, update2_h, update2_l, sort2 = call(
+    )
+    strips, strip_skeleton, send_a, send_b = call(
+        functools.partial(fine_edge_kernel, narrow),
+        [inner, edge, packed, solver, solution1, got_a.reshape(192, 256), got_b.reshape(192, 256)],
+        [((4, 128, 512), BF16), ((4, 24, 512), F32)] + [((24, 1280), F32)] * 2,
+        [((256, 128), F32)],
+        unread=(0,),
+    )
+    after = send_a
+    plane_a, plane_b = swap_slab(send_a, send_b)
+    rest, strip_rest = call(
+        fine_strip_kernel,
+        [packed, send_a, inner, strips, strip_skeleton],
+        [((4, 24, 1024), F32), ((4, 24, 512), F32)],
+        flops=1 << 29,
+        unread=(1,),
+    )
+    *solve2, update2_h, update2_l, sort2, sort_strip = call(
         operators_mid_kernel,
         [send_a, skel2, elim2, update2.reshape(1296, 144)],
-        [((192, 144), BF16)] * 2 + [((1296, 144), BF16)] * 2 + [((256, 256), BF16)],
+        [((192, 144), BF16)] * 2
+        + [((1296, 144), BF16)] * 2
+        + [((256, 256), BF16), ((128, 512), BF16)],
         unread=(0,),
     )
 
-    solution2, skeleton, send_a, send_b = call(
-        functools.partial(mid_solve_kernel, slabs),
-        [rest, above, below, plane_a, plane_b, sort2, *solve2, update2_h, update2_l],
+    solution2, skeleton, above, below = call(
+        functools.partial(mid_solve_kernel, slabs, narrow),
+        [rest, strip_rest, plane_a, plane_b, sort2, sort_strip, *solve2, update2_h, update2_l],
         [((144, 512), F32), ((48, 512), F32), ((48, 128), F32), ((48, 128), F32)],
-        [((16, 48, 256), BF16), ((192, 512), F32)],
+        [((16, 48, 256), BF16), ((16, 48, 128), BF16), ((192, 640), F32)],
         flops=1 << 29,
     )
-    got_a, got_b = swap_narrow(send_a, send_b)
-    rest, edge = call(
-        mid_update_kernel,
-        [solution2, skeleton, update2_h, update2_l],
-        [((48, 512), F32), ((48, 512), F32)],
-        [((1296, 512), F32)],
-        flops=1 << 30,
-    )
-    send_a, send_b = call(
-        functools.partial(mid_edge_kernel, narrow),
-        [edge, got_a, got_b],
-        [((48, 256), F32)] * 2,
+    partial, send_a, send_b = call(
+        mid_outside_kernel,
+        [solution2, skeleton, above, below, update2_h, update2_l],
+        [((48, 512), F32), ((48, 256), F32), ((48, 256), F32)],
+        [((2, 432, 512), F32)],
+        flops=1 << 29,
     )
     plane_a, plane_b = swap_slab(send_a, send_b)
+    (rest,) = call(
+        mid_inside_kernel,
+        [send_a, solution2, partial, above, below, update2_h, update2_l],
+        [((48, 512), F32)],
+        [((432, 512), F32)],
+        flops=1 << 29,
+        unread=(0,),
+    )
     (solved2,) = call(
         mid_solved_kernel,
         [send_a, solution2],
@@ -567,14 +638,14 @@
     )
     *solve3, update3_h, update3_l, sort3 = call(
         operators_coarse_kernel,
-        [after, skel3, elim3, update3.reshape(2592, 288)],
+        [send_a, skel3, elim3, update3.reshape(2592, 288)],
         [((384, 288), BF16)] * 2 + [((2592, 288), BF16)] * 2 + [((128, 256), BF16)],
         unread=(0,),
     )
 
     solution3, skeleton, send_a, send_b = call(
-        functools.partial(coarse_solve_kernel, slabs, narrow),
-        [rest, got_a, got_b, plane_a, plane_b, sort3, *solve3, update3_h, update3_l],
+        functools.partial(coarse_solve_kernel, slabs),
+        [rest, plane_a, plane_b, sort3, *solve3, update3_h, update3_l],
         [((288, 128), F32), ((96, 128), F32), ((96, 128), F32), ((96, 128), F32)],
         [((4, 96, 128), BF16), ((384, 128), F32)],
         flops=1 << 29,

time: 49.4 us -> 48.7 us (0.986)
  Pallas kernels: 15.5 us -> 16.7 us
  waiting for transfers between devices: 11.4 us -> 10.3 us
  starting transfers between devices: 21.5 us -> 20.7 us
    ppermute x4 -> x2, starting transfers between devices: 4.65 us -> 1.96 us  [swap_narrow(): lax.ppermute(value, 'narrow', pair)]
    ppermute x4 -> x2, waiting for transfers between devices: 2.71 us -> 0.24 us  [swap_narrow(): lax.ppermute(value, 'narrow', pair)]
    ppermute x6, waiting for transfers between devices: 4.96 us -> 6.35 us  [swap_slab(): results.append(lax.ppermute(value, ('slab', 'narrow'), pairs))]
    pallas_call x16 -> x17, Pallas kernels: 15.5 us -> 16.7 us  [call(): pl.pallas_call(kernel, out_shape=out_shape, in_specs=specs, out_specs=[vm...]
    ppermute x1, starting transfers between devices: 3.06 us -> 4.21 us  [local(): other = lax.ppermute(own, 'narrow', [(i, i ^ 1) for i in range(narrow)])]
    ppermute x3, starting transfers between devices: 4.11 us -> 4.8 us  [local(): lax.ppermute(mine, 'narrow', [(i, i ^ 2 * d) for i in range(narrow)])]
  transfers between devices with their start and end apart: 14 -> 12, of which waited for: 8 -> 8; matrix products, arithmetic and copies ran while one was open for 0% -> 0% of each run, Pallas kernels for 18% -> 18%
where the time goes in v4:
time: 48.7 us; the launch traced here: 48.6 us
  starting transfers between devices  20.7 us (43%)
  Pallas kernels  16.7 us (34%)
  waiting for transfers between devices  10.3 us (21%)
  between operations  0.81 us (2%)
    pallas_call x17, Pallas kernels, call(): pl.pallas_call(kernel, out_shape=out_shape, in_specs=specs, out_specs=[vm...  16.7 us
    ppermute x6, starting transfers between devices, swap_slab(): results.append(lax.ppermute(value, ('slab', 'narrow'), pairs))  9.68 us
    ppermute x6, waiting for transfers between devices, swap_slab(): results.append(lax.ppermute(value, ('slab', 'narrow'), pairs))  6.35 us
    ppermute x3, starting transfers between devices, local(): lax.ppermute(mine, 'narrow', [(i, i ^ 2 * d) for i in range(narrow)])  4.8 us
    ppermute x1, starting transfers between devices, local(): other = lax.ppermute(own, 'narrow', [(i, i ^ 1) for i in range(narrow)])  4.21 us
    ppermute x3, waiting for transfers between devices, local(): lax.ppermute(mine, 'narrow', [(i, i ^ 2 * d) for i in range(narrow)])  3.64 us
    ppermute x2, starting transfers between devices, swap_narrow(): lax.ppermute(value, 'narrow', pair)  1.96 us
  transfers between devices with their start and end apart: 12, of which 8 were waited for; matrix products, arithmetic and copies ran while one was open for 0% of the time, Pallas kernels for 18%

profile of v4, /device:TPU:25, one launch (start us, length us, event | category | flops | bytes accessed | tf_op | source)
XLA Modules:
  0.0 48.6 jit_solution(8195368641668621956)
XLA Ops:
  0.7 1.1 %shard_map.132 = (f32[4,3,16,256]{3,2,1,0:T(8,128)S(1)}, f32[4,3,16,256]{3,2,1,0:T(8,128)S(1)}) custom-call(f32[4,16,16,256]{3,2,1,0:T(8,128)} %rhs.1), custom_call_target="tpu_custom_call" | custom-call | flops 2147483648 | bytes 1441792 | tf_op jit(solution)/shard_map/pallas_call | solution.py:515
  1.8 0.8 %collective-permute-start = (f32[4,3,16,256]{3,2,1,0:T(8,128)S(1)}, f32[4,3,16,256]{3,2,1,0:T(8,128)S(1)}, u32[]{:S(2)}, u32[]{:S(2)}) collective-permute-start(f32[4,3,16,256]{3,2,1,0:T(8,128)S(1)} %get-tuple-element.50), channel_id=1, source_target_pairs={{0,1},{1,0},{2,3},{3,2},{4,5},{5,4},{6,7},{7,6},{8,9},{9,8},{10,11... | collective-permute-start | bytes 589832 | tf_op jit(solution)/shard_map/ppermute | solution.py:529
  2.6 1.2 %collective-permute-start.1 = (f32[4,3,16,256]{3,2,1,0:T(8,128)S(1)}, f32[4,3,16,256]{3,2,1,0:T(8,128)S(1)}, u32[]{:S(2)}, u32[]{:S(2)}) collective-permute-start(f32[4,3,16,256]{3,2,1,0:T(8,128)S(1)} %get-tuple-element.51), channel_id=1, source_target_pairs={{0,7},{1,2},{2,1},{3,4},{4,3},{5,6},{6,5},{7,0},{8,15},{9,10},{10,... | collective-permute-start | bytes 589832 | tf_op jit(solution)/shard_map/ppermute | solution.py:529
  3.8 0.7 %shard_map.129 = (f32[4,4,40,256]{3,2,1,0:T(8,128)S(1)}, f32[4,24,1024]{2,1,0:T(8,128)S(1)}, bf16[4,4,128,256]{3,2,1,0:T(8,128)(2,1)S(1)}, bf16[216,384]{1,0:T(8,128)(2,1)S(1)}, bf16[64,128]{1,0:T(8,128)(2,1)S(1)}) custom-call(f32[1024,256]{1,0:T(8,128)S(1)} %bitcast.14, f32[24,40]{1,0:T(8,128)S(1)} %copy-done.9, f32[40,40]{1,0:T(8,128)S(1)} %copy-done.8, ...), custom_call_target="tpu_custom_call" | custom-call | flops 536870912 | bytes 3441920 | tf_op jit(solution)/shard_map/pallas_call | solution.py:515
  5.2 2.5 %shard_map.130 = (f32[1024,160]{1,0:T(8,128)}, f32[4,24,1024]{2,1,0:T(8,128)S(1)}) custom-call(bf16[4,4,128,256]{3,2,1,0:T(8,128)(2,1)S(1)} %get-tuple-element.43.cat, bf16[216,384]{1,0:T(8,128)(2,1)S(1)} %get-tuple-element.44.packed, f32[4,4,40,256]{3,2,1,0:T(8,128)S(1)} %get-tuple-element.45.solution_in, f32[4,24,1024]{2,1,0:T(8,128)S(1)} %get-tuple-element.46.skeleton), custom_call_target="tpu_custom_call" | custom-call | flops 1073741824 | bytes 3311616 | tf_op jit(solution)/shard_map/pallas_call | solution.py:515
  8.0 1.0 %shard_map.133 = (bf16[4,128,512]{2,1,0:T(8,128)(2,1)S(1)}, f32[4,24,512]{2,1,0:T(8,128)S(1)}, f32[24,1280]{1,0:T(8,128)S(1)}, f32[24,1280]{1,0:T(8,128)S(1)}) custom-call(f32[4,24,1024]{2,1,0:T(8,128)S(1)} %get-tuple-element.48.after.inner, f32[2,24,1024]{2,1,0:T(8,128)S(1)} %shard_map.131.edge, bf16[216,384]{1,0:T(8,128)(2,1)S(1)} %get-tuple-element.44.packed, ...), custom_call_target="tpu_custom_call" | custom-call | bytes 2394112 | tf_op jit(solution)/shard_map/pallas_call | solution.py:515
  9.0 5.8 %collective-permute-start.3 = (f32[24,1280]{1,0:T(8,128)S(1)}, f32[24,1280]{1,0:T(8,128)S(1)}, u32[]{:S(2)}, u32[]{:S(2)}) collective-permute-start(f32[24,1280]{1,0:T(8,128)S(1)} %get-tuple-element.57), channel_id=1, source_target_pairs={{0,1},{1,0},{2,3},{3,2},{4,5},{5,4},{6,7},{7,6},{8,16},{9,17},{10,... | collective-permute-start | bytes 368648 | tf_op jit(solution)/shard_map/ppermute | solution.py:542
  15.2 0.9 %shard_map.134 = (f32[4,24,1024]{2,1,0:T(8,128)S(1)}, f32[4,24,512]{2,1,0:T(8,128)S(1)}) custom-call(bf16[216,384]{1,0:T(8,128)(2,1)S(1)} %get-tuple-element.44.packed, f32[24,1280]{1,0:T(8,128)S(1)} %get-tuple-element.52.after, f32[4,24,1024]{2,1,0:T(8,128)S(1)} %get-tuple-element.48.after.inner, bf16[4,128,512]{2,1,0:T(8,128)(2,1)S(1)} %get-tuple-element.53.strips, ...), custom_call_target="tpu_custom_call" | custom-call | flops 536870912 | bytes 1869824 | tf_op jit(solution)/shard_map/pallas_call | solution.py:515
  16.1 1.0 %collective-permute-done.3.plane_b = f32[24,1280]{1,0:T(8,128)S(1)} collective-permute-done((f32[24,1280]{1,0:T(8,128)S(1)}, f32[24,1280]{1,0:T(8,128)S(1)}, u32[]{:S(2)}, u32[]{:S(2)}) %collective-permute-start.3) | collective-permute-done | bytes 122912 | tf_op jit(solution)/shard_map/ppermute | solution.py:542
  17.1 1.8 %collective-permute-done.2.plane_a = f32[24,1280]{1,0:T(8,128)S(1)} collective-permute-done((f32[24,1280]{1,0:T(8,128)S(1)}, f32[24,1280]{1,0:T(8,128)S(1)}, u32[]{:S(2)}, u32[]{:S(2)}) %collective-permute-start.2) | collective-permute-done | bytes 122912 | tf_op jit(solution)/shard_map/ppermute | solution.py:542
  18.8 1.9 %shard_map.136 = (f32[144,512]{1,0:T(8,128)S(1)}, f32[48,512]{1,0:T(8,128)S(1)}, f32[48,128]{1,0:T(8,128)S(1)}, f32[48,128]{1,0:T(8,128)S(1)}) custom-call(f32[4,24,1024]{2,1,0:T(8,128)S(1)} %get-tuple-element.55.rest1, f32[4,24,512]{2,1,0:T(8,128)S(1)} %get-tuple-element.56.strip_rest, f32[24,1280]{1,0:T(8,128)S(1)} %collective-permute-done.2.plane_a, ...), custom_call_target="tpu_custom_call" | custom-call | flops 536870912 | bytes 2397184 | tf_op jit(solution)/shard_map/pallas_call | solution.py:515
  20.7 1.1 %shard_map.137 = (f32[48,512]{1,0:T(8,128)S(1)}, f32[48,256]{1,0:T(8,128)S(1)}, f32[48,256]{1,0:T(8,128)S(1)}) custom-call(f32[144,512]{1,0:T(8,128)S(1)} %get-tuple-element.64.solution_in, f32[48,512]{1,0:T(8,128)S(1)} %get-tuple-element.65.skeleton, f32[48,128]{1,0:T(8,128)S(1)} %get-tuple-element.66.above, f32[48,128]{1,0:T(8,128)S(1)} %get-tuple-element.67.below, ...), custom_call_target="tpu_custom_call" | custom-call | flops 536870912 | bytes 1385472 | tf_op jit(solution)/shard_map/pallas_call | solution.py:515
  21.8 1.9 %collective-permute-start.5 = (f32[48,256]{1,0:T(8,128)S(1)}, f32[48,256]{1,0:T(8,128)S(1)}, u32[]{:S(2)}, u32[]{:S(2)}) collective-permute-start(f32[48,256]{1,0:T(8,128)S(1)} %get-tuple-element.70), channel_id=1, source_target_pairs={{0,1},{1,0},{2,3},{3,2},{4,5},{5,4},{6,7},{7,6},{8,16},{9,17},{10,... | collective-permute-start | bytes 147464 | tf_op jit(solution)/shard_map/ppermute | solution.py:542
  23.8 0.8 %shard_map.140 = (bf16[384,288]{1,0:T(8,128)(2,1)S(1)}, bf16[384,288]{1,0:T(8,128)(2,1)S(1)}, bf16[2592,288]{1,0:T(8,128)(2,1)S(1)}, bf16[2592,288]{1,0:T(8,128)(2,1)S(1)}, bf16[128,256]{1,0:T(8,128)(2,1)S(1)}) custom-call(f32[48,256]{1,0:T(8,128)S(1)} %get-tuple-element.68.after, f32[96,288]{1,0:T(8,128)S(1)} %copy-done.4, f32[288,288]{1,0:T(8,128)S(1)} %copy-done.2, ...), custom_call_target="tpu_custom_call" | custom-call | bytes 6922240 | tf_op jit(solution)/shard_map/pallas_call | solution.py:515
  25.3 1.7 %collective-permute-done.5.plane_b = f32[48,256]{1,0:T(8,128)S(1)} collective-permute-done((f32[48,256]{1,0:T(8,128)S(1)}, f32[48,256]{1,0:T(8,128)S(1)}, u32[]{:S(2)}, u32[]{:S(2)}) %collective-permute-start.5) | collective-permute-done | bytes 49184 | tf_op jit(solution)/shard_map/ppermute | solution.py:542
  27.0 1.8 %shard_map.141 = (f32[288,128]{1,0:T(8,128)S(1)}, f32[96,128]{1,0:T(8,128)S(1)}, f32[96,128]{1,0:T(8,128)S(1)}, f32[96,128]{1,0:T(8,128)S(1)}) custom-call(f32[48,512]{1,0:T(8,128)S(1)} %shard_map.139.rest2, f32[48,256]{1,0:T(8,128)S(1)} %collective-permute-done.4.plane_a, f32[48,256]{1,0:T(8,128)S(1)} %collective-permute-done.5.plane_b, ...), custom_call_target="tpu_custom_call" | custom-call | flops 536870912 | bytes 3985408 | tf_op jit(solution)/shard_map/pallas_call | solution.py:515
  28.8 1.9 %collective-permute-start.7 = (f32[96,128]{1,0:T(8,128)S(1)}, f32[96,128]{1,0:T(8,128)S(1)}, u32[]{:S(2)}, u32[]{:S(2)}) collective-permute-start(f32[96,128]{1,0:T(8,128)S(1)} %get-tuple-element.81), channel_id=1, source_target_pairs={{0,1},{1,0},{2,3},{3,2},{4,5},{5,4},{6,7},{7,6},{8,16},{9,17},{10,... | collective-permute-start | bytes 147464 | tf_op jit(solution)/shard_map/ppermute | solution.py:542
  30.7 1.3 %shard_map.142 = (f32[4,4,1152]{2,1,0:T(4,128)}, f32[96,128]{1,0:T(8,128)S(1)}) custom-call(f32[96,128]{1,0:T(8,128)S(1)} %get-tuple-element.76.after, f32[288,128]{1,0:T(8,128)S(1)} %get-tuple-element.77.solution_in, f32[96,128]{1,0:T(8,128)S(1)} %get-tuple-element.78.skeleton, bf16[2592,288]{1,0:T(8,128)(2,1)S(1)} %get-tuple-element.74.update_h, ...), custom_call_target="tpu_custom_call" | custom-call | flops 536870912 | bytes 3305472 | tf_op jit(solution)/shard_map/pallas_call | solution.py:515
  32.0 1.9 %collective-permute-done.7.plane_b = f32[96,128]{1,0:T(8,128)S(1)} collective-permute-done((f32[96,128]{1,0:T(8,128)S(1)}, f32[96,128]{1,0:T(8,128)S(1)}, u32[]{:S(2)}, u32[]{:S(2)}) %collective-permute-start.7) | collective-permute-done | bytes 49184 | tf_op jit(solution)/shard_map/ppermute | solution.py:542
  34.1 4.1 %collective-permute-start.10 = (f32[24,384]{1,0:T(8,128)S(1)}, f32[24,384]{1,0:T(8,128)S(1)}, u32[]{:S(2)}, u32[]{:S(2)}) collective-permute-start(f32[24,384]{1,0:T(8,128)S(1)} %shard_map.143.refs_0_), channel_id=1, source_target_pairs={{0,6},{1,7},{2,4},{3,5},{4,2},{5,3},{6,0},{7,1},{8,14},{9,15},{10,... | collective-permute-start | bytes 110600 | tf_op jit(solution)/shard_map/ppermute | solution.py:670
  39.6 3.0 %collective-permute-done.9.refs_2_ = f32[24,384]{1,0:T(8,128)S(1)} collective-permute-done((f32[24,384]{1,0:T(8,128)S(1)}, f32[24,384]{1,0:T(8,128)S(1)}, u32[]{:S(2)}, u32[]{:S(2)}) %collective-permute-start.9) | collective-permute-done | bytes 36896 | tf_op jit(solution)/shard_map/ppermute | solution.py:670
  42.6 4.2 %collective-permute-start.11 = (f32[96,384]{1,0:T(8,128)S(1)}, f32[96,384]{1,0:T(8,128)S(1)}, u32[]{:S(2)}, u32[]{:S(2)}) collective-permute-start(f32[96,384]{1,0:T(8,128)S(1)} %shard_map.144.own), channel_id=1, source_target_pairs={{0,1},{1,0},{2,3},{3,2},{4,5},{5,4},{6,7},{7,6},{8,9},{9,8},{10,11... | collective-permute-start | bytes 442376 | tf_op jit(solution)/shard_map/ppermute | solution.py:674
  46.8 0.9 %shard_map.138 = f32[128,576]{1,0:T(8,128)} custom-call(f32[48,256]{1,0:T(8,128)S(1)} %get-tuple-element.68.after, f32[144,512]{1,0:T(8,128)S(1)} %get-tuple-element.64.solution_in), custom_call_target="tpu_custom_call" | custom-call | bytes 589824 | tf_op jit(solution)/shard_map/pallas_call | solution.py:515
  47.8 0.8 %shard_map.145 = f32[32,4,384]{2,1,0:T(4,128)} custom-call(f32[96,384]{1,0:T(8,128)S(1)} %shard_map.144.own, f32[96,384]{1,0:T(8,128)S(1)} %collective-permute-done.11.other), custom_call_target="tpu_custom_call" | custom-call | bytes 491520 | tf_op jit(solution)/shard_map/pallas_call | solution.py:515
  (37 shorter events, 3.7 us)
Async XLA Ops:
  0.6 3.2 %copy-start.6 = (f32[4,16,16,256]{3,2,1,0:T(8,128)S(1)}, f32[4,16,16,256]{3,2,1,0:T(8,128)}, u32[]{:S(2)}) copy-start(f32[4,16,16,256]{3,2,1,0:T(8,128)} %rhs.1) | copy-start | bytes 3145732
  0.6 3.2 %copy-start.7 = (f32[27,24,40]{2,1,0:T(8,128)S(1)}, f32[27,24,40]{2,1,0:T(8,128)}, u32[]{:S(2)}) copy-start(f32[27,24,40]{2,1,0:T(8,128)} %param.13) | copy-start | bytes 311044
  0.7 3.1 %copy-start.8 = (f32[40,40]{1,0:T(8,128)S(1)}, f32[40,40]{1,0:T(8,128)}, u32[]{:S(2)}) copy-start(f32[40,40]{1,0:T(8,128)} %elim.3) | copy-start | bytes 19204
  0.7 3.1 %copy-start.9 = (f32[24,40]{1,0:T(8,128)S(1)}, f32[24,40]{1,0:T(8,128)}, u32[]{:S(2)}) copy-start(f32[24,40]{1,0:T(8,128)} %skel.3) | copy-start | bytes 11524
  1.8 5.9 %collective-permute-start = (f32[4,3,16,256]{3,2,1,0:T(8,128)S(1)}, f32[4,3,16,256]{3,2,1,0:T(8,128)S(1)}, u32[]{:S(2)}, u32[]{:S(2)}) collective-permute-start(f32[4,3,16,256]{3,2,1,0:T(8,128)S(1)} %get-tuple-element.50), channel_id=1, source_target_pairs={{0,1},{1,0},{2,3},{3,2},{4,5},{5,4},{6,7},{7,6},{8,9},{9,8},{10,11... | collective-permute-start | bytes 589832 | tf_op jit(solution)/shard_map/ppermute | solution.py:529
  2.6 5.4 %collective-permute-start.1 = (f32[4,3,16,256]{3,2,1,0:T(8,128)S(1)}, f32[4,3,16,256]{3,2,1,0:T(8,128)S(1)}, u32[]{:S(2)}, u32[]{:S(2)}) collective-permute-start(f32[4,3,16,256]{3,2,1,0:T(8,128)S(1)} %get-tuple-element.51), channel_id=1, source_target_pairs={{0,7},{1,2},{2,1},{3,4},{4,3},{5,6},{6,5},{7,0},{8,15},{9,10},{10,... | collective-permute-start | bytes 589832 | tf_op jit(solution)/shard_map/ppermute | solution.py:529
  5.2 9.6 %copy-start.1 = (f32[27,48,144]{2,1,0:T(8,128)S(1)}, f32[27,48,144]{2,1,0:T(8,128)}, u32[]{:S(2)}) copy-start(f32[27,48,144]{2,1,0:T(8,128)} %param.16) | copy-start | bytes 2239492
  5.2 9.6 %copy-start.3 = (f32[144,144]{1,0:T(8,128)S(1)}, f32[144,144]{1,0:T(8,128)}, u32[]{:S(2)}) copy-start(f32[144,144]{1,0:T(8,128)} %elim.4) | copy-start | bytes 248836
  5.2 9.6 %copy-start.5 = (f32[48,144]{1,0:T(8,128)S(1)}, f32[48,144]{1,0:T(8,128)}, u32[]{:S(2)}) copy-start(f32[48,144]{1,0:T(8,128)} %skel.4) | copy-start | bytes 82948
  9.0 8.1 %collective-permute-start.3 = (f32[24,1280]{1,0:T(8,128)S(1)}, f32[24,1280]{1,0:T(8,128)S(1)}, u32[]{:S(2)}, u32[]{:S(2)}) collective-permute-start(f32[24,1280]{1,0:T(8,128)S(1)} %get-tuple-element.57), channel_id=1, source_target_pairs={{0,1},{1,0},{2,3},{3,2},{4,5},{5,4},{6,7},{7,6},{8,16},{9,17},{10,... | collective-permute-start | bytes 368648 | tf_op jit(solution)/shard_map/ppermute | solution.py:542
  14.8 4.0 %collective-permute-start.2 = (f32[24,1280]{1,0:T(8,128)S(1)}, f32[24,1280]{1,0:T(8,128)S(1)}, u32[]{:S(2)}, u32[]{:S(2)}) collective-permute-start(f32[24,1280]{1,0:T(8,128)S(1)} %get-tuple-element.52.after), channel_id=1, source_target_pairs={{0,8},{1,9},{2,10},{3,11},{4,12},{5,13},{6,14},{7,15},{8,0},{9,1},... | collective-permute-start | bytes 368648 | tf_op jit(solution)/shard_map/ppermute | solution.py:542
  18.8 4.9 %copy-start = (f32[27,96,288]{2,1,0:T(8,128)S(1)}, f32[27,96,288]{2,1,0:T(8,128)}, u32[]{:S(2)}) copy-start(f32[27,96,288]{2,1,0:T(8,128)} %param.19) | copy-start | bytes 8957956
  18.8 4.9 %copy-start.2 = (f32[288,288]{1,0:T(8,128)S(1)}, f32[288,288]{1,0:T(8,128)}, u32[]{:S(2)}) copy-start(f32[288,288]{1,0:T(8,128)} %elim.5) | copy-start | bytes 995332
  18.8 4.9 %copy-start.4 = (f32[96,288]{1,0:T(8,128)S(1)}, f32[96,288]{1,0:T(8,128)}, u32[]{:S(2)}) copy-start(f32[96,288]{1,0:T(8,128)} %skel.5) | copy-start | bytes 331780
  21.8 5.1 %collective-permute-start.5 = (f32[48,256]{1,0:T(8,128)S(1)}, f32[48,256]{1,0:T(8,128)S(1)}, u32[]{:S(2)}, u32[]{:S(2)}) collective-permute-start(f32[48,256]{1,0:T(8,128)S(1)} %get-tuple-element.70), channel_id=1, source_target_pairs={{0,1},{1,0},{2,3},{3,2},{4,5},{5,4},{6,7},{7,6},{8,16},{9,17},{10,... | collective-permute-start | bytes 147464 | tf_op jit(solution)/shard_map/ppermute | solution.py:542
  23.8 3.2 %collective-permute-start.4 = (f32[48,256]{1,0:T(8,128)S(1)}, f32[48,256]{1,0:T(8,128)S(1)}, u32[]{:S(2)}, u32[]{:S(2)}) collective-permute-start(f32[48,256]{1,0:T(8,128)S(1)} %get-tuple-element.68.after), channel_id=1, source_target_pairs={{0,8},{1,9},{2,10},{3,11},{4,12},{5,13},{6,14},{7,15},{8,0},{9,1},... | collective-permute-start | bytes 147464 | tf_op jit(solution)/shard_map/ppermute | solution.py:542
  28.8 5.1 %collective-permute-start.7 = (f32[96,128]{1,0:T(8,128)S(1)}, f32[96,128]{1,0:T(8,128)S(1)}, u32[]{:S(2)}, u32[]{:S(2)}) collective-permute-start(f32[96,128]{1,0:T(8,128)S(1)} %get-tuple-element.81), channel_id=1, source_target_pairs={{0,1},{1,0},{2,3},{3,2},{4,5},{5,4},{6,7},{7,6},{8,16},{9,17},{10,... | collective-permute-start | bytes 147464 | tf_op jit(solution)/shard_map/ppermute | solution.py:542
  30.7 3.2 %collective-permute-start.6 = (f32[96,128]{1,0:T(8,128)S(1)}, f32[96,128]{1,0:T(8,128)S(1)}, u32[]{:S(2)}, u32[]{:S(2)}) collective-permute-start(f32[96,128]{1,0:T(8,128)S(1)} %get-tuple-element.76.after), channel_id=1, source_target_pairs={{0,8},{1,9},{2,10},{3,11},{4,12},{5,13},{6,14},{7,15},{8,0},{9,1},... | collective-permute-start | bytes 147464 | tf_op jit(solution)/shard_map/ppermute | solution.py:542
  34.1 5.5 %collective-permute-start.10 = (f32[24,384]{1,0:T(8,128)S(1)}, f32[24,384]{1,0:T(8,128)S(1)}, u32[]{:S(2)}, u32[]{:S(2)}) collective-permute-start(f32[24,384]{1,0:T(8,128)S(1)} %shard_map.143.refs_0_), channel_id=1, source_target_pairs={{0,6},{1,7},{2,4},{3,5},{4,2},{5,3},{6,0},{7,1},{8,14},{9,15},{10,... | collective-permute-start | bytes 110600 | tf_op jit(solution)/shard_map/ppermute | solution.py:670
  38.3 4.3 %collective-permute-start.9 = (f32[24,384]{1,0:T(8,128)S(1)}, f32[24,384]{1,0:T(8,128)S(1)}, u32[]{:S(2)}, u32[]{:S(2)}) collective-permute-start(f32[24,384]{1,0:T(8,128)S(1)} %shard_map.143.refs_0_), channel_id=1, source_target_pairs={{0,4},{1,5},{2,6},{3,7},{4,0},{5,1},{6,2},{7,3},{8,12},{9,13},{10,... | collective-permute-start | bytes 110600 | tf_op jit(solution)/shard_map/ppermute | solution.py:670
  38.3 4.3 %collective-permute-start.8 = (f32[24,384]{1,0:T(8,128)S(1)}, f32[24,384]{1,0:T(8,128)S(1)}, u32[]{:S(2)}, u32[]{:S(2)}) collective-permute-start(f32[24,384]{1,0:T(8,128)S(1)} %shard_map.143.refs_0_), channel_id=1, source_target_pairs={{0,2},{1,3},{2,0},{3,1},{4,6},{5,7},{6,4},{7,5},{8,10},{9,11},{10,... | collective-permute-start | bytes 110600 | tf_op jit(solution)/shard_map/ppermute | solution.py:670
  42.6 5.2 %collective-permute-start.11 = (f32[96,384]{1,0:T(8,128)S(1)}, f32[96,384]{1,0:T(8,128)S(1)}, u32[]{:S(2)}, u32[]{:S(2)}) collective-permute-start(f32[96,384]{1,0:T(8,128)S(1)} %shard_map.144.own), channel_id=1, source_target_pairs={{0,1},{1,0},{2,3},{3,2},{4,5},{5,4},{6,7},{7,6},{8,9},{9,8},{10,11... | collective-permute-start | bytes 442376 | tf_op jit(solution)/shard_map/ppermute | solution.py:674

commit v5 on v4

--- a/solution.py
+++ b/solution.py
@@ -24,6 +24,12 @@
 def dot3(a_high, a_low, b):
     b_high, b_low = halves(b)
     return dot(a_high, b_high) + dot(a_low, b_high) + dot(a_high, b_low)
+
+
+def dot3_narrow(a_high, a_low, b):
+    b_high, b_low = halves(b)
+    both = dot(a_high, jnp.concatenate([b_high, b_low], axis=1))
+    return both[:, :128] + both[:, 128:] + dot(a_low, b_high)
 
 
 def lanes(shape):
@@ -65,10 +71,14 @@
 
 def fine_ends_kernel(rhs, send_a, send_b, sems):
     upward = jnp.where(lax.axis_index("narrow") % 2 == 0, 13, 0)
-    copies = [
-        pltpu.make_async_copy(rhs.at[:, pl.ds(upward, 3)], send_a, sems.at[0]),
-        pltpu.make_async_copy(rhs.at[:, pl.ds(13 - upward, 3)], send_b, sems.at[1]),
-    ]
+    copies = []
+    for x in range(4):
+        for side, (start, out) in enumerate(((upward, send_a), (13 - upward, send_b))):
+            copies.append(
+                pltpu.make_async_copy(
+                    rhs.at[x, pl.ds(start, 3)], out.at[x], sems.at[x * 2 + side]
+                )
+            )
     for copy in copies:
         copy.start()
     for copy in copies:
@@ -326,7 +336,7 @@
         for dy in (0, 2):
             base = (dx * 9 + dy * 3) * 48
             rows.append(slice(base, base + 144))
-        both = [dot3(update_h[r, :], update_l[r, :], right) for r in rows]
+        both = [dot3_narrow(update_h[r, :], update_l[r, :], right) for r in rows]
         for end in range(2):
             sums[end].append(along_z(both[end], 48, l, 7))
     x = spot // 8 % 2
@@ -434,7 +444,7 @@
             moved = roll(value, 32 * (k - child % 4))
             total = moved if total is None else jnp.where(half // 32 == k, moved, total)
         vector[child * 48 : (child + 1) * 48, :] = total
-    result = dot3(solve_h[...], solve_l[...], vector[96:, :])
+    result = dot3_narrow(solve_h[...], solve_l[...], vector[96:, :])
     solution_vector = result[:288]
     solution_out[...] = solution_vector
     skeleton[...] = vector[:96, :] - result[288:]
@@ -553,7 +563,7 @@
             [((4, 3, 16, 256), F32)] * 2,
             flops=1 << 31,
             where=pltpu.HBM,
-            sems=2,
+            sems=8,
         )
     )
     solution1, skeleton, cat, packed, solver = call(

time: 48.7 us -> 48.6 us (level)
  no operation moved by 1% of the time
where the time goes in v5:
time: 48.6 us; the launch traced here: 48.5 us
  starting transfers between devices  20.6 us (42%)
  Pallas kernels  16.6 us (34%)
  waiting for transfers between devices  10.3 us (21%)
  between operations  0.8 us (2%)
    pallas_call x17, Pallas kernels, call(): pl.pallas_call(kernel, out_shape=out_shape, in_specs=specs, out_specs=[vm...  16.6 us
    ppermute x6, starting transfers between devices, swap_slab(): results.append(lax.ppermute(value, ('slab', 'narrow'), pairs))  9.66 us
    ppermute x6, waiting for transfers between devices, swap_slab(): results.append(lax.ppermute(value, ('slab', 'narrow'), pairs))  6.36 us
    ppermute x3, starting transfers between devices, local(): lax.ppermute(mine, 'narrow', [(i, i ^ 2 * d) for i in range(narrow)])  4.8 us
    ppermute x1, starting transfers between devices, local(): other = lax.ppermute(own, 'narrow', [(i, i ^ 1) for i in range(narrow)])  4.21 us
    ppermute x3, waiting for transfers between devices, local(): lax.ppermute(mine, 'narrow', [(i, i ^ 2 * d) for i in range(narrow)])  3.64 us
    ppermute x2, starting transfers between devices, swap_narrow(): lax.ppermute(value, 'narrow', pair)  1.96 us
  transfers between devices with their start and end apart: 12, of which 8 were waited for; matrix products, arithmetic and copies ran while one was open for 0% of the time, Pallas kernels for 18%

profile of v5, /device:TPU:25, one launch (start us, length us, event | category | flops | bytes accessed | tf_op | source)
XLA Modules:
  0.0 48.5 jit_solution(9343232887707903829)
XLA Ops:
  0.7 1.1 %shard_map.132 = (f32[4,3,16,256]{3,2,1,0:T(8,128)S(1)}, f32[4,3,16,256]{3,2,1,0:T(8,128)S(1)}) custom-call(f32[4,16,16,256]{3,2,1,0:T(8,128)} %rhs.1), custom_call_target="tpu_custom_call" | custom-call | flops 2147483648 | bytes 1441792 | tf_op jit(solution)/shard_map/pallas_call | solution.py:525
  1.8 0.8 %collective-permute-start = (f32[4,3,16,256]{3,2,1,0:T(8,128)S(1)}, f32[4,3,16,256]{3,2,1,0:T(8,128)S(1)}, u32[]{:S(2)}, u32[]{:S(2)}) collective-permute-start(f32[4,3,16,256]{3,2,1,0:T(8,128)S(1)} %get-tuple-element.50), channel_id=1, source_target_pairs={{0,1},{1,0},{2,3},{3,2},{4,5},{5,4},{6,7},{7,6},{8,9},{9,8},{10,11... | collective-permute-start | bytes 589832 | tf_op jit(solution)/shard_map/ppermute | solution.py:539
  2.6 1.2 %collective-permute-start.1 = (f32[4,3,16,256]{3,2,1,0:T(8,128)S(1)}, f32[4,3,16,256]{3,2,1,0:T(8,128)S(1)}, u32[]{:S(2)}, u32[]{:S(2)}) collective-permute-start(f32[4,3,16,256]{3,2,1,0:T(8,128)S(1)} %get-tuple-element.51), channel_id=1, source_target_pairs={{0,7},{1,2},{2,1},{3,4},{4,3},{5,6},{6,5},{7,0},{8,15},{9,10},{10,... | collective-permute-start | bytes 589832 | tf_op jit(solution)/shard_map/ppermute | solution.py:539
  3.8 0.7 %shard_map.129 = (f32[4,4,40,256]{3,2,1,0:T(8,128)S(1)}, f32[4,24,1024]{2,1,0:T(8,128)S(1)}, bf16[4,4,128,256]{3,2,1,0:T(8,128)(2,1)S(1)}, bf16[216,384]{1,0:T(8,128)(2,1)S(1)}, bf16[64,128]{1,0:T(8,128)(2,1)S(1)}) custom-call(f32[1024,256]{1,0:T(8,128)S(1)} %bitcast.14, f32[24,40]{1,0:T(8,128)S(1)} %copy-done.9, f32[40,40]{1,0:T(8,128)S(1)} %copy-done.8, ...), custom_call_target="tpu_custom_call" | custom-call | flops 536870912 | bytes 3441920 | tf_op jit(solution)/shard_map/pallas_call | solution.py:525
  5.2 2.5 %shard_map.130 = (f32[1024,160]{1,0:T(8,128)}, f32[4,24,1024]{2,1,0:T(8,128)S(1)}) custom-call(bf16[4,4,128,256]{3,2,1,0:T(8,128)(2,1)S(1)} %get-tuple-element.43.cat, bf16[216,384]{1,0:T(8,128)(2,1)S(1)} %get-tuple-element.44.packed, f32[4,4,40,256]{3,2,1,0:T(8,128)S(1)} %get-tuple-element.45.solution_in, f32[4,24,1024]{2,1,0:T(8,128)S(1)} %get-tuple-element.46.skeleton), custom_call_target="tpu_custom_call" | custom-call | flops 1073741824 | bytes 3311616 | tf_op jit(solution)/shard_map/pallas_call | solution.py:525
  8.0 1.0 %shard_map.133 = (bf16[4,128,512]{2,1,0:T(8,128)(2,1)S(1)}, f32[4,24,512]{2,1,0:T(8,128)S(1)}, f32[24,1280]{1,0:T(8,128)S(1)}, f32[24,1280]{1,0:T(8,128)S(1)}) custom-call(f32[4,24,1024]{2,1,0:T(8,128)S(1)} %get-tuple-element.48.after.inner, f32[2,24,1024]{2,1,0:T(8,128)S(1)} %shard_map.131.edge, bf16[216,384]{1,0:T(8,128)(2,1)S(1)} %get-tuple-element.44.packed, ...), custom_call_target="tpu_custom_call" | custom-call | bytes 2394112 | tf_op jit(solution)/shard_map/pallas_call | solution.py:525
  9.0 5.8 %collective-permute-start.3 = (f32[24,1280]{1,0:T(8,128)S(1)}, f32[24,1280]{1,0:T(8,128)S(1)}, u32[]{:S(2)}, u32[]{:S(2)}) collective-permute-start(f32[24,1280]{1,0:T(8,128)S(1)} %get-tuple-element.57), channel_id=1, source_target_pairs={{0,1},{1,0},{2,3},{3,2},{4,5},{5,4},{6,7},{7,6},{8,16},{9,17},{10,... | collective-permute-start | bytes 368648 | tf_op jit(solution)/shard_map/ppermute | solution.py:552
  15.2 0.9 %shard_map.134 = (f32[4,24,1024]{2,1,0:T(8,128)S(1)}, f32[4,24,512]{2,1,0:T(8,128)S(1)}) custom-call(bf16[216,384]{1,0:T(8,128)(2,1)S(1)} %get-tuple-element.44.packed, f32[24,1280]{1,0:T(8,128)S(1)} %get-tuple-element.52.after, f32[4,24,1024]{2,1,0:T(8,128)S(1)} %get-tuple-element.48.after.inner, bf16[4,128,512]{2,1,0:T(8,128)(2,1)S(1)} %get-tuple-element.53.strips, ...), custom_call_target="tpu_custom_call" | custom-call | flops 536870912 | bytes 1869824 | tf_op jit(solution)/shard_map/pallas_call | solution.py:525
  16.1 1.0 %collective-permute-done.3.plane_b = f32[24,1280]{1,0:T(8,128)S(1)} collective-permute-done((f32[24,1280]{1,0:T(8,128)S(1)}, f32[24,1280]{1,0:T(8,128)S(1)}, u32[]{:S(2)}, u32[]{:S(2)}) %collective-permute-start.3) | collective-permute-done | bytes 122912 | tf_op jit(solution)/shard_map/ppermute | solution.py:552
  17.1 1.8 %collective-permute-done.2.plane_a = f32[24,1280]{1,0:T(8,128)S(1)} collective-permute-done((f32[24,1280]{1,0:T(8,128)S(1)}, f32[24,1280]{1,0:T(8,128)S(1)}, u32[]{:S(2)}, u32[]{:S(2)}) %collective-permute-start.2) | collective-permute-done | bytes 122912 | tf_op jit(solution)/shard_map/ppermute | solution.py:552
  18.8 1.8 %shard_map.136 = (f32[144,512]{1,0:T(8,128)S(1)}, f32[48,512]{1,0:T(8,128)S(1)}, f32[48,128]{1,0:T(8,128)S(1)}, f32[48,128]{1,0:T(8,128)S(1)}) custom-call(f32[4,24,1024]{2,1,0:T(8,128)S(1)} %get-tuple-element.55.rest1, f32[4,24,512]{2,1,0:T(8,128)S(1)} %get-tuple-element.56.strip_rest, f32[24,1280]{1,0:T(8,128)S(1)} %collective-permute-done.2.plane_a, ...), custom_call_target="tpu_custom_call" | custom-call | flops 536870912 | bytes 2397184 | tf_op jit(solution)/shard_map/pallas_call | solution.py:525
  20.7 1.1 %shard_map.137 = (f32[48,512]{1,0:T(8,128)S(1)}, f32[48,256]{1,0:T(8,128)S(1)}, f32[48,256]{1,0:T(8,128)S(1)}) custom-call(f32[144,512]{1,0:T(8,128)S(1)} %get-tuple-element.64.solution_in, f32[48,512]{1,0:T(8,128)S(1)} %get-tuple-element.65.skeleton, f32[48,128]{1,0:T(8,128)S(1)} %get-tuple-element.66.above, f32[48,128]{1,0:T(8,128)S(1)} %get-tuple-element.67.below, ...), custom_call_target="tpu_custom_call" | custom-call | flops 536870912 | bytes 1385472 | tf_op jit(solution)/shard_map/pallas_call | solution.py:525
  21.8 1.9 %collective-permute-start.5 = (f32[48,256]{1,0:T(8,128)S(1)}, f32[48,256]{1,0:T(8,128)S(1)}, u32[]{:S(2)}, u32[]{:S(2)}) collective-permute-start(f32[48,256]{1,0:T(8,128)S(1)} %get-tuple-element.70), channel_id=1, source_target_pairs={{0,1},{1,0},{2,3},{3,2},{4,5},{5,4},{6,7},{7,6},{8,16},{9,17},{10,... | collective-permute-start | bytes 147464 | tf_op jit(solution)/shard_map/ppermute | solution.py:552
  23.7 0.8 %shard_map.140 = (bf16[384,288]{1,0:T(8,128)(2,1)S(1)}, bf16[384,288]{1,0:T(8,128)(2,1)S(1)}, bf16[2592,288]{1,0:T(8,128)(2,1)S(1)}, bf16[2592,288]{1,0:T(8,128)(2,1)S(1)}, bf16[128,256]{1,0:T(8,128)(2,1)S(1)}) custom-call(f32[48,256]{1,0:T(8,128)S(1)} %get-tuple-element.68.after, f32[96,288]{1,0:T(8,128)S(1)} %copy-done.4, f32[288,288]{1,0:T(8,128)S(1)} %copy-done.2, ...), custom_call_target="tpu_custom_call" | custom-call | bytes 6922240 | tf_op jit(solution)/shard_map/pallas_call | solution.py:525
  25.3 1.7 %collective-permute-done.5.plane_b = f32[48,256]{1,0:T(8,128)S(1)} collective-permute-done((f32[48,256]{1,0:T(8,128)S(1)}, f32[48,256]{1,0:T(8,128)S(1)}, u32[]{:S(2)}, u32[]{:S(2)}) %collective-permute-start.5) | collective-permute-done | bytes 49184 | tf_op jit(solution)/shard_map/ppermute | solution.py:552
  26.9 1.7 %shard_map.141 = (f32[288,128]{1,0:T(8,128)S(1)}, f32[96,128]{1,0:T(8,128)S(1)}, f32[96,128]{1,0:T(8,128)S(1)}, f32[96,128]{1,0:T(8,128)S(1)}) custom-call(f32[48,512]{1,0:T(8,128)S(1)} %shard_map.139.rest2, f32[48,256]{1,0:T(8,128)S(1)} %collective-permute-done.4.plane_a, f32[48,256]{1,0:T(8,128)S(1)} %collective-permute-done.5.plane_b, ...), custom_call_target="tpu_custom_call" | custom-call | flops 536870912 | bytes 3985408 | tf_op jit(solution)/shard_map/pallas_call | solution.py:525
  28.7 1.9 %collective-permute-start.7 = (f32[96,128]{1,0:T(8,128)S(1)}, f32[96,128]{1,0:T(8,128)S(1)}, u32[]{:S(2)}, u32[]{:S(2)}) collective-permute-start(f32[96,128]{1,0:T(8,128)S(1)} %get-tuple-element.81), channel_id=1, source_target_pairs={{0,1},{1,0},{2,3},{3,2},{4,5},{5,4},{6,7},{7,6},{8,16},{9,17},{10,... | collective-permute-start | bytes 147464 | tf_op jit(solution)/shard_map/ppermute | solution.py:552
  30.6 1.3 %shard_map.142 = (f32[4,4,1152]{2,1,0:T(4,128)}, f32[96,128]{1,0:T(8,128)S(1)}) custom-call(f32[96,128]{1,0:T(8,128)S(1)} %get-tuple-element.76.after, f32[288,128]{1,0:T(8,128)S(1)} %get-tuple-element.77.solution_in, f32[96,128]{1,0:T(8,128)S(1)} %get-tuple-element.78.skeleton, bf16[2592,288]{1,0:T(8,128)(2,1)S(1)} %get-tuple-element.74.update_h, ...), custom_call_target="tpu_custom_call" | custom-call | flops 536870912 | bytes 3305472 | tf_op jit(solution)/shard_map/pallas_call | solution.py:525
  31.9 1.9 %collective-permute-done.7.plane_b = f32[96,128]{1,0:T(8,128)S(1)} collective-permute-done((f32[96,128]{1,0:T(8,128)S(1)}, f32[96,128]{1,0:T(8,128)S(1)}, u32[]{:S(2)}, u32[]{:S(2)}) %collective-permute-start.7) | collective-permute-done | bytes 49184 | tf_op jit(solution)/shard_map/ppermute | solution.py:552
  34.0 4.1 %collective-permute-start.10 = (f32[24,384]{1,0:T(8,128)S(1)}, f32[24,384]{1,0:T(8,128)S(1)}, u32[]{:S(2)}, u32[]{:S(2)}) collective-permute-start(f32[24,384]{1,0:T(8,128)S(1)} %shard_map.143.refs_0_), channel_id=1, source_target_pairs={{0,6},{1,7},{2,4},{3,5},{4,2},{5,3},{6,0},{7,1},{8,14},{9,15},{10,... | collective-permute-start | bytes 110600 | tf_op jit(solution)/shard_map/ppermute | solution.py:680
  39.5 3.0 %collective-permute-done.9.refs_2_ = f32[24,384]{1,0:T(8,128)S(1)} collective-permute-done((f32[24,384]{1,0:T(8,128)S(1)}, f32[24,384]{1,0:T(8,128)S(1)}, u32[]{:S(2)}, u32[]{:S(2)}) %collective-permute-start.9) | collective-permute-done | bytes 36896 | tf_op jit(solution)/shard_map/ppermute | solution.py:680
  42.5 4.2 %collective-permute-start.11 = (f32[96,384]{1,0:T(8,128)S(1)}, f32[96,384]{1,0:T(8,128)S(1)}, u32[]{:S(2)}, u32[]{:S(2)}) collective-permute-start(f32[96,384]{1,0:T(8,128)S(1)} %shard_map.144.own), channel_id=1, source_target_pairs={{0,1},{1,0},{2,3},{3,2},{4,5},{5,4},{6,7},{7,6},{8,9},{9,8},{10,11... | collective-permute-start | bytes 442376 | tf_op jit(solution)/shard_map/ppermute | solution.py:684
  46.7 0.9 %shard_map.138 = f32[128,576]{1,0:T(8,128)} custom-call(f32[48,256]{1,0:T(8,128)S(1)} %get-tuple-element.68.after, f32[144,512]{1,0:T(8,128)S(1)} %get-tuple-element.64.solution_in), custom_call_target="tpu_custom_call" | custom-call | bytes 589824 | tf_op jit(solution)/shard_map/pallas_call | solution.py:525
  47.7 0.8 %shard_map.145 = f32[32,4,384]{2,1,0:T(4,128)} custom-call(f32[96,384]{1,0:T(8,128)S(1)} %shard_map.144.own, f32[96,384]{1,0:T(8,128)S(1)} %collective-permute-done.11.other), custom_call_target="tpu_custom_call" | custom-call | bytes 491520 | tf_op jit(solution)/shard_map/pallas_call | solution.py:525
  (37 shorter events, 3.7 us)
Async XLA Ops:
  0.6 3.2 %copy-start.6 = (f32[4,16,16,256]{3,2,1,0:T(8,128)S(1)}, f32[4,16,16,256]{3,2,1,0:T(8,128)}, u32[]{:S(2)}) copy-start(f32[4,16,16,256]{3,2,1,0:T(8,128)} %rhs.1) | copy-start | bytes 3145732
  0.6 3.1 %copy-start.7 = (f32[27,24,40]{2,1,0:T(8,128)S(1)}, f32[27,24,40]{2,1,0:T(8,128)}, u32[]{:S(2)}) copy-start(f32[27,24,40]{2,1,0:T(8,128)} %param.13) | copy-start | bytes 311044
  0.7 3.1 %copy-start.8 = (f32[40,40]{1,0:T(8,128)S(1)}, f32[40,40]{1,0:T(8,128)}, u32[]{:S(2)}) copy-start(f32[40,40]{1,0:T(8,128)} %elim.3) | copy-start | bytes 19204
  0.7 3.1 %copy-start.9 = (f32[24,40]{1,0:T(8,128)S(1)}, f32[24,40]{1,0:T(8,128)}, u32[]{:S(2)}) copy-start(f32[24,40]{1,0:T(8,128)} %skel.3) | copy-start | bytes 11524
  1.8 5.9 %collective-permute-start = (f32[4,3,16,256]{3,2,1,0:T(8,128)S(1)}, f32[4,3,16,256]{3,2,1,0:T(8,128)S(1)}, u32[]{:S(2)}, u32[]{:S(2)}) collective-permute-start(f32[4,3,16,256]{3,2,1,0:T(8,128)S(1)} %get-tuple-element.50), channel_id=1, source_target_pairs={{0,1},{1,0},{2,3},{3,2},{4,5},{5,4},{6,7},{7,6},{8,9},{9,8},{10,11... | collective-permute-start | bytes 589832 | tf_op jit(solution)/shard_map/ppermute | solution.py:539
  2.6 5.4 %collective-permute-start.1 = (f32[4,3,16,256]{3,2,1,0:T(8,128)S(1)}, f32[4,3,16,256]{3,2,1,0:T(8,128)S(1)}, u32[]{:S(2)}, u32[]{:S(2)}) collective-permute-start(f32[4,3,16,256]{3,2,1,0:T(8,128)S(1)} %get-tuple-element.51), channel_id=1, source_target_pairs={{0,7},{1,2},{2,1},{3,4},{4,3},{5,6},{6,5},{7,0},{8,15},{9,10},{10,... | collective-permute-start | bytes 589832 | tf_op jit(solution)/shard_map/ppermute | solution.py:539
  5.2 9.6 %copy-start.1 = (f32[27,48,144]{2,1,0:T(8,128)S(1)}, f32[27,48,144]{2,1,0:T(8,128)}, u32[]{:S(2)}) copy-start(f32[27,48,144]{2,1,0:T(8,128)} %param.16) | copy-start | bytes 2239492
  5.2 9.6 %copy-start.3 = (f32[144,144]{1,0:T(8,128)S(1)}, f32[144,144]{1,0:T(8,128)}, u32[]{:S(2)}) copy-start(f32[144,144]{1,0:T(8,128)} %elim.4) | copy-start | bytes 248836
  5.2 9.6 %copy-start.5 = (f32[48,144]{1,0:T(8,128)S(1)}, f32[48,144]{1,0:T(8,128)}, u32[]{:S(2)}) copy-start(f32[48,144]{1,0:T(8,128)} %skel.4) | copy-start | bytes 82948
  9.0 8.1 %collective-permute-start.3 = (f32[24,1280]{1,0:T(8,128)S(1)}, f32[24,1280]{1,0:T(8,128)S(1)}, u32[]{:S(2)}, u32[]{:S(2)}) collective-permute-start(f32[24,1280]{1,0:T(8,128)S(1)} %get-tuple-element.57), channel_id=1, source_target_pairs={{0,1},{1,0},{2,3},{3,2},{4,5},{5,4},{6,7},{7,6},{8,16},{9,17},{10,... | collective-permute-start | bytes 368648 | tf_op jit(solution)/shard_map/ppermute | solution.py:552
  14.8 4.0 %collective-permute-start.2 = (f32[24,1280]{1,0:T(8,128)S(1)}, f32[24,1280]{1,0:T(8,128)S(1)}, u32[]{:S(2)}, u32[]{:S(2)}) collective-permute-start(f32[24,1280]{1,0:T(8,128)S(1)} %get-tuple-element.52.after), channel_id=1, source_target_pairs={{0,8},{1,9},{2,10},{3,11},{4,12},{5,13},{6,14},{7,15},{8,0},{9,1},... | collective-permute-start | bytes 368648 | tf_op jit(solution)/shard_map/ppermute | solution.py:552
  18.8 4.9 %copy-start = (f32[27,96,288]{2,1,0:T(8,128)S(1)}, f32[27,96,288]{2,1,0:T(8,128)}, u32[]{:S(2)}) copy-start(f32[27,96,288]{2,1,0:T(8,128)} %param.19) | copy-start | bytes 8957956
  18.8 4.9 %copy-start.2 = (f32[288,288]{1,0:T(8,128)S(1)}, f32[288,288]{1,0:T(8,128)}, u32[]{:S(2)}) copy-start(f32[288,288]{1,0:T(8,128)} %elim.5) | copy-start | bytes 995332
  18.8 4.9 %copy-start.4 = (f32[96,288]{1,0:T(8,128)S(1)}, f32[96,288]{1,0:T(8,128)}, u32[]{:S(2)}) copy-start(f32[96,288]{1,0:T(8,128)} %skel.5) | copy-start | bytes 331780
  21.8 5.1 %collective-permute-start.5 = (f32[48,256]{1,0:T(8,128)S(1)}, f32[48,256]{1,0:T(8,128)S(1)}, u32[]{:S(2)}, u32[]{:S(2)}) collective-permute-start(f32[48,256]{1,0:T(8,128)S(1)} %get-tuple-element.70), channel_id=1, source_target_pairs={{0,1},{1,0},{2,3},{3,2},{4,5},{5,4},{6,7},{7,6},{8,16},{9,17},{10,... | collective-permute-start | bytes 147464 | tf_op jit(solution)/shard_map/ppermute | solution.py:552
  23.7 3.2 %collective-permute-start.4 = (f32[48,256]{1,0:T(8,128)S(1)}, f32[48,256]{1,0:T(8,128)S(1)}, u32[]{:S(2)}, u32[]{:S(2)}) collective-permute-start(f32[48,256]{1,0:T(8,128)S(1)} %get-tuple-element.68.after), channel_id=1, source_target_pairs={{0,8},{1,9},{2,10},{3,11},{4,12},{5,13},{6,14},{7,15},{8,0},{9,1},... | collective-permute-start | bytes 147464 | tf_op jit(solution)/shard_map/ppermute | solution.py:552
  28.7 5.1 %collective-permute-start.7 = (f32[96,128]{1,0:T(8,128)S(1)}, f32[96,128]{1,0:T(8,128)S(1)}, u32[]{:S(2)}, u32[]{:S(2)}) collective-permute-start(f32[96,128]{1,0:T(8,128)S(1)} %get-tuple-element.81), channel_id=1, source_target_pairs={{0,1},{1,0},{2,3},{3,2},{4,5},{5,4},{6,7},{7,6},{8,16},{9,17},{10,... | collective-permute-start | bytes 147464 | tf_op jit(solution)/shard_map/ppermute | solution.py:552
  30.6 3.2 %collective-permute-start.6 = (f32[96,128]{1,0:T(8,128)S(1)}, f32[96,128]{1,0:T(8,128)S(1)}, u32[]{:S(2)}, u32[]{:S(2)}) collective-permute-start(f32[96,128]{1,0:T(8,128)S(1)} %get-tuple-element.76.after), channel_id=1, source_target_pairs={{0,8},{1,9},{2,10},{3,11},{4,12},{5,13},{6,14},{7,15},{8,0},{9,1},... | collective-permute-start | bytes 147464 | tf_op jit(solution)/shard_map/ppermute | solution.py:552
  34.0 5.5 %collective-permute-start.10 = (f32[24,384]{1,0:T(8,128)S(1)}, f32[24,384]{1,0:T(8,128)S(1)}, u32[]{:S(2)}, u32[]{:S(2)}) collective-permute-start(f32[24,384]{1,0:T(8,128)S(1)} %shard_map.143.refs_0_), channel_id=1, source_target_pairs={{0,6},{1,7},{2,4},{3,5},{4,2},{5,3},{6,0},{7,1},{8,14},{9,15},{10,... | collective-permute-start | bytes 110600 | tf_op jit(solution)/shard_map/ppermute | solution.py:680
  38.2 4.3 %collective-permute-start.9 = (f32[24,384]{1,0:T(8,128)S(1)}, f32[24,384]{1,0:T(8,128)S(1)}, u32[]{:S(2)}, u32[]{:S(2)}) collective-permute-start(f32[24,384]{1,0:T(8,128)S(1)} %shard_map.143.refs_0_), channel_id=1, source_target_pairs={{0,4},{1,5},{2,6},{3,7},{4,0},{5,1},{6,2},{7,3},{8,12},{9,13},{10,... | collective-permute-start | bytes 110600 | tf_op jit(solution)/shard_map/ppermute | solution.py:680
  38.2 4.3 %collective-permute-start.8 = (f32[24,384]{1,0:T(8,128)S(1)}, f32[24,384]{1,0:T(8,128)S(1)}, u32[]{:S(2)}, u32[]{:S(2)}) collective-permute-start(f32[24,384]{1,0:T(8,128)S(1)} %shard_map.143.refs_0_), channel_id=1, source_target_pairs={{0,2},{1,3},{2,0},{3,1},{4,6},{5,7},{6,4},{7,5},{8,10},{9,11},{10,... | collective-permute-start | bytes 110600 | tf_op jit(solution)/shard_map/ppermute | solution.py:680
  42.5 5.2 %collective-permute-start.11 = (f32[96,384]{1,0:T(8,128)S(1)}, f32[96,384]{1,0:T(8,128)S(1)}, u32[]{:S(2)}, u32[]{:S(2)}) collective-permute-start(f32[96,384]{1,0:T(8,128)S(1)} %shard_map.144.own), channel_id=1, source_target_pairs={{0,1},{1,0},{2,3},{3,2},{4,5},{5,4},{6,7},{7,6},{8,9},{9,8},{10,11... | collective-permute-start | bytes 442376 | tf_op jit(solution)/shard_map/ppermute | solution.py:684
